TPU v7x, 32 devices: a whole 2x2x4 slice. The times are simulated.
32 devices in a mesh: gx: 4 (over y, x), gy: 8 (over z, core).
Axes of the slice: x: 2, y: 2, z: 4, core: 2. Of those that a mesh axis runs over, the one named last changes fastest.
Arguments:
- adjoint_vel: float32 [128, 2, 62, 32, 128], P(('gx', 'gy')), may hold values from -6 to 6
- velocity: bfloat16 [128, 2, 62, 32, 128], P(('gx', 'gy')), may hold values from -6 to 6
- drag_coef: float32 [128, 32, 128], P(('gx', 'gy')), may hold values from 0.3 to 3
- level_count: int32 [128, 32, 128], P(('gx', 'gy')), may hold values from 1 to 62
- block_ids: int32 [128], P(('gx', 'gy')), may hold values from 0 to 64, as said below
- bathymetry: float32 [256, 1024], P('gy', 'gx'), may hold values from 0.25 to 1
- land_mask: int32 [256, 1024], P('gy', 'gx'), may hold values 0 or 1
Outputs:
- corrected_adjoint: float32 [128, 2, 62, 32, 128], P(('gx', 'gy'))
- drag_gradient: float32 [128, 32, 128], P(('gx', 'gy'))
- surface_height: float32 [256, 1024], P('gy', 'gx')
- bathy_sensitivity: float32 [256, 1024], P('gy', 'gx')
Inputs may be any that keep to these rules, and one draw needn't show every extreme that they name: `block_ids`: each device's 4 entries name the blocks it holds, then 64 in unused slots; each block number below 64 appears exactly once over all devices; each device holds 1 to 4 blocks, and some device holds 4.
All inputs are finite; a program needn't handle non-finite values. No bound on the sum of `land_mask` on one device may be relied on, other than what follows from the above.
Results may differ from a plain program's by a relative error of at most 0.0003.
Values sent between devices are 32-bit elements; how exact they have to be, the bound alone decides.
No kernel may reach another device: no remote copies, remote signals or barrier semaphores. Data moves between devices by JAX's collectives and lax.ppermute only.
A program may use at most 128 MiB of HBM per device.

v0:
```python
import functools

import jax
import jax.numpy as jnp
import numpy as np
from jax import lax
from jax.experimental import pallas as pl
from jax.experimental.pallas import tpu as pltpu
from jax.sharding import PartitionSpec as P

STEPS = 32

mix_rate = 0.25
drag_step = 0.5
force_scale = 0.25
pressure_gain = 0.5
surface_shift = 1.0 / 64.0
speed_floor = 0.01

LANES = 128
SUBLANES = 8
MIB = 1024 * 1024
FIRST_VMEM = 61 * MIB
MIXING_VMEM = 52 * MIB
SOLVE_VMEM = 50 * MIB
WINDOW_VMEM = 16 * MIB


def chebyshev_sum(total_steps):
    highest = surface_shift + 8.0
    centre = 0.5 * (highest + surface_shift)
    radius = 0.5 * (highest - surface_shift)
    sigma_ratio = centre / radius

    def operate(series):
        shifted = np.zeros_like(series)
        shifted[1] += series[0]
        for k in range(1, len(series) - 1):
            shifted[k + 1] += 0.5 * series[k]
            shifted[k - 1] += 0.5 * series[k]
        return centre * series - radius * shifted

    height = np.zeros(total_steps + 2)
    residual = np.zeros(total_steps + 2)
    residual[0] = 1.0
    direction = residual / centre
    ratio_prev = 1.0 / sigma_ratio
    for _ in range(total_steps):
        height = height + direction
        residual = residual - operate(direction)
        ratio_next = 1.0 / (2.0 * sigma_ratio - ratio_prev)
        direction = ratio_next * ratio_prev * direction + 2.0 * ratio_next / radius * residual
        ratio_prev = ratio_next
    return [float(c) for c in height[:total_steps]], 2.0 / radius


def params(limit):
    return pltpu.CompilerParams(vmem_limit_bytes=limit)


SMEM = pl.BlockSpec(memory_space=pltpu.SMEM)
VMEM = pl.BlockSpec(memory_space=pltpu.VMEM)
ANYWHERE = pl.BlockSpec(memory_space=pl.ANY)
HBM = pl.BlockSpec(memory_space=pltpu.HBM)


def forcing_kernel(levels_ref, adjoint_ref, out_ref, levels_held, held, level_sem, sems):
    slots, comps, depth, rows, cols = held.shape
    level_copy = pltpu.make_async_copy(levels_ref, levels_held, level_sem)
    level_copy.start()
    for b in range(slots):
        for c in range(comps):
            pltpu.make_async_copy(adjoint_ref.at[b, c], held.at[b, c], sems.at[b, c]).start()
    level_copy.wait()

    def one_slot(b, carry):
        levels = levels_held[b]
        total = jnp.zeros((rows, cols), jnp.float32)
        for c in range(comps):
            pltpu.make_async_copy(adjoint_ref.at[b, c], held.at[b, c], sems.at[b, c]).wait()
            for k in range(depth):
                total = total + jnp.where(levels > k, held[b, c, k], 0.0)
        out_ref[b] = force_scale * total
        return carry

    lax.fori_loop(0, slots, one_slot, 0)


def column_forcing(adjoint_vel, level_count):
    slots, comps, depth, rows, cols = adjoint_vel.shape
    return pl.pallas_call(
        forcing_kernel,
        in_specs=[HBM, HBM],
        out_specs=VMEM,
        out_shape=pltpu.VMEM((slots, rows, cols), jnp.float32),
        scratch_shapes=[
            pltpu.VMEM(level_count.shape, jnp.int32),
            pltpu.VMEM(adjoint_vel.shape, jnp.float32),
            pltpu.SemaphoreType.DMA,
            pltpu.SemaphoreType.DMA((slots, comps)),
        ],
        compiler_params=params(FIRST_VMEM),
        cost_estimate=pl.CostEstimate(
            flops=2 * adjoint_vel.size, bytes_accessed=4 * adjoint_vel.size, transcendentals=0
        ),
        name="column_forcing",
    )(level_count, adjoint_vel)


DEEP_CHUNK = 16


def mixing_kernel(block_total, first, earlier, ids_ref, levels_ref, drag_ref, adjoint_ref,
                  velocity_ref, after_ref, *rest):
    if earlier:
        for target, ref in zip(rest[3:5], rest[:2]):
            target[0:first] = ref[...]
        rest = rest[2:]
    column_ref, bottom_ref, gradient_ref, adjoint, velocity, column, in_sems, out_sems = rest
    slots, comps, depth, rows, cols = adjoint.shape
    group = 16
    parts = rows // group

    def copies_in(b, index):
        span = pl.ds(pl.multiple_of(index * group, group), group)
        return (
            pltpu.make_async_copy(
                adjoint_ref.at[first + b, :, :, span], adjoint.at[b, :, :, span],
                in_sems.at[0, b, index],
            ),
            pltpu.make_async_copy(
                velocity_ref.at[first + b, :, :, span], velocity.at[b, :, :, span],
                in_sems.at[1, b, index],
            ),
        )

    def copy_out(b, index):
        span = pl.ds(pl.multiple_of(index * group, group), group)
        return pltpu.make_async_copy(
            column.at[b, :, pl.ds(2, depth), span], column_ref.at[b, :, :, span],
            out_sems.at[b, index],
        )

    for b in range(slots):
        for index in range(parts):
            for copy in copies_in(b, index):
                copy.start()

    def one_group(b, index):
        flag = jnp.where(ids_ref[first + b] < block_total, 1.0, 0.0)
        span = pl.ds(pl.multiple_of(index * group, group), group)
        levels = levels_ref[first + b, span, :]
        zero = jnp.zeros(levels.shape, jnp.float32)

        def one_component(c):
            def some_levels(chunk, carry):
                x, once, first_flux, second_flux, flow, field, rate_before = carry
                base = chunk * DEEP_CHUNK
                done = []
                for j in range(DEEP_CHUNK):
                    k = base + j
                    inside = jnp.minimum(k, depth - 1)
                    wet = levels > k
                    rate = jnp.where(wet, jnp.where(k > 0, mix_rate, 0.0), 0.0)
                    fresh = jnp.where(wet, adjoint[b, c, inside, span, :], 0.0)
                    flow = jnp.where(
                        levels == k + 1, velocity[b, c, inside, span, :].astype(jnp.float32), flow
                    )
                    flux = (fresh - x) * rate
                    fresh_once = x + (flux - first_flux)
                    first_flux = flux
                    x = fresh
                    flux = (fresh_once - once) * rate_before
                    twice = once + (flux - second_flux)
                    second_flux = flux
                    once = fresh_once
                    rate_before = rate
                    field = jnp.where(levels == k - 1, twice, field)
                    done.append((k, twice))
                for k, value in done:
                    column[b, c, k, span, :] = value
                return x, once, first_flux, second_flux, flow, field, rate_before

            end = lax.fori_loop(0, (depth + 2) // DEEP_CHUNK, some_levels, (zero,) * 7)
            return end[4], end[5]

        flow, field = zip(one_component(0), one_component(1))
        speed = jnp.sqrt(flow[0] * flow[0] + flow[1] * flow[1] + speed_floor)
        along = flow[0] * field[0] + flow[1] * field[1]
        ratio = along / speed
        drag = drag_ref[first + b, span, :]
        for c in range(2):
            bottom_ref[first + b, c, span, :] = field[c] - drag_step * drag * (
                speed * field[c] + flow[c] * ratio
            )
        gradient_ref[first + b, span, :] = -drag_step * speed * along * flag

    def one(step, carry):
        b = lax.div(step, parts)
        index = lax.rem(step, parts)
        for copy in copies_in(b, index):
            copy.wait()
        one_group(b, index)
        copy_out(b, index).start()
        return carry

    lax.fori_loop(0, slots * parts, one, 0)
    for b in range(slots):
        for index in range(parts):
            copy_out(b, index).wait()


def column_mixing(adjoint_vel, velocity, drag_coef, level_count, block_ids, after, block_total,
                  first, last, earlier=()):
    comps, depth, rows, cols = adjoint_vel.shape[1:]
    assert (depth + 2) % DEEP_CHUNK == 0
    slots = last - first
    part = (slots, comps, depth, rows, cols)
    size = slots * comps * depth * rows * cols
    return pl.pallas_call(
        functools.partial(mixing_kernel, block_total, first, len(earlier)),
        in_specs=[SMEM, VMEM, VMEM, HBM, HBM, ANYWHERE] + [VMEM] * len(earlier),
        out_specs=[HBM, VMEM, VMEM],
        out_shape=[
            pltpu.HBM(part, jnp.float32),
            pltpu.VMEM((last, comps, rows, cols), jnp.float32),
            pltpu.HBM((last, rows, cols), jnp.float32),
        ],
        scratch_shapes=[
            pltpu.VMEM(part, adjoint_vel.dtype),
            pltpu.VMEM(part, velocity.dtype),
            pltpu.VMEM((slots, comps, depth + 2, rows, cols), jnp.float32),
            pltpu.SemaphoreType.DMA((2, slots, rows // 16)),
            pltpu.SemaphoreType.DMA((slots, rows // 16)),
        ],
        compiler_params=params(MIXING_VMEM),
        cost_estimate=pl.CostEstimate(
            flops=14 * size, bytes_accessed=10 * size, transcendentals=0
        ),
        name="column_mixing",
    )(block_ids, level_count, drag_coef, adjoint_vel, velocity, after, *earlier)


CHUNK = 8
PAD = SUBLANES
WIDTH = LANES + 2 * STEPS
PITCH = WIDTH + 2 * PAD
NEIGHBOURS = [(down, right) for down in (-1, 0, 1) for right in (0, 1, -1)]


def window_shape(slots, rows):
    strips = LANES // (slots + 2)
    deep = pl.cdiv(rows + 2 * STEPS, strips)
    return strips, deep, strips * deep


def log2(count):
    bits = count.bit_length() - 1
    assert 1 << bits == count
    return bits


def window_places(me_ref, ids_ref, slots, lon_count, lat_count):
    places = []
    for w in range(slots + 2):
        if w < slots:
            block = jnp.where(ids_ref[w] < 2 * lon_count * lat_count, ids_ref[w], 0)
        else:
            block = (me_ref[0] * lat_count + me_ref[1]) * 2 + (w - slots)
        pair = block >> 1
        column = (pair >> log2(lat_count)) * 2 + (block & 1)
        places.append((pair & (lat_count - 1), column))
    return places


def put_window(natural, base, rows, blocks, lane):
    for i in range(3):
        here, east, west = blocks[3 * i:3 * i + 3]
        sides = jnp.where(lane < STEPS, east, jnp.where(lane >= LANES - STEPS, west, 0.0))
        start = base + i * rows
        natural[0, start:start + rows, :] = here
        natural[1, start:start + rows, :] = sides


def turn(natural, deep, put):
    for i in range(deep):
        put(i, STEPS, natural[0, pl.ds(i, LANES, stride=deep), :].T)
        sides = natural[1, pl.ds(i, LANES, stride=deep), :].T
        put(i, STEPS + LANES, sides[:STEPS])
        put(i, 0, sides[LANES - STEPS:])


def rows_at(ref, start, shift=0):
    return ref[pl.ds(start + shift, SUBLANES), :]


def strip_rows(ref, chunk, deep):
    at = [pl.multiple_of(i * PITCH + PAD + chunk * SUBLANES, SUBLANES) for i in range(deep)]
    here = [rows_at(ref, a) for a in at]
    above = [pltpu.roll(here[-1], 1, 1)] + here[:-1]
    below = here[1:] + [pltpu.roll(here[0], LANES - 1, 1)]
    return here, above, below, at


def depth_kernel(ids_ref, bathymetry_ref, mask_ref, out_ref, ids, bathymetry, mask, sems):
    copies = [
        pltpu.make_async_copy(ids_ref, ids, sems.at[0]),
        pltpu.make_async_copy(bathymetry_ref, bathymetry, sems.at[1]),
        pltpu.make_async_copy(mask_ref, mask, sems.at[2]),
    ]
    for copy in copies:
        copy.start()
    for copy in copies:
        copy.wait()
    rows = bathymetry.shape[0]
    scaled = bathymetry[...] * mask[...].astype(jnp.float32)
    out_ref[0:rows, :] = scaled[:, :LANES]
    out_ref[rows:2 * rows, :] = scaled[:, LANES:]
    lane = lax.broadcasted_iota(jnp.int32, (SUBLANES, LANES), 1)
    listed = jnp.zeros((SUBLANES, LANES), jnp.int32)
    for s in range(ids.shape[0]):
        listed = jnp.where(lane == s, ids[s], listed)
    out_ref[2 * rows:2 * rows + SUBLANES, :] = listed.astype(jnp.float32)


def depth_payload(bathymetry, land_mask, block_ids):
    rows = bathymetry.shape[0]
    return pl.pallas_call(
        depth_kernel,
        in_specs=[HBM, HBM, HBM],
        out_specs=VMEM,
        out_shape=pltpu.VMEM((2 * rows + SUBLANES, LANES), jnp.float32),
        scratch_shapes=[
            pltpu.SMEM(block_ids.shape, jnp.int32),
            pltpu.VMEM(bathymetry.shape, jnp.float32),
            pltpu.VMEM(land_mask.shape, jnp.int32),
            pltpu.SemaphoreType.DMA((3,)),
        ],
        compiler_params=params(FIRST_VMEM),
        name="depth_payload",
    )(block_ids, bathymetry, land_mask)


def weights_kernel(slots, lon_count, lat_count, me_ref, ids_ref, near_ref, far_ref,
                   root_ref, centre_ref, around_ref, table_ref,
                   natural, all_ids, places_of, sems):
    half = lat_count // 2
    count = lon_count * half
    rows = (near_ref.shape[1] - SUBLANES) // 2
    strips, deep, tall = window_shape(slots, rows)
    column_count = 2 * lon_count
    parts = (near_ref, far_ref)
    copies = [
        pltpu.make_async_copy(
            parts[p].at[:, pl.ds(2 * rows, 1), :], all_ids.at[p], sems.at[p]
        )
        for p in range(2)
    ]
    for copy in copies:
        copy.start()
    natural[...] = jnp.zeros_like(natural)

    def load(lat, column):
        inside = (lat >= 0) & (lat < lat_count) & (column >= 0) & (column < column_count)
        lat_safe = jnp.clip(lat, 0, lat_count - 1)
        column_safe = jnp.clip(column, 0, column_count - 1)
        lon_xor = (column_safe >> 1) ^ me_ref[0]
        lat_xor = lat_safe ^ me_ref[1]
        place = lon_xor * half + (lat_xor >> 1)
        start = pl.multiple_of((column_safe & 1) * rows, SUBLANES)
        near = near_ref[place, pl.ds(start, rows), :]
        far = far_ref[place, pl.ds(start, rows), :]
        here = jnp.where((lat_xor & 1) == 0, near, far)
        return here * jnp.where(inside, 1.0, 0.0)

    lane = lax.broadcasted_iota(jnp.int32, (rows, LANES), 1)
    places = window_places(me_ref, ids_ref, slots, lon_count, lat_count)
    for w, (lat, column) in enumerate(places):
        blocks = [load(lat + down, column + right) for down, right in NEIGHBOURS]
        put_window(natural, w * tall, rows, blocks, lane)

    for copy in copies:
        copy.wait()

    def one_device(n, carry):
        for p in range(2):
            for s in range(slots):
                block = all_ids[p, n, 0, s].astype(jnp.int32)
                places_of[block] = (p * count + n) * slots + s
        return carry

    lax.fori_loop(0, count, one_device, 0)
    for w, (lat, column) in enumerate(places):
        for n, (down, right) in enumerate(NEIGHBOURS):
            lat_safe = jnp.clip(lat + down, 0, lat_count - 1)
            column_safe = jnp.clip(column + right, 0, column_count - 1)
            block = ((column_safe >> 1) * lat_count + lat_safe) * 2 + (column_safe & 1)
            table_ref[w * len(NEIGHBOURS) + n] = places_of[block]

    scale = chebyshev_sum(STEPS)[1]

    def put(i, x, values):
        start = i * PITCH + PAD + x
        root_ref[start:start + values.shape[0], :] = jnp.sqrt(values)
        around_ref[start:start + values.shape[0], :] = scale * values

    turn(natural, deep, put)
    zeros = jnp.zeros((PAD, LANES), jnp.float32)
    for i in range(deep):
        root_ref[i * PITCH:i * PITCH + PAD, :] = zeros
        root_ref[(i + 1) * PITCH - PAD:(i + 1) * PITCH, :] = zeros

    def one_chunk(chunk, carry):
        out = []
        here, above, below, at = strip_rows(root_ref, chunk, deep)
        for i, a in enumerate(at):
            others = (rows_at(root_ref, a, 1) + rows_at(root_ref, a, -1)) + (above[i] + below[i])
            out.append((a, 2.0 - scale * here[i] * others))
        for a, value in out:
            centre_ref[pl.ds(a, SUBLANES), :] = value
        return carry

    lax.fori_loop(0, WIDTH // SUBLANES, one_chunk, 0)


def surface_weights(near, far, me, block_ids, rows, lon_count, lat_count):
    slots = block_ids.shape[0]
    assert near.shape[-1] == LANES
    strips, deep, tall = window_shape(slots, rows)
    shape = jax.ShapeDtypeStruct((deep * PITCH, LANES), jnp.float32)
    return pl.pallas_call(
        functools.partial(weights_kernel, slots, lon_count, lat_count),
        in_specs=[SMEM, SMEM, VMEM, VMEM],
        out_specs=[VMEM, VMEM, VMEM, SMEM],
        out_shape=[
            shape,
            shape,
            shape,
            jax.ShapeDtypeStruct(((slots + 2) * len(NEIGHBOURS),), jnp.int32),
        ],
        scratch_shapes=[
            pltpu.VMEM((2, LANES * deep, LANES), jnp.float32),
            pltpu.SMEM((2, near.shape[0], 1, LANES), jnp.float32),
            pltpu.SMEM((2 * lon_count * lat_count + 1,), jnp.int32),
            pltpu.SemaphoreType.DMA((2,)),
        ],
        compiler_params=params(WINDOW_VMEM),
        cost_estimate=pl.CostEstimate(
            flops=0, bytes_accessed=8 * MIB, transcendentals=0
        ),
        name="surface_weights",
    )(me, block_ids, near, far)


def solve_kernel(block_total, ids_ref, table_ref, coefs_ref, root_ref, centre_ref, around_ref,
                 levels_ref, bottom_ref, first_column_ref, last_column_ref, near_ref, far_ref,
                 corrected_ref, height_ref, sensitivity_ref,
                 natural, source, even, odd, extra, column, in_sems, out_sems):
    slots, comps, depth, rows, cols = column.shape
    strips, deep, tall = window_shape(slots, rows)

    middle = first_column_ref.shape[0]
    copies_in = [
        pltpu.make_async_copy(first_column_ref, column.at[pl.ds(0, middle)], in_sems.at[0]),
        pltpu.make_async_copy(
            last_column_ref, column.at[pl.ds(middle, slots - middle)], in_sems.at[1]
        ),
    ]
    for copy in copies_in:
        copy.start()

    count = near_ref.shape[0]

    def load(place):
        inner = place & (count - 1)
        return jnp.where(place < count, near_ref[inner], far_ref[inner])

    lane = lax.broadcasted_iota(jnp.int32, (rows, LANES), 1)
    for w in range(slots + 2):
        places = [table_ref[w * len(NEIGHBOURS) + n] for n in range(len(NEIGHBOURS))]
        put_window(natural, w * tall, rows, [load(place) for place in places], lane)

    coefs, step_scale = chebyshev_sum(STEPS)

    def put(i, x, values):
        start = i * PITCH + PAD + x
        stop = start + values.shape[0]
        root = root_ref[start:stop, :]
        values = jnp.where(root > 0.0, root * values, 0.0)
        source[start:stop, :] = values
        even[start:stop, :] = coefs[STEPS - 1] * values
        odd[start:stop, :] = jnp.zeros_like(values)

    zeros = jnp.zeros((PAD, LANES), jnp.float32)
    for ref in (even, odd):
        for i in range(deep):
            ref[i * PITCH:i * PITCH + PAD, :] = zeros
            ref[(i + 1) * PITCH - PAD:(i + 1) * PITCH, :] = zeros
    turn(natural, deep, put)

    chunks = WIDTH // SUBLANES

    def apply(current, target, coef, gain, low, count):
        size = (chunks - 2 * low) // count

        def group(index, carry):
            out = []
            for n in range(size):
                here, above, below, at = strip_rows(current, low + index * size + n, deep)
                for i, a in enumerate(at):
                    others = (rows_at(current, a, 1) + rows_at(current, a, -1)) + (
                        above[i] + below[i]
                    )
                    pushed = rows_at(centre_ref, a) * here[i] + rows_at(around_ref, a) * others
                    if gain != 1.0:
                        pushed = gain * pushed
                    kept = coef * rows_at(source, a) - rows_at(target, a)
                    out.append((a, kept + pushed))
            for a, value in out:
                target[pl.ds(a, SUBLANES), :] = value
            return carry

        lax.fori_loop(0, count, group, 0)

    def bounds(m):
        low = m // (2 * SUBLANES) * 2
        count = chunks - 2 * low
        return low, count // (5 if count % 5 == 0 else 4)

    runs = []
    for m in range(1, STEPS - 1, 2):
        if runs and runs[-1][1] == bounds(m):
            runs[-1][2] += 1
        else:
            runs.append([m, bounds(m), 1])
    for first, (low, count), pairs in runs:
        def two_steps(pair, carry, first=first, low=low, count=count):
            m = first + 2 * pair
            apply(even, odd, coefs_ref[m], 1.0, low, count)
            apply(odd, even, coefs_ref[m + 1], 1.0, low, count)
            return carry

        lax.fori_loop(0, pairs, two_steps, 0)
    low, count = bounds(STEPS - 1)
    apply(even, odd, coefs[0], 0.5, low, count)

    low = STEPS // SUBLANES - 1

    def one_height(chunk, carry):
        out = []
        for i in range(deep):
            a = pl.multiple_of(i * PITCH + PAD + chunk * SUBLANES, SUBLANES)
            root = rows_at(root_ref, a)
            out.append((a, jnp.where(root > 0.0, rows_at(odd, a) / root, 0.0)))
        for a, value in out:
            extra[pl.ds(a, SUBLANES), :] = value
        return carry

    lax.fori_loop(low, chunks - low, one_height, 0)

    def differences(chunk, carry):
        here, above, below, at = strip_rows(extra, chunk, deep)
        root, root_above, root_below, _ = strip_rows(root_ref, chunk, deep)
        out = []
        for i, a in enumerate(at):
            east_step = rows_at(extra, a, 1) - here[i]
            west_step = here[i] - rows_at(extra, a, -1)
            south_step = below[i] - here[i]
            north_step = here[i] - above[i]
            energy = root[i] * (
                (rows_at(root_ref, a, 1) * east_step * east_step
                 + rows_at(root_ref, a, -1) * west_step * west_step)
                + (root_below[i] * south_step * south_step
                   + root_above[i] * north_step * north_step)
            )
            scaled = rows_at(around_ref, a) * (1.0 / step_scale)
            out.append((even, a, east_step))
            out.append((source, a, 0.25 * energy / jnp.maximum(scaled, 0.25)))
        for ref, a, value in out:
            ref[pl.ds(a, SUBLANES), :] = value
        return carry

    lax.fori_loop(low + 1, chunks - low - 1, differences, 0)

    def turn_back(ref, tile):
        for i in range(deep):
            start = i * PITCH + PAD + STEPS
            natural[tile, pl.ds(i, LANES, stride=deep), :] = ref[start:start + LANES, :].T

    def cut(tile, w, shift=0):
        return natural[tile, pl.ds(w * tall + STEPS + shift, rows), :]

    def copy_out(b, c):
        return pltpu.make_async_copy(column.at[b, c], corrected_ref.at[b, c], out_sems.at[b, c])

    def correct(b, c, step):
        levels = levels_ref[b] * jnp.where(ids_ref[b] < block_total, 1, 0)
        push = pressure_gain * step
        lowest = bottom_ref[b, c] - push

        def some_levels(base, size):
            out = []
            for j in range(size):
                k = base + j
                value = jnp.where(levels == k + 1, lowest, column[b, c, k] - push)
                out.append((k, jnp.where(levels > k, value, 0.0)))
            for k, value in out:
                column[b, c, k] = value

        def one_chunk(chunk, inner):
            some_levels(chunk * CHUNK, CHUNK)
            return inner

        lax.fori_loop(0, depth // CHUNK, one_chunk, 0)
        some_levels(depth // CHUNK * CHUNK, depth % CHUNK)
        copy_out(b, c).start()

    turn_back(even, 0)
    for copy in copies_in:
        copy.wait()

    def correct_east(b, carry):
        correct(b, 0, cut(0, b))
        return carry

    def correct_north(b, carry):
        correct(b, 1, cut(1, b, 1) - cut(1, b))
        return carry

    lax.fori_loop(0, slots, correct_east, 0)
    turn_back(extra, 1)
    lax.fori_loop(0, slots, correct_north, 0)
    turn_back(source, 0)
    for h in range(2):
        height_ref[:, h * LANES:(h + 1) * LANES] = cut(1, slots + h)
        sensitivity_ref[:, h * LANES:(h + 1) * LANES] = cut(0, slots + h)

    for b in range(slots):
        for c in range(comps):
            copy_out(b, c).wait()


def surface_solve(near, far, weights, block_ids, level_count, bottom, columns, block_total):
    root, centre, around, table = weights
    comps, depth, rows, cols = columns[0].shape[1:]
    slots = level_count.shape[0]
    assert comps == 2
    full = (slots, comps, depth, rows, cols)
    deep = window_shape(slots, rows)[1]
    turned = pltpu.VMEM(root.shape, jnp.float32)
    coefs = jnp.array(chebyshev_sum(STEPS)[0][::-1], jnp.float32)
    return pl.pallas_call(
        functools.partial(solve_kernel, block_total),
        in_specs=[SMEM, SMEM, SMEM] + [VMEM] * 5 + [HBM] * 2 + [VMEM] * 2,
        out_specs=[HBM, VMEM, VMEM],
        out_shape=[
            jax.ShapeDtypeStruct(full, jnp.float32),
            jax.ShapeDtypeStruct((rows, 2 * cols), jnp.float32),
            jax.ShapeDtypeStruct((rows, 2 * cols), jnp.float32),
        ],
        scratch_shapes=[
            pltpu.VMEM((2, LANES * deep, LANES), jnp.float32),
            turned,
            turned,
            turned,
            turned,
            pltpu.VMEM(full, jnp.float32),
            pltpu.SemaphoreType.DMA((2,)),
            pltpu.SemaphoreType.DMA((slots, comps)),
        ],
        compiler_params=params(SOLVE_VMEM),
        cost_estimate=pl.CostEstimate(
            flops=9 * STEPS * root.size, bytes_accessed=16 * root.size, transcendentals=0
        ),
        name="surface_solve",
    )(block_ids, table, coefs, root, centre, around, level_count, bottom, *columns, near, far)


def stack_kernel(parts, *refs):
    out_ref = refs[-1]
    for p in range(parts):
        out_ref[p] = refs[p][...]


def stack_after(parts, *tokens):
    return pl.pallas_call(
        functools.partial(stack_kernel, len(parts)),
        in_specs=[VMEM] * len(parts) + [ANYWHERE] * len(tokens),
        out_specs=VMEM,
        out_shape=jax.ShapeDtypeStruct((len(parts),) + parts[0].shape, jnp.float32),
        compiler_params=params(WINDOW_VMEM),
        name="stack_after",
    )(*parts, *tokens)


def swap(values, axis, mask):
    count = lax.axis_size(axis)
    return lax.ppermute(values, axis, [(i, i ^ mask) for i in range(count)])


def per_device(adjoint_vel, velocity, drag_coef, level_count, block_ids, bathymetry, land_mask):
    slots = block_ids.shape[0]
    rows, cols = drag_coef.shape[1:]
    lon_count = lax.axis_size("gx")
    lat_count = lax.axis_size("gy")
    half = lat_count // 2
    block_total = 2 * lon_count * lat_count
    me = jnp.stack([lax.axis_index("gx"), lax.axis_index("gy")]).astype(jnp.int32)

    depths = depth_payload(bathymetry, land_mask, block_ids)
    depth_parts = [depths] + [swap(depths, "gy", 2 * m) for m in range(1, half)]
    forcing = column_forcing(adjoint_vel, level_count)

    parts = [forcing] + [swap(forcing, "gy", 2 * m) for m in range(1, half)]
    near_depths = stack_after(depth_parts, forcing)
    near_depths = [near_depths] + [swap(near_depths, "gx", m) for m in range(1, lon_count)]
    columns = (adjoint_vel, velocity, drag_coef, level_count, block_ids)
    middle = (slots + 1) // 2
    first_column, *first_rest = column_mixing(*columns, forcing, block_total, 0, middle)
    line = stack_after(parts, first_rest[0])

    near = [line] + [swap(line, "gx", m) for m in range(1, lon_count)]
    near_depths = stack_after(near_depths, line)
    near_depths = near_depths.reshape((lon_count * half,) + depths.shape)
    far_depths = swap(near_depths, "gy", 1)
    last_column, bottom, drag_gradient = column_mixing(
        *columns, line, block_total, middle, slots, first_rest
    )
    weights = surface_weights(
        near_depths, far_depths, me, block_ids, rows, lon_count, lat_count
    )

    near = stack_after(near, bottom, weights[0])
    far = swap(near, "gy", 1)

    corrected, height, sensitivity = surface_solve(
        near.reshape((-1, rows, cols)), far.reshape((-1, rows, cols)), weights,
        block_ids, level_count, bottom, (first_column, last_column), block_total,
    )
    return corrected, drag_gradient, height, sensitivity


def solution(mesh):
    in_specs = (
        P(("gx", "gy"), None, None, None, None),
        P(("gx", "gy"), None, None, None, None),
        P(("gx", "gy"), None, None),
        P(("gx", "gy"), None, None),
        P(("gx", "gy")),
        P("gy", "gx"),
        P("gy", "gx"),
    )
    out_specs = (
        P(("gx", "gy"), None, None, None, None),
        P(("gx", "gy"), None, None),
        P("gy", "gx"),
        P("gy", "gx"),
    )
    return jax.shard_map(
        per_device, mesh=mesh, in_specs=in_specs, out_specs=out_specs, check_vma=False
    )
```

profile of v0, /device:TPU:0, one launch (start us, length us, event | category | flops | bytes accessed | tf_op | source)
XLA Modules:
  0.0 65.9 jit_solution(3020702228925441183)
XLA Ops:
  0.6 0.8 %depth_payload.1.refs_0_ = f32[72,128]{1,0:T(8,128)S(1)} custom-call(s32[4]{0:T(128)} %ids_ref.9, f32[32,256]{1,0:T(8,128)} %bathymetry_ref.1, s32[32,256]{1,0:T(8,128)} %mask_ref.1), custom_call_target="tpu_custom_call" | custom-call | tf_op jit(solution)/shard_map/depth_payload/pallas_call | solution.py:328
  1.4 0.0 copy-start
  1.5 0.0 copy-start.1
  1.5 0.0 copy-start.3
  1.5 5.1 %collective-permute-start.2 = (f32[72,128]{1,0:T(8,128)S(1)}, f32[72,128]{1,0:T(8,128)S(1)}, u32[]{:S(2)}, u32[]{:S(2)}) collective-permute-start(f32[72,128]{1,0:T(8,128)S(1)} %depth_payload.1.refs_0_), channel_id=1, source_target_pairs={{0,6},{1,7},{2,4},{3,5},{4,2},{5,3},{6,0},{7,1},{8,14},{9,15},{10,... | collective-permute-start | bytes 110600 | tf_op jit(solution)/shard_map/ppermute | solution.py:698
  6.6 0.0 collective-permute-start.1
  6.6 0.6 collective-permute-start
  7.2 3.9 %column_forcing.1.refs_4_.after_ref.refs_0_ = f32[4,32,128]{2,1,0:T(8,128)S(1)} custom-call(s32[4,32,128]{2,1,0:T(8,128)} %levels_ref.7, f32[4,2,62,32,128]{4,3,2,1,0:T(8,128)} %adjoint_ref.5), custom_call_target="tpu_custom_call" | custom-call | flops 4063232 | bytes 8126464 | tf_op jit(solution)/shard_map/column_forcing/pallas_call | solution.py:91
  11.1 0.0 collective-permute-done.2.refs_3_
  11.1 0.3 collective-permute-done.1.refs_2_
  11.5 0.0 collective-permute-done.refs_1_
  11.5 2.5 %collective-permute-start.5 = (f32[4,72,128]{2,1,0:T(8,128)S(1)}, f32[4,72,128]{2,1,0:T(8,128)S(1)}, u32[]{:S(2)}, u32[]{:S(2)}) collective-permute-start(f32[4,72,128]{2,1,0:T(8,128)S(1)} %stack_after.4.refs_0_), channel_id=1, source_target_pairs={{0,24},{8,16},{16,8},{24,0},{1,25},{9,17},{17,9},{25,1},{2,26},{10... | collective-permute-start | bytes 442376 | tf_op jit(solution)/shard_map/ppermute | solution.py:698
  14.0 0.5 collective-permute-start.4
  14.5 0.5 collective-permute-start.3
  15.0 3.4 %collective-permute-start.8 = (f32[4,32,128]{2,1,0:T(8,128)S(1)}, f32[4,32,128]{2,1,0:T(8,128)S(1)}, u32[]{:S(2)}, u32[]{:S(2)}) collective-permute-start(f32[4,32,128]{2,1,0:T(8,128)S(1)} %column_forcing.1.refs_4_.after_ref.refs_0_), channel_id=1, source_target_pairs={{0,6},{1,7},{2,4},{3,5},{4,2},{5,3},{6,0},{7,1},{8,14},{9,15},{10,... | collective-permute-start | bytes 196616 | tf_op jit(solution)/shard_map/ppermute | solution.py:698
  18.5 0.0 collective-permute-start.7
  18.5 2.8 %collective-permute-done.8.refs_3_ = f32[4,32,128]{2,1,0:T(8,128)S(1)} collective-permute-done((f32[4,32,128]{2,1,0:T(8,128)S(1)}, f32[4,32,128]{2,1,0:T(8,128)S(1)}, u32[]{:S(2)}, u32[]{:S(2)}) %collective-permute-start.8) | collective-permute-done | bytes 65568 | tf_op jit(solution)/shard_map/ppermute | solution.py:698
  21.3 0.0 collective-permute-start.6
  21.3 0.0 copy-done
  21.3 0.0 copy-done.1
  21.3 0.0 copy-done.3
  21.3 6.3 %column_mixing.2 = (f32[2,2,62,32,128]{4,3,2,1,0:T(8,128)}, f32[2,2,32,128]{3,2,1,0:T(8,128)S(1)}, f32[2,32,128]{2,1,0:T(8,128)}) custom-call(s32[4]{0:T(128)S(1)} %copy-done.3, s32[4,32,128]{2,1,0:T(8,128)S(1)} %copy-done, f32[4,32,128]{2,1,0:T(8,128)S(1)} %copy-done.1, f32[4,2,62,32,128]{4,3,2,1,0:T(8,128)} %adjoint_ref.5, ...), custom_call_target="tpu_custom_call" | custom-call | flops 14221312 | bytes 10158080 | tf_op jit(solution)/shard_map/column_mixing/pallas_call | solution.py:220
  27.5 0.0 collective-permute-done.7.refs_2_
  27.6 0.0 collective-permute-done.6.refs_1_
  27.6 0.0 collective-permute-done.5.refs_3_
  27.6 0.0 collective-permute-done.4.refs_2_
  27.6 0.0 collective-permute-done.3.refs_1_
  27.7 0.1 collective-permute-start.9
  27.8 2.5 %collective-permute-start.12 = (f32[4,4,32,128]{3,2,1,0:T(8,128)S(1)}, f32[4,4,32,128]{3,2,1,0:T(8,128)S(1)}, u32[]{:S(2)}, u32[]{:S(2)}) collective-permute-start(f32[4,4,32,128]{3,2,1,0:T(8,128)S(1)} %stack_after.5.refs_4_.after_ref.refs_0_), channel_id=1, source_target_pairs={{0,24},{8,16},{16,8},{24,0},{1,25},{9,17},{17,9},{25,1},{2,26},{10... | collective-permute-start | bytes 786440 | tf_op jit(solution)/shard_map/ppermute | solution.py:698
  30.3 0.5 collective-permute-start.11
  30.8 0.5 collective-permute-start.10
  31.3 0.1 pad_add_fusion.me_ref
  31.4 0.0 copy-start.2
  31.4 0.8 %copy-done.2 = f32[2,32,128]{2,1,0:T(8,128)S(1)} copy-done((f32[2,32,128]{2,1,0:T(8,128)S(1)}, f32[2,32,128]{2,1,0:T(8,128)}, u32[]{:S(2)}) %copy-start.2) | copy-done | bytes 32792
  32.1 0.0 copy-start.4
  32.1 6.3 %column_mixing.3 = (f32[2,2,62,32,128]{4,3,2,1,0:T(8,128)}, f32[4,2,32,128]{3,2,1,0:T(8,128)S(1)}, f32[4,32,128]{2,1,0:T(8,128)}) custom-call(s32[4]{0:T(128)S(1)} %copy-done.3, s32[4,32,128]{2,1,0:T(8,128)S(1)} %copy-done, f32[4,32,128]{2,1,0:T(8,128)S(1)} %copy-done.1, f32[4,2,62,32,128]{4,3,2,1,0:T(8,128)} %adjoint_ref.5, ...), custom_call_target="tpu_custom_call" | custom-call | flops 14221312 | bytes 10158080 | tf_op jit(solution)/shard_map/column_mixing/pallas_call | solution.py:220
  38.5 0.0 collective-permute-done.9.far_ref
  38.5 4.3 %surface_weights.1 = (f32[1040,128]{1,0:T(8,128)S(1)}, f32[1040,128]{1,0:T(8,128)S(1)}, f32[1040,128]{1,0:T(8,128)S(1)}, s32[54]{0:T(128)S(1)}) custom-call(s32[2]{0:T(128)S(1)} %pad_add_fusion.me_ref, s32[4]{0:T(128)S(1)} %copy-done.3, f32[16,72,128]{2,1,0:T(8,128)S(1)} %bitcast.7, f32[16,72,128]{2,1,0:T(8,128)S(1)} %collective-permute-done.9.far_ref), custom_call_target="tpu_custom_call" | custom-call | bytes 8388608 | tf_op jit(solution)/shard_map/surface_weights/pallas_call | solution.py:431
  42.8 0.0 collective-permute-done.12.refs_3_
  42.8 0.2 collective-permute-done.11.refs_2_
  43.0 0.1 collective-permute-done.10.refs_1_
  43.1 0.1 stack_after.7
  43.2 0.1 collective-permute-start.13
  43.2 2.6 %collective-permute-done.13 = f32[4,4,4,32,128]{4,3,2,1,0:T(8,128)S(1)} collective-permute-done((f32[4,4,4,32,128]{4,3,2,1,0:T(8,128)S(1)}, f32[4,4,4,32,128]{4,3,2,1,0:T(8,128)S(1)}, u32[]{:S(2)}, u32[]{:S(2)}) %collective-permute-start.13) | collective-permute-done | bytes 1048608 | tf_op jit(solution)/shard_map/ppermute | solution.py:698
  45.9 0.0 copy-done.4
  45.9 20.0 %surface_solve.1 = (f32[4,2,62,32,128]{4,3,2,1,0:T(8,128)}, f32[32,256]{1,0:T(8,128)}, f32[32,256]{1,0:T(8,128)}) custom-call(s32[4]{0:T(128)S(1)} %copy-done.3, s32[54]{0:T(128)S(1)} %get-tuple-element.18.table_ref, f32[32]{0:T(128)S(1)} %copy-done.4, f32[1040,128]{1,0:T(8,128)S(1)} %get-tuple-element.19.refs_5_.root_ref, ...), custom_call_target="tpu_custom_call" | custom-call | flops 38338560 | bytes 2129920 | tf_op jit(solution)/shard_map/surface_solve/pallas_call | solution.py:652
  (3 shorter events, 0.1 us)
Async XLA Ops:
  1.4 19.8 %copy-start = (s32[4,32,128]{2,1,0:T(8,128)S(1)}, s32[4,32,128]{2,1,0:T(8,128)}, u32[]{:S(2)}) copy-start(s32[4,32,128]{2,1,0:T(8,128)} %levels_ref.7) | copy-start | bytes 196612
  1.5 19.8 %copy-start.1 = (f32[4,32,128]{2,1,0:T(8,128)S(1)}, f32[4,32,128]{2,1,0:T(8,128)}, u32[]{:S(2)}) copy-start(f32[4,32,128]{2,1,0:T(8,128)} %drag_ref.3) | copy-start | bytes 196612
  1.5 19.8 %copy-start.3 = (s32[4]{0:T(128)S(1)}, s32[4]{0:T(128)}, u32[]{:S(2)}) copy-start(s32[4]{0:T(128)} %ids_ref.9) | copy-start | bytes 52
  1.5 9.6 %collective-permute-start.2 = (f32[72,128]{1,0:T(8,128)S(1)}, f32[72,128]{1,0:T(8,128)S(1)}, u32[]{:S(2)}, u32[]{:S(2)}) collective-permute-start(f32[72,128]{1,0:T(8,128)S(1)} %depth_payload.1.refs_0_), channel_id=1, source_target_pairs={{0,6},{1,7},{2,4},{3,5},{4,2},{5,3},{6,0},{7,1},{8,14},{9,15},{10,... | collective-permute-start | bytes 110600 | tf_op jit(solution)/shard_map/ppermute | solution.py:698
  6.6 4.9 %collective-permute-start.1 = (f32[72,128]{1,0:T(8,128)S(1)}, f32[72,128]{1,0:T(8,128)S(1)}, u32[]{:S(2)}, u32[]{:S(2)}) collective-permute-start(f32[72,128]{1,0:T(8,128)S(1)} %depth_payload.1.refs_0_), channel_id=1, source_target_pairs={{0,4},{1,5},{2,6},{3,7},{4,0},{5,1},{6,2},{7,3},{8,12},{9,13},{10,... | collective-permute-start | bytes 110600 | tf_op jit(solution)/shard_map/ppermute | solution.py:698
  6.6 4.9 %collective-permute-start = (f32[72,128]{1,0:T(8,128)S(1)}, f32[72,128]{1,0:T(8,128)S(1)}, u32[]{:S(2)}, u32[]{:S(2)}) collective-permute-start(f32[72,128]{1,0:T(8,128)S(1)} %depth_payload.1.refs_0_), channel_id=1, source_target_pairs={{0,2},{1,3},{2,0},{3,1},{4,6},{5,7},{6,4},{7,5},{8,10},{9,11},{10,... | collective-permute-start | bytes 110600 | tf_op jit(solution)/shard_map/ppermute | solution.py:698
  11.5 16.1 %collective-permute-start.5 = (f32[4,72,128]{2,1,0:T(8,128)S(1)}, f32[4,72,128]{2,1,0:T(8,128)S(1)}, u32[]{:S(2)}, u32[]{:S(2)}) collective-permute-start(f32[4,72,128]{2,1,0:T(8,128)S(1)} %stack_after.4.refs_0_), channel_id=1, source_target_pairs={{0,24},{8,16},{16,8},{24,0},{1,25},{9,17},{17,9},{25,1},{2,26},{10... | collective-permute-start | bytes 442376 | tf_op jit(solution)/shard_map/ppermute | solution.py:698
  14.0 13.6 %collective-permute-start.4 = (f32[4,72,128]{2,1,0:T(8,128)S(1)}, f32[4,72,128]{2,1,0:T(8,128)S(1)}, u32[]{:S(2)}, u32[]{:S(2)}) collective-permute-start(f32[4,72,128]{2,1,0:T(8,128)S(1)} %stack_after.4.refs_0_), channel_id=1, source_target_pairs={{0,16},{8,24},{16,0},{24,8},{1,17},{9,25},{17,1},{25,9},{2,18},{10... | collective-permute-start | bytes 442376 | tf_op jit(solution)/shard_map/ppermute | solution.py:698
  14.5 13.1 %collective-permute-start.3 = (f32[4,72,128]{2,1,0:T(8,128)S(1)}, f32[4,72,128]{2,1,0:T(8,128)S(1)}, u32[]{:S(2)}, u32[]{:S(2)}) collective-permute-start(f32[4,72,128]{2,1,0:T(8,128)S(1)} %stack_after.4.refs_0_), channel_id=1, source_target_pairs={{0,8},{8,0},{16,24},{24,16},{1,9},{9,1},{17,25},{25,17},{2,10},{10... | collective-permute-start | bytes 442376 | tf_op jit(solution)/shard_map/ppermute | solution.py:698
  15.0 6.2 %collective-permute-start.8 = (f32[4,32,128]{2,1,0:T(8,128)S(1)}, f32[4,32,128]{2,1,0:T(8,128)S(1)}, u32[]{:S(2)}, u32[]{:S(2)}) collective-permute-start(f32[4,32,128]{2,1,0:T(8,128)S(1)} %column_forcing.1.refs_4_.after_ref.refs_0_), channel_id=1, source_target_pairs={{0,6},{1,7},{2,4},{3,5},{4,2},{5,3},{6,0},{7,1},{8,14},{9,15},{10,... | collective-permute-start | bytes 196616 | tf_op jit(solution)/shard_map/ppermute | solution.py:698
  18.5 9.1 %collective-permute-start.7 = (f32[4,32,128]{2,1,0:T(8,128)S(1)}, f32[4,32,128]{2,1,0:T(8,128)S(1)}, u32[]{:S(2)}, u32[]{:S(2)}) collective-permute-start(f32[4,32,128]{2,1,0:T(8,128)S(1)} %column_forcing.1.refs_4_.after_ref.refs_0_), channel_id=1, source_target_pairs={{0,4},{1,5},{2,6},{3,7},{4,0},{5,1},{6,2},{7,3},{8,12},{9,13},{10,... | collective-permute-start | bytes 196616 | tf_op jit(solution)/shard_map/ppermute | solution.py:698
  21.3 6.3 %collective-permute-start.6 = (f32[4,32,128]{2,1,0:T(8,128)S(1)}, f32[4,32,128]{2,1,0:T(8,128)S(1)}, u32[]{:S(2)}, u32[]{:S(2)}) collective-permute-start(f32[4,32,128]{2,1,0:T(8,128)S(1)} %column_forcing.1.refs_4_.after_ref.refs_0_), channel_id=1, source_target_pairs={{0,2},{1,3},{2,0},{3,1},{4,6},{5,7},{6,4},{7,5},{8,10},{9,11},{10,... | collective-permute-start | bytes 196616 | tf_op jit(solution)/shard_map/ppermute | solution.py:698
  27.7 10.8 %collective-permute-start.9 = (f32[16,72,128]{2,1,0:T(8,128)S(1)}, f32[16,72,128]{2,1,0:T(8,128)S(1)}, u32[]{:S(2)}, u32[]{:S(2)}) collective-permute-start(f32[16,72,128]{2,1,0:T(8,128)S(1)} %bitcast.6), channel_id=1, source_target_pairs={{0,1},{1,0},{2,3},{3,2},{4,5},{5,4},{6,7},{7,6},{8,9},{9,8},{10,11... | collective-permute-start | bytes 1769480 | tf_op jit(solution)/shard_map/ppermute | solution.py:698
  27.8 15.1 %collective-permute-start.12 = (f32[4,4,32,128]{3,2,1,0:T(8,128)S(1)}, f32[4,4,32,128]{3,2,1,0:T(8,128)S(1)}, u32[]{:S(2)}, u32[]{:S(2)}) collective-permute-start(f32[4,4,32,128]{3,2,1,0:T(8,128)S(1)} %stack_after.5.refs_4_.after_ref.refs_0_), channel_id=1, source_target_pairs={{0,24},{8,16},{16,8},{24,0},{1,25},{9,17},{17,9},{25,1},{2,26},{10... | collective-permute-start | bytes 786440 | tf_op jit(solution)/shard_map/ppermute | solution.py:698
  30.3 12.7 %collective-permute-start.11 = (f32[4,4,32,128]{3,2,1,0:T(8,128)S(1)}, f32[4,4,32,128]{3,2,1,0:T(8,128)S(1)}, u32[]{:S(2)}, u32[]{:S(2)}) collective-permute-start(f32[4,4,32,128]{3,2,1,0:T(8,128)S(1)} %stack_after.5.refs_4_.after_ref.refs_0_), channel_id=1, source_target_pairs={{0,16},{8,24},{16,0},{24,8},{1,17},{9,25},{17,1},{25,9},{2,18},{10... | collective-permute-start | bytes 786440 | tf_op jit(solution)/shard_map/ppermute | solution.py:698
  30.8 12.3 %collective-permute-start.10 = (f32[4,4,32,128]{3,2,1,0:T(8,128)S(1)}, f32[4,4,32,128]{3,2,1,0:T(8,128)S(1)}, u32[]{:S(2)}, u32[]{:S(2)}) collective-permute-start(f32[4,4,32,128]{3,2,1,0:T(8,128)S(1)} %stack_after.5.refs_4_.after_ref.refs_0_), channel_id=1, source_target_pairs={{0,8},{8,0},{16,24},{24,16},{1,9},{9,1},{17,25},{25,17},{2,10},{10... | collective-permute-start | bytes 786440 | tf_op jit(solution)/shard_map/ppermute | solution.py:698
  31.4 0.8 %copy-start.2 = (f32[2,32,128]{2,1,0:T(8,128)S(1)}, f32[2,32,128]{2,1,0:T(8,128)}, u32[]{:S(2)}) copy-start(f32[2,32,128]{2,1,0:T(8,128)} %get-tuple-element.22.rest_1_) | copy-start | bytes 98308
  32.1 13.8 %copy-start.4 = (f32[32]{0:T(128)S(1)}, f32[32]{0:T(128)}, u32[]{:S(2)}) copy-start(f32[32]{0:T(128)} %constant.10.clone.coefs_ref) | copy-start | bytes 388
  43.2 2.7 %collective-permute-start.13 = (f32[4,4,4,32,128]{4,3,2,1,0:T(8,128)S(1)}, f32[4,4,4,32,128]{4,3,2,1,0:T(8,128)S(1)}, u32[]{:S(2)}, u32[]{:S(2)}) collective-permute-start(f32[4,4,4,32,128]{4,3,2,1,0:T(8,128)S(1)} %stack_after.7), channel_id=1, source_target_pairs={{0,1},{1,0},{2,3},{3,2},{4,5},{5,4},{6,7},{7,6},{8,9},{9,8},{10,11... | collective-permute-start | bytes 3145736 | tf_op jit(solution)/shard_map/ppermute | solution.py:698
where the time goes:
time: 66.4 us; the launch traced here: 65.9 us
  Pallas kernels  41.7 us (63%)
  starting transfers between devices  16.5 us (25%)
  waiting for transfers between devices  6.04 us (9%)
  between operations  0.82 us (1%)
  local copies, waits for them, and re-layouts  0.78 us (1%)
    pallas_call x1, Pallas kernels, surface_solve(): pl.pallas_call(functools.partial(solve_kernel, block_total), in_specs=[SM...  20 us
    ppermute x14, starting transfers between devices, swap(): return lax.ppermute(values, axis, [(i, i ^ mask) for i in range(count)])  16.5 us
    pallas_call x2, Pallas kernels, column_mixing(): pl.pallas_call(functools.partial(mixing_kernel, block_total, first, len(e...  12.6 us
    ppermute x14, waiting for transfers between devices, swap(): return lax.ppermute(values, axis, [(i, i ^ mask) for i in range(count)])  6.04 us
    pallas_call x1, Pallas kernels, surface_weights(): pl.pallas_call(functools.partial(weights_kernel, slots, lon_count, lat_co...  4.33 us
    pallas_call x1, Pallas kernels, column_forcing(): pl.pallas_call(forcing_kernel, in_specs=[HBM, HBM], out_specs=VMEM, out_s...  3.88 us
  transfers between devices with their start and end apart: 14, of which 5 were waited for; matrix products, arithmetic and copies ran while one was open for 0% of the time, Pallas kernels for 32%

commit v1 on v0

--- a/solution.py
+++ b/solution.py
@@ -64,23 +64,43 @@
 HBM = pl.BlockSpec(memory_space=pltpu.HBM)
 
 
+CUTS = 2
+
+
+def level_cuts(depth):
+    step = pl.cdiv(depth, CUTS)
+    return [(n, n * step, min(step, depth - n * step)) for n in range(CUTS)]
+
+
 def forcing_kernel(levels_ref, adjoint_ref, out_ref, levels_held, held, level_sem, sems):
     slots, comps, depth, rows, cols = held.shape
     level_copy = pltpu.make_async_copy(levels_ref, levels_held, level_sem)
     level_copy.start()
+
+    def copies_in(b):
+        return [
+            pltpu.make_async_copy(
+                adjoint_ref.at[b, c, pl.ds(low, size)], held.at[b, c, pl.ds(low, size)],
+                sems.at[b, c, n],
+            )
+            for c in range(comps)
+            for n, low, size in level_cuts(depth)
+        ]
+
     for b in range(slots):
-        for c in range(comps):
-            pltpu.make_async_copy(adjoint_ref.at[b, c], held.at[b, c], sems.at[b, c]).start()
+        for copy in copies_in(b):
+            copy.start()
     level_copy.wait()
 
     def one_slot(b, carry):
+        for copy in copies_in(b):
+            copy.wait()
         levels = levels_held[b]
-        total = jnp.zeros((rows, cols), jnp.float32)
-        for c in range(comps):
-            pltpu.make_async_copy(adjoint_ref.at[b, c], held.at[b, c], sems.at[b, c]).wait()
-            for k in range(depth):
-                total = total + jnp.where(levels > k, held[b, c, k], 0.0)
-        out_ref[b] = force_scale * total
+        totals = [jnp.zeros((rows, cols), jnp.float32) for _ in range(4)]
+        for k in range(depth):
+            both = held[b, 0, k] + held[b, 1, k]
+            totals[k % 4] = totals[k % 4] + jnp.where(levels > k, both, 0.0)
+        out_ref[b] = force_scale * ((totals[0] + totals[1]) + (totals[2] + totals[3]))
         return carry
 
     lax.fori_loop(0, slots, one_slot, 0)
@@ -97,7 +117,7 @@
             pltpu.VMEM(level_count.shape, jnp.int32),
             pltpu.VMEM(adjoint_vel.shape, jnp.float32),
             pltpu.SemaphoreType.DMA,
-            pltpu.SemaphoreType.DMA((slots, comps)),
+            pltpu.SemaphoreType.DMA((slots, comps, CUTS)),
         ],
         compiler_params=params(FIRST_VMEM),
         cost_estimate=pl.CostEstimate(
@@ -107,7 +127,7 @@
     )(level_count, adjoint_vel)
 
 
-DEEP_CHUNK = 16
+CHUNK = 8
 
 
 def mixing_kernel(block_total, first, earlier, ids_ref, levels_ref, drag_ref, adjoint_ref,
@@ -121,70 +141,78 @@
     group = 16
     parts = rows // group
 
-    def copies_in(b, index):
-        span = pl.ds(pl.multiple_of(index * group, group), group)
-        return (
+    def copies_in(b):
+        return [
             pltpu.make_async_copy(
-                adjoint_ref.at[first + b, :, :, span], adjoint.at[b, :, :, span],
-                in_sems.at[0, b, index],
-            ),
-            pltpu.make_async_copy(
-                velocity_ref.at[first + b, :, :, span], velocity.at[b, :, :, span],
-                in_sems.at[1, b, index],
-            ),
-        )
-
-    def copy_out(b, index):
-        span = pl.ds(pl.multiple_of(index * group, group), group)
-        return pltpu.make_async_copy(
-            column.at[b, :, pl.ds(2, depth), span], column_ref.at[b, :, :, span],
-            out_sems.at[b, index],
-        )
+                source.at[first + b, c, pl.ds(low, size)], target.at[b, c, pl.ds(low, size)],
+                in_sems.at[which, b, c, n],
+            )
+            for which, (source, target) in enumerate(
+                ((adjoint_ref, adjoint), (velocity_ref, velocity))
+            )
+            for c in range(comps)
+            for n, low, size in level_cuts(depth)
+        ]
+
+    def copies_out(b):
+        return [
+            pltpu.make_async_copy(column.at[b, c], column_ref.at[b, c], out_sems.at[b, c])
+            for c in range(comps)
+        ]
 
     for b in range(slots):
-        for index in range(parts):
-            for copy in copies_in(b, index):
-                copy.start()
+        for copy in copies_in(b):
+            copy.start()
+
+    def one_component(b, c, span, levels):
+        zero = jnp.zeros(levels.shape, jnp.float32)
+        x = once = first_flux = second_flux = flow = field = rate_before = zero
+
+        def store(batch):
+            for k, value in batch:
+                column[b, c, k, span, :] = value
+
+        late = []
+        for low in range(0, depth + 2, CHUNK):
+            batch = []
+            for k in range(low, min(low + CHUNK, depth + 2)):
+                fresh_once = None
+                if k < depth:
+                    wet = levels > k
+                    rate = jnp.where(wet, mix_rate, 0.0)
+                    fresh = jnp.where(wet, adjoint[b, c, k, span, :], 0.0)
+                    flow = jnp.where(
+                        levels == k + 1, velocity[b, c, k, span, :].astype(jnp.float32), flow
+                    )
+                    if 1 <= k:
+                        flux = (fresh - x) * rate
+                        fresh_once = x + (flux - first_flux)
+                        first_flux = flux
+                    x = fresh
+                elif k == depth:
+                    fresh_once = x - first_flux
+                if 2 <= k:
+                    if k <= depth:
+                        flux = (fresh_once - once) * rate_before
+                        twice = once + (flux - second_flux)
+                        second_flux = flux
+                    else:
+                        twice = once - second_flux
+                    batch.append((k - 2, twice))
+                    field = jnp.where(levels == k - 1, twice, field)
+                if fresh_once is not None:
+                    once = fresh_once
+                rate_before = rate
+            store(late)
+            late = batch
+        store(late)
+        return flow, field
 
     def one_group(b, index):
         flag = jnp.where(ids_ref[first + b] < block_total, 1.0, 0.0)
         span = pl.ds(pl.multiple_of(index * group, group), group)
         levels = levels_ref[first + b, span, :]
-        zero = jnp.zeros(levels.shape, jnp.float32)
-
-        def one_component(c):
-            def some_levels(chunk, carry):
-                x, once, first_flux, second_flux, flow, field, rate_before = carry
-                base = chunk * DEEP_CHUNK
-                done = []
-                for j in range(DEEP_CHUNK):
-                    k = base + j
-                    inside = jnp.minimum(k, depth - 1)
-                    wet = levels > k
-                    rate = jnp.where(wet, jnp.where(k > 0, mix_rate, 0.0), 0.0)
-                    fresh = jnp.where(wet, adjoint[b, c, inside, span, :], 0.0)
-                    flow = jnp.where(
-                        levels == k + 1, velocity[b, c, inside, span, :].astype(jnp.float32), flow
-                    )
-                    flux = (fresh - x) * rate
-                    fresh_once = x + (flux - first_flux)
-                    first_flux = flux
-                    x = fresh
-                    flux = (fresh_once - once) * rate_before
-                    twice = once + (flux - second_flux)
-                    second_flux = flux
-                    once = fresh_once
-                    rate_before = rate
-                    field = jnp.where(levels == k - 1, twice, field)
-                    done.append((k, twice))
-                for k, value in done:
-                    column[b, c, k, span, :] = value
-                return x, once, first_flux, second_flux, flow, field, rate_before
-
-            end = lax.fori_loop(0, (depth + 2) // DEEP_CHUNK, some_levels, (zero,) * 7)
-            return end[4], end[5]
-
-        flow, field = zip(one_component(0), one_component(1))
+        flow, field = zip(*[one_component(b, c, span, levels) for c in range(2)])
         speed = jnp.sqrt(flow[0] * flow[0] + flow[1] * flow[1] + speed_floor)
         along = flow[0] * field[0] + flow[1] * field[1]
         ratio = along / speed
@@ -198,22 +226,30 @@
     def one(step, carry):
         b = lax.div(step, parts)
         index = lax.rem(step, parts)
-        for copy in copies_in(b, index):
-            copy.wait()
+
+        @pl.when(index == 0)
+        def _():
+            for copy in copies_in(b):
+                copy.wait()
+
         one_group(b, index)
-        copy_out(b, index).start()
+
+        @pl.when(index == parts - 1)
+        def _():
+            for copy in copies_out(b):
+                copy.start()
+
         return carry
 
     lax.fori_loop(0, slots * parts, one, 0)
     for b in range(slots):
-        for index in range(parts):
-            copy_out(b, index).wait()
+        for copy in copies_out(b):
+            copy.wait()
 
 
 def column_mixing(adjoint_vel, velocity, drag_coef, level_count, block_ids, after, block_total,
                   first, last, earlier=()):
     comps, depth, rows, cols = adjoint_vel.shape[1:]
-    assert (depth + 2) % DEEP_CHUNK == 0
     slots = last - first
     part = (slots, comps, depth, rows, cols)
     size = slots * comps * depth * rows * cols
@@ -224,14 +260,14 @@
         out_shape=[
             pltpu.HBM(part, jnp.float32),
             pltpu.VMEM((last, comps, rows, cols), jnp.float32),
-            pltpu.HBM((last, rows, cols), jnp.float32),
+            (pltpu.HBM if last == level_count.shape[0] else pltpu.VMEM)((last, rows, cols), jnp.float32),
         ],
         scratch_shapes=[
             pltpu.VMEM(part, adjoint_vel.dtype),
             pltpu.VMEM(part, velocity.dtype),
-            pltpu.VMEM((slots, comps, depth + 2, rows, cols), jnp.float32),
-            pltpu.SemaphoreType.DMA((2, slots, rows // 16)),
-            pltpu.SemaphoreType.DMA((slots, rows // 16)),
+            pltpu.VMEM(part, jnp.float32),
+            pltpu.SemaphoreType.DMA((2, slots, comps, CUTS)),
+            pltpu.SemaphoreType.DMA((slots, comps)),
         ],
         compiler_params=params(MIXING_VMEM),
         cost_estimate=pl.CostEstimate(
@@ -241,8 +277,8 @@
     )(block_ids, level_count, drag_coef, adjoint_vel, velocity, after, *earlier)
 
 
-CHUNK = 8
 PAD = SUBLANES
+BATCH = 3
 WIDTH = LANES + 2 * STEPS
 PITCH = WIDTH + 2 * PAD
 NEIGHBOURS = [(down, right) for down in (-1, 0, 1) for right in (0, 1, -1)]
@@ -294,8 +330,19 @@
     return ref[pl.ds(start + shift, SUBLANES), :]
 
 
+def in_batches(chunks, work):
+    late = []
+    for start in range(0, len(chunks), BATCH):
+        batch = [item for chunk in chunks[start:start + BATCH] for item in work(chunk)]
+        for ref, a, value in late:
+            ref[pl.ds(a, SUBLANES), :] = value
+        late = batch
+    for ref, a, value in late:
+        ref[pl.ds(a, SUBLANES), :] = value
+
+
 def strip_rows(ref, chunk, deep):
-    at = [pl.multiple_of(i * PITCH + PAD + chunk * SUBLANES, SUBLANES) for i in range(deep)]
+    at = [i * PITCH + PAD + chunk * SUBLANES for i in range(deep)]
     here = [rows_at(ref, a) for a in at]
     above = [pltpu.roll(here[-1], 1, 1)] + here[:-1]
     below = here[1:] + [pltpu.roll(here[0], LANES - 1, 1)]
@@ -410,17 +457,15 @@
         root_ref[i * PITCH:i * PITCH + PAD, :] = zeros
         root_ref[(i + 1) * PITCH - PAD:(i + 1) * PITCH, :] = zeros
 
-    def one_chunk(chunk, carry):
+    def work(chunk):
+        here, above, below, at = strip_rows(root_ref, chunk, deep)
         out = []
-        here, above, below, at = strip_rows(root_ref, chunk, deep)
         for i, a in enumerate(at):
             others = (rows_at(root_ref, a, 1) + rows_at(root_ref, a, -1)) + (above[i] + below[i])
-            out.append((a, 2.0 - scale * here[i] * others))
-        for a, value in out:
-            centre_ref[pl.ds(a, SUBLANES), :] = value
-        return carry
-
-    lax.fori_loop(0, WIDTH // SUBLANES, one_chunk, 0)
+            out.append((centre_ref, a, 2.0 - scale * here[i] * others))
+        return out
+
+    in_batches(range(WIDTH // SUBLANES), work)
 
 
 def surface_weights(near, far, me, block_ids, rows, lon_count, lat_count):
@@ -500,65 +545,52 @@
 
     chunks = WIDTH // SUBLANES
 
-    def apply(current, target, coef, gain, low, count):
-        size = (chunks - 2 * low) // count
-
-        def group(index, carry):
+    def apply(current, target, coef, gain, m):
+        def work(chunk):
+            here, above, below, at = strip_rows(current, chunk, deep)
             out = []
-            for n in range(size):
-                here, above, below, at = strip_rows(current, low + index * size + n, deep)
-                for i, a in enumerate(at):
-                    others = (rows_at(current, a, 1) + rows_at(current, a, -1)) + (
-                        above[i] + below[i]
-                    )
-                    pushed = rows_at(centre_ref, a) * here[i] + rows_at(around_ref, a) * others
-                    if gain != 1.0:
-                        pushed = gain * pushed
-                    kept = coef * rows_at(source, a) - rows_at(target, a)
-                    out.append((a, kept + pushed))
-            for a, value in out:
-                target[pl.ds(a, SUBLANES), :] = value
-            return carry
-
-        lax.fori_loop(0, count, group, 0)
-
-    def bounds(m):
-        low = m // (2 * SUBLANES) * 2
-        count = chunks - 2 * low
-        return low, count // (5 if count % 5 == 0 else 4)
+            for i, a in enumerate(at):
+                others = (rows_at(current, a, 1) + rows_at(current, a, -1)) + (
+                    above[i] + below[i]
+                )
+                pushed = rows_at(centre_ref, a) * here[i] + rows_at(around_ref, a) * others
+                if gain != 1.0:
+                    pushed = gain * pushed
+                kept = coef * rows_at(source, a) - rows_at(target, a)
+                out.append((target, a, kept + pushed))
+            return out
+
+        in_batches(range(m // SUBLANES, chunks - m // SUBLANES), work)
 
     runs = []
     for m in range(1, STEPS - 1, 2):
-        if runs and runs[-1][1] == bounds(m):
-            runs[-1][2] += 1
+        if runs and runs[-1][0] // SUBLANES == m // SUBLANES:
+            runs[-1][1] += 1
         else:
-            runs.append([m, bounds(m), 1])
-    for first, (low, count), pairs in runs:
-        def two_steps(pair, carry, first=first, low=low, count=count):
+            runs.append([m, 1])
+    for first, pairs in runs:
+        def two_steps(pair, carry, first=first):
             m = first + 2 * pair
-            apply(even, odd, coefs_ref[m], 1.0, low, count)
-            apply(odd, even, coefs_ref[m + 1], 1.0, low, count)
+            apply(even, odd, coefs_ref[m], 1.0, first)
+            apply(odd, even, coefs_ref[m + 1], 1.0, first)
             return carry
 
         lax.fori_loop(0, pairs, two_steps, 0)
-    low, count = bounds(STEPS - 1)
-    apply(even, odd, coefs[0], 0.5, low, count)
+    apply(even, odd, coefs[0], 0.5, STEPS - 1)
 
     low = STEPS // SUBLANES - 1
 
-    def one_height(chunk, carry):
+    def one_height(chunk):
         out = []
         for i in range(deep):
-            a = pl.multiple_of(i * PITCH + PAD + chunk * SUBLANES, SUBLANES)
+            a = i * PITCH + PAD + chunk * SUBLANES
             root = rows_at(root_ref, a)
-            out.append((a, jnp.where(root > 0.0, rows_at(odd, a) / root, 0.0)))
-        for a, value in out:
-            extra[pl.ds(a, SUBLANES), :] = value
-        return carry
-
-    lax.fori_loop(low, chunks - low, one_height, 0)
-
-    def differences(chunk, carry):
+            out.append((extra, a, jnp.where(root > 0.0, rows_at(odd, a) / root, 0.0)))
+        return out
+
+    in_batches(range(low, chunks - low), one_height)
+
+    def differences(chunk):
         here, above, below, at = strip_rows(extra, chunk, deep)
         root, root_above, root_below, _ = strip_rows(root_ref, chunk, deep)
         out = []
@@ -576,11 +608,9 @@
             scaled = rows_at(around_ref, a) * (1.0 / step_scale)
             out.append((even, a, east_step))
             out.append((source, a, 0.25 * energy / jnp.maximum(scaled, 0.25)))
-        for ref, a, value in out:
-            ref[pl.ds(a, SUBLANES), :] = value
-        return carry
-
-    lax.fori_loop(low + 1, chunks - low - 1, differences, 0)
+        return out
+
+    in_batches(range(low + 1, chunks - low - 1), differences)
 
     def turn_back(ref, tile):
         for i in range(deep):
@@ -598,21 +628,17 @@
         push = pressure_gain * step
         lowest = bottom_ref[b, c] - push
 
-        def some_levels(base, size):
-            out = []
-            for j in range(size):
-                k = base + j
+        late = []
+        for low in range(0, depth, CHUNK):
+            batch = []
+            for k in range(low, min(low + CHUNK, depth)):
                 value = jnp.where(levels == k + 1, lowest, column[b, c, k] - push)
-                out.append((k, jnp.where(levels > k, value, 0.0)))
-            for k, value in out:
+                batch.append((k, jnp.where(levels > k, value, 0.0)))
+            for k, value in late:
                 column[b, c, k] = value
-
-        def one_chunk(chunk, inner):
-            some_levels(chunk * CHUNK, CHUNK)
-            return inner
-
-        lax.fori_loop(0, depth // CHUNK, one_chunk, 0)
-        some_levels(depth // CHUNK * CHUNK, depth % CHUNK)
+            late = batch
+        for k, value in late:
+            column[b, c, k] = value
         copy_out(b, c).start()
 
     turn_back(even, 0)

time: 66.4 us -> 58.6 us (0.88)
  Pallas kernels: 41.7 us -> 32.7 us
  waiting for transfers between devices: 6.04 us -> 7.42 us
  starting transfers between devices: 16.5 us -> 17.5 us
  local copies, waits for them, and re-layouts: 0.78 us -> 0.02 us
    pallas_call x1, Pallas kernels: 20 us -> 12.4 us  [surface_solve(): pl.pallas_call(functools.partial(solve_kernel, block_total), in_specs=[SM...]
    pallas_call x1, Pallas kernels: 4.33 us -> 2.74 us  [surface_weights(): pl.pallas_call(functools.partial(weights_kernel, slots, lon_count, lat_co...]
    ppermute x14, waiting for transfers between devices: 6.04 us -> 7.42 us  [swap(): return lax.ppermute(values, axis, [(i, i ^ mask) for i in range(count)])]
    ppermute x14, starting transfers between devices: 16.5 us -> 17.5 us  [swap(): return lax.ppermute(values, axis, [(i, i ^ mask) for i in range(count)])]
    unnamed x10 -> x8, local copies, waits for them, and re-layouts: 0.78 us -> 0.02 us
  transfers between devices with their start and end apart: 14 -> 14, of which waited for: 5 -> 3; matrix products, arithmetic and copies ran while one was open for 0% -> 0% of each run, Pallas kernels for 32% -> 33%
where the time goes in v1:
time: 58.6 us; the launch traced here: 58.4 us
  Pallas kernels  32.7 us (56%)
  starting transfers between devices  17.5 us (30%)
  waiting for transfers between devices  7.42 us (13%)
  between operations  0.81 us (1%)
    ppermute x14, starting transfers between devices, swap(): return lax.ppermute(values, axis, [(i, i ^ mask) for i in range(count)])  17.5 us
    pallas_call x1, Pallas kernels, surface_solve(): pl.pallas_call(functools.partial(solve_kernel, block_total), in_specs=[SM...  12.4 us
    pallas_call x2, Pallas kernels, column_mixing(): pl.pallas_call(functools.partial(mixing_kernel, block_total, first, len(e...  12.4 us
    ppermute x14, waiting for transfers between devices, swap(): return lax.ppermute(values, axis, [(i, i ^ mask) for i in range(count)])  7.42 us
    pallas_call x1, Pallas kernels, column_forcing(): pl.pallas_call(forcing_kernel, in_specs=[HBM, HBM], out_specs=VMEM, out_s...  4.18 us
    pallas_call x1, Pallas kernels, surface_weights(): pl.pallas_call(functools.partial(weights_kernel, slots, lon_count, lat_co...  2.74 us
  transfers between devices with their start and end apart: 14, of which 3 were waited for; matrix products, arithmetic and copies ran while one was open for 0% of the time, Pallas kernels for 33%

profile of v1, /device:TPU:0, one launch (start us, length us, event | category | flops | bytes accessed | tf_op | source)
XLA Modules:
  0.0 58.4 jit_solution(3439311358680407714)
XLA Ops:
  0.6 0.8 %depth_payload.1.refs_0_ = f32[72,128]{1,0:T(8,128)S(1)} custom-call(s32[4]{0:T(128)} %ids_ref.9, f32[32,256]{1,0:T(8,128)} %bathymetry_ref.1, s32[32,256]{1,0:T(8,128)} %mask_ref.1), custom_call_target="tpu_custom_call" | custom-call | tf_op jit(solution)/shard_map/depth_payload/pallas_call | solution.py:375
  1.4 0.0 copy-start
  1.5 0.0 copy-start.1
  1.5 0.0 copy-start.2
  1.5 5.1 %collective-permute-start.2 = (f32[72,128]{1,0:T(8,128)S(1)}, f32[72,128]{1,0:T(8,128)S(1)}, u32[]{:S(2)}, u32[]{:S(2)}) collective-permute-start(f32[72,128]{1,0:T(8,128)S(1)} %depth_payload.1.refs_0_), channel_id=1, source_target_pairs={{0,6},{1,7},{2,4},{3,5},{4,2},{5,3},{6,0},{7,1},{8,14},{9,15},{10,... | collective-permute-start | bytes 110600 | tf_op jit(solution)/shard_map/ppermute | solution.py:724
  6.6 0.0 collective-permute-start.1
  6.6 0.6 %collective-permute-start = (f32[72,128]{1,0:T(8,128)S(1)}, f32[72,128]{1,0:T(8,128)S(1)}, u32[]{:S(2)}, u32[]{:S(2)}) collective-permute-start(f32[72,128]{1,0:T(8,128)S(1)} %depth_payload.1.refs_0_), channel_id=1, source_target_pairs={{0,2},{1,3},{2,0},{3,1},{4,6},{5,7},{6,4},{7,5},{8,10},{9,11},{10,... | collective-permute-start | bytes 110600 | tf_op jit(solution)/shard_map/ppermute | solution.py:724
  7.2 4.2 %column_forcing.1.refs_4_.after_ref.refs_0_ = f32[4,32,128]{2,1,0:T(8,128)S(1)} custom-call(s32[4,32,128]{2,1,0:T(8,128)} %levels_ref.7, f32[4,2,62,32,128]{4,3,2,1,0:T(8,128)} %adjoint_ref.5), custom_call_target="tpu_custom_call" | custom-call | flops 4063232 | bytes 8126464 | tf_op jit(solution)/shard_map/column_forcing/pallas_call | solution.py:111
  11.4 0.0 collective-permute-done.2.refs_3_
  11.4 0.0 collective-permute-done.1.refs_2_
  11.5 0.0 collective-permute-done.refs_1_
  11.5 2.7 %collective-permute-start.5 = (f32[4,72,128]{2,1,0:T(8,128)S(1)}, f32[4,72,128]{2,1,0:T(8,128)S(1)}, u32[]{:S(2)}, u32[]{:S(2)}) collective-permute-start(f32[4,72,128]{2,1,0:T(8,128)S(1)} %stack_after.4.refs_0_), channel_id=1, source_target_pairs={{0,24},{8,16},{16,8},{24,0},{1,25},{9,17},{17,9},{25,1},{2,26},{10... | collective-permute-start | bytes 442376 | tf_op jit(solution)/shard_map/ppermute | solution.py:724
  14.1 0.5 collective-permute-start.4
  14.6 0.4 collective-permute-start.3
  15.0 3.7 %collective-permute-start.8 = (f32[4,32,128]{2,1,0:T(8,128)S(1)}, f32[4,32,128]{2,1,0:T(8,128)S(1)}, u32[]{:S(2)}, u32[]{:S(2)}) collective-permute-start(f32[4,32,128]{2,1,0:T(8,128)S(1)} %column_forcing.1.refs_4_.after_ref.refs_0_), channel_id=1, source_target_pairs={{0,6},{1,7},{2,4},{3,5},{4,2},{5,3},{6,0},{7,1},{8,14},{9,15},{10,... | collective-permute-start | bytes 196616 | tf_op jit(solution)/shard_map/ppermute | solution.py:724
  18.8 0.0 collective-permute-start.7
  18.8 2.4 %collective-permute-done.8.refs_3_ = f32[4,32,128]{2,1,0:T(8,128)S(1)} collective-permute-done((f32[4,32,128]{2,1,0:T(8,128)S(1)}, f32[4,32,128]{2,1,0:T(8,128)S(1)}, u32[]{:S(2)}, u32[]{:S(2)}) %collective-permute-start.8) | collective-permute-done | bytes 65568 | tf_op jit(solution)/shard_map/ppermute | solution.py:724
  21.2 0.7 %collective-permute-start.6 = (f32[4,32,128]{2,1,0:T(8,128)S(1)}, f32[4,32,128]{2,1,0:T(8,128)S(1)}, u32[]{:S(2)}, u32[]{:S(2)}) collective-permute-start(f32[4,32,128]{2,1,0:T(8,128)S(1)} %column_forcing.1.refs_4_.after_ref.refs_0_), channel_id=1, source_target_pairs={{0,2},{1,3},{2,0},{3,1},{4,6},{5,7},{6,4},{7,5},{8,10},{9,11},{10,... | collective-permute-start | bytes 196616 | tf_op jit(solution)/shard_map/ppermute | solution.py:724
  21.9 0.0 copy-done
  21.9 0.0 copy-done.1
  21.9 0.0 copy-done.2
  21.9 5.8 %column_mixing.2 = (f32[2,2,62,32,128]{4,3,2,1,0:T(8,128)}, f32[2,2,32,128]{3,2,1,0:T(8,128)S(1)}, f32[2,32,128]{2,1,0:T(8,128)S(1)}) custom-call(s32[4]{0:T(128)S(1)} %copy-done.2, s32[4,32,128]{2,1,0:T(8,128)S(1)} %copy-done, f32[4,32,128]{2,1,0:T(8,128)S(1)} %copy-done.1, f32[4,2,62,32,128]{4,3,2,1,0:T(8,128)} %adjoint_ref.5, ...), custom_call_target="tpu_custom_call" | custom-call | flops 14221312 | bytes 10158080 | tf_op jit(solution)/shard_map/column_mixing/pallas_call | solution.py:256
  27.8 0.0 collective-permute-done.7.refs_2_
  27.8 0.0 collective-permute-done.6.refs_1_
  27.8 0.0 collective-permute-done.5.refs_3_
  27.8 0.0 collective-permute-done.4.refs_2_
  27.8 0.0 collective-permute-done.3.refs_1_
  27.9 0.1 collective-permute-start.9
  28.0 2.0 %collective-permute-start.12 = (f32[4,4,32,128]{3,2,1,0:T(8,128)S(1)}, f32[4,4,32,128]{3,2,1,0:T(8,128)S(1)}, u32[]{:S(2)}, u32[]{:S(2)}) collective-permute-start(f32[4,4,32,128]{3,2,1,0:T(8,128)S(1)} %stack_after.5.refs_4_.after_ref.refs_0_), channel_id=1, source_target_pairs={{0,24},{8,16},{16,8},{24,0},{1,25},{9,17},{17,9},{25,1},{2,26},{10... | collective-permute-start | bytes 786440 | tf_op jit(solution)/shard_map/ppermute | solution.py:724
  30.0 0.5 collective-permute-start.11
  30.5 1.0 %collective-permute-start.10 = (f32[4,4,32,128]{3,2,1,0:T(8,128)S(1)}, f32[4,4,32,128]{3,2,1,0:T(8,128)S(1)}, u32[]{:S(2)}, u32[]{:S(2)}) collective-permute-start(f32[4,4,32,128]{3,2,1,0:T(8,128)S(1)} %stack_after.5.refs_4_.after_ref.refs_0_), channel_id=1, source_target_pairs={{0,8},{8,0},{16,24},{24,16},{1,9},{9,1},{17,25},{25,17},{2,10},{10... | collective-permute-start | bytes 786440 | tf_op jit(solution)/shard_map/ppermute | solution.py:724
  31.5 0.1 pad_add_fusion.me_ref
  31.6 0.0 copy-start.3
  31.6 6.5 %column_mixing.3 = (f32[2,2,62,32,128]{4,3,2,1,0:T(8,128)}, f32[4,2,32,128]{3,2,1,0:T(8,128)S(1)}, f32[4,32,128]{2,1,0:T(8,128)}) custom-call(s32[4]{0:T(128)S(1)} %copy-done.2, s32[4,32,128]{2,1,0:T(8,128)S(1)} %copy-done, f32[4,32,128]{2,1,0:T(8,128)S(1)} %copy-done.1, f32[4,2,62,32,128]{4,3,2,1,0:T(8,128)} %adjoint_ref.5, ...), custom_call_target="tpu_custom_call" | custom-call | flops 14221312 | bytes 10158080 | tf_op jit(solution)/shard_map/column_mixing/pallas_call | solution.py:256
  38.1 0.0 collective-permute-done.9.far_ref
  38.1 2.7 %surface_weights.1 = (f32[1040,128]{1,0:T(8,128)S(1)}, f32[1040,128]{1,0:T(8,128)S(1)}, f32[1040,128]{1,0:T(8,128)S(1)}, s32[54]{0:T(128)S(1)}) custom-call(s32[2]{0:T(128)S(1)} %pad_add_fusion.me_ref, s32[4]{0:T(128)S(1)} %copy-done.2, f32[16,72,128]{2,1,0:T(8,128)S(1)} %bitcast.7, f32[16,72,128]{2,1,0:T(8,128)S(1)} %collective-permute-done.9.far_ref), custom_call_target="tpu_custom_call" | custom-call | bytes 8388608 | tf_op jit(solution)/shard_map/surface_weights/pallas_call | solution.py:476
  40.9 0.0 collective-permute-done.12.refs_3_
  40.9 2.3 %collective-permute-done.11.refs_2_ = f32[4,4,32,128]{3,2,1,0:T(8,128)S(1)} collective-permute-done((f32[4,4,32,128]{3,2,1,0:T(8,128)S(1)}, f32[4,4,32,128]{3,2,1,0:T(8,128)S(1)}, u32[]{:S(2)}, u32[]{:S(2)}) %collective-permute-start.11) | collective-permute-done | bytes 262176 | tf_op jit(solution)/shard_map/ppermute | solution.py:724
  43.2 0.0 collective-permute-done.10.refs_1_
  43.2 0.1 stack_after.7
  43.3 0.1 collective-permute-start.13
  43.4 2.6 %collective-permute-done.13 = f32[4,4,4,32,128]{4,3,2,1,0:T(8,128)S(1)} collective-permute-done((f32[4,4,4,32,128]{4,3,2,1,0:T(8,128)S(1)}, f32[4,4,4,32,128]{4,3,2,1,0:T(8,128)S(1)}, u32[]{:S(2)}, u32[]{:S(2)}) %collective-permute-start.13) | collective-permute-done | bytes 1048608 | tf_op jit(solution)/shard_map/ppermute | solution.py:724
  46.0 0.0 copy-done.3
  46.0 12.4 %surface_solve.1 = (f32[4,2,62,32,128]{4,3,2,1,0:T(8,128)}, f32[32,256]{1,0:T(8,128)}, f32[32,256]{1,0:T(8,128)}) custom-call(s32[4]{0:T(128)S(1)} %copy-done.2, s32[54]{0:T(128)S(1)} %get-tuple-element.18.table_ref, f32[32]{0:T(128)S(1)} %copy-done.3, f32[1040,128]{1,0:T(8,128)S(1)} %get-tuple-element.19.refs_5_.root_ref, ...), custom_call_target="tpu_custom_call" | custom-call | flops 38338560 | bytes 2129920 | tf_op jit(solution)/shard_map/surface_solve/pallas_call | solution.py:678
  (3 shorter events, 0.1 us)
Async XLA Ops:
  1.4 20.5 %copy-start = (s32[4,32,128]{2,1,0:T(8,128)S(1)}, s32[4,32,128]{2,1,0:T(8,128)}, u32[]{:S(2)}) copy-start(s32[4,32,128]{2,1,0:T(8,128)} %levels_ref.7) | copy-start | bytes 196612
  1.5 20.4 %copy-start.1 = (f32[4,32,128]{2,1,0:T(8,128)S(1)}, f32[4,32,128]{2,1,0:T(8,128)}, u32[]{:S(2)}) copy-start(f32[4,32,128]{2,1,0:T(8,128)} %drag_ref.3) | copy-start | bytes 196612
  1.5 20.4 %copy-start.2 = (s32[4]{0:T(128)S(1)}, s32[4]{0:T(128)}, u32[]{:S(2)}) copy-start(s32[4]{0:T(128)} %ids_ref.9) | copy-start | bytes 52
  1.5 9.9 %collective-permute-start.2 = (f32[72,128]{1,0:T(8,128)S(1)}, f32[72,128]{1,0:T(8,128)S(1)}, u32[]{:S(2)}, u32[]{:S(2)}) collective-permute-start(f32[72,128]{1,0:T(8,128)S(1)} %depth_payload.1.refs_0_), channel_id=1, source_target_pairs={{0,6},{1,7},{2,4},{3,5},{4,2},{5,3},{6,0},{7,1},{8,14},{9,15},{10,... | collective-permute-start | bytes 110600 | tf_op jit(solution)/shard_map/ppermute | solution.py:724
  6.6 4.9 %collective-permute-start.1 = (f32[72,128]{1,0:T(8,128)S(1)}, f32[72,128]{1,0:T(8,128)S(1)}, u32[]{:S(2)}, u32[]{:S(2)}) collective-permute-start(f32[72,128]{1,0:T(8,128)S(1)} %depth_payload.1.refs_0_), channel_id=1, source_target_pairs={{0,4},{1,5},{2,6},{3,7},{4,0},{5,1},{6,2},{7,3},{8,12},{9,13},{10,... | collective-permute-start | bytes 110600 | tf_op jit(solution)/shard_map/ppermute | solution.py:724
  6.6 4.9 %collective-permute-start = (f32[72,128]{1,0:T(8,128)S(1)}, f32[72,128]{1,0:T(8,128)S(1)}, u32[]{:S(2)}, u32[]{:S(2)}) collective-permute-start(f32[72,128]{1,0:T(8,128)S(1)} %depth_payload.1.refs_0_), channel_id=1, source_target_pairs={{0,2},{1,3},{2,0},{3,1},{4,6},{5,7},{6,4},{7,5},{8,10},{9,11},{10,... | collective-permute-start | bytes 110600 | tf_op jit(solution)/shard_map/ppermute | solution.py:724
  11.5 16.3 %collective-permute-start.5 = (f32[4,72,128]{2,1,0:T(8,128)S(1)}, f32[4,72,128]{2,1,0:T(8,128)S(1)}, u32[]{:S(2)}, u32[]{:S(2)}) collective-permute-start(f32[4,72,128]{2,1,0:T(8,128)S(1)} %stack_after.4.refs_0_), channel_id=1, source_target_pairs={{0,24},{8,16},{16,8},{24,0},{1,25},{9,17},{17,9},{25,1},{2,26},{10... | collective-permute-start | bytes 442376 | tf_op jit(solution)/shard_map/ppermute | solution.py:724
  14.1 13.7 %collective-permute-start.4 = (f32[4,72,128]{2,1,0:T(8,128)S(1)}, f32[4,72,128]{2,1,0:T(8,128)S(1)}, u32[]{:S(2)}, u32[]{:S(2)}) collective-permute-start(f32[4,72,128]{2,1,0:T(8,128)S(1)} %stack_after.4.refs_0_), channel_id=1, source_target_pairs={{0,16},{8,24},{16,0},{24,8},{1,17},{9,25},{17,1},{25,9},{2,18},{10... | collective-permute-start | bytes 442376 | tf_op jit(solution)/shard_map/ppermute | solution.py:724
  14.6 13.2 %collective-permute-start.3 = (f32[4,72,128]{2,1,0:T(8,128)S(1)}, f32[4,72,128]{2,1,0:T(8,128)S(1)}, u32[]{:S(2)}, u32[]{:S(2)}) collective-permute-start(f32[4,72,128]{2,1,0:T(8,128)S(1)} %stack_after.4.refs_0_), channel_id=1, source_target_pairs={{0,8},{8,0},{16,24},{24,16},{1,9},{9,1},{17,25},{25,17},{2,10},{10... | collective-permute-start | bytes 442376 | tf_op jit(solution)/shard_map/ppermute | solution.py:724
  15.0 6.2 %collective-permute-start.8 = (f32[4,32,128]{2,1,0:T(8,128)S(1)}, f32[4,32,128]{2,1,0:T(8,128)S(1)}, u32[]{:S(2)}, u32[]{:S(2)}) collective-permute-start(f32[4,32,128]{2,1,0:T(8,128)S(1)} %column_forcing.1.refs_4_.after_ref.refs_0_), channel_id=1, source_target_pairs={{0,6},{1,7},{2,4},{3,5},{4,2},{5,3},{6,0},{7,1},{8,14},{9,15},{10,... | collective-permute-start | bytes 196616 | tf_op jit(solution)/shard_map/ppermute | solution.py:724
  18.8 9.0 %collective-permute-start.7 = (f32[4,32,128]{2,1,0:T(8,128)S(1)}, f32[4,32,128]{2,1,0:T(8,128)S(1)}, u32[]{:S(2)}, u32[]{:S(2)}) collective-permute-start(f32[4,32,128]{2,1,0:T(8,128)S(1)} %column_forcing.1.refs_4_.after_ref.refs_0_), channel_id=1, source_target_pairs={{0,4},{1,5},{2,6},{3,7},{4,0},{5,1},{6,2},{7,3},{8,12},{9,13},{10,... | collective-permute-start | bytes 196616 | tf_op jit(solution)/shard_map/ppermute | solution.py:724
  21.2 6.6 %collective-permute-start.6 = (f32[4,32,128]{2,1,0:T(8,128)S(1)}, f32[4,32,128]{2,1,0:T(8,128)S(1)}, u32[]{:S(2)}, u32[]{:S(2)}) collective-permute-start(f32[4,32,128]{2,1,0:T(8,128)S(1)} %column_forcing.1.refs_4_.after_ref.refs_0_), channel_id=1, source_target_pairs={{0,2},{1,3},{2,0},{3,1},{4,6},{5,7},{6,4},{7,5},{8,10},{9,11},{10,... | collective-permute-start | bytes 196616 | tf_op jit(solution)/shard_map/ppermute | solution.py:724
  27.9 10.2 %collective-permute-start.9 = (f32[16,72,128]{2,1,0:T(8,128)S(1)}, f32[16,72,128]{2,1,0:T(8,128)S(1)}, u32[]{:S(2)}, u32[]{:S(2)}) collective-permute-start(f32[16,72,128]{2,1,0:T(8,128)S(1)} %bitcast.6), channel_id=1, source_target_pairs={{0,1},{1,0},{2,3},{3,2},{4,5},{5,4},{6,7},{7,6},{8,9},{9,8},{10,11... | collective-permute-start | bytes 1769480 | tf_op jit(solution)/shard_map/ppermute | solution.py:724
  28.0 12.9 %collective-permute-start.12 = (f32[4,4,32,128]{3,2,1,0:T(8,128)S(1)}, f32[4,4,32,128]{3,2,1,0:T(8,128)S(1)}, u32[]{:S(2)}, u32[]{:S(2)}) collective-permute-start(f32[4,4,32,128]{3,2,1,0:T(8,128)S(1)} %stack_after.5.refs_4_.after_ref.refs_0_), channel_id=1, source_target_pairs={{0,24},{8,16},{16,8},{24,0},{1,25},{9,17},{17,9},{25,1},{2,26},{10... | collective-permute-start | bytes 786440 | tf_op jit(solution)/shard_map/ppermute | solution.py:724
  30.0 13.2 %collective-permute-start.11 = (f32[4,4,32,128]{3,2,1,0:T(8,128)S(1)}, f32[4,4,32,128]{3,2,1,0:T(8,128)S(1)}, u32[]{:S(2)}, u32[]{:S(2)}) collective-permute-start(f32[4,4,32,128]{3,2,1,0:T(8,128)S(1)} %stack_after.5.refs_4_.after_ref.refs_0_), channel_id=1, source_target_pairs={{0,16},{8,24},{16,0},{24,8},{1,17},{9,25},{17,1},{25,9},{2,18},{10... | collective-permute-start | bytes 786440 | tf_op jit(solution)/shard_map/ppermute | solution.py:724
  30.5 12.7 %collective-permute-start.10 = (f32[4,4,32,128]{3,2,1,0:T(8,128)S(1)}, f32[4,4,32,128]{3,2,1,0:T(8,128)S(1)}, u32[]{:S(2)}, u32[]{:S(2)}) collective-permute-start(f32[4,4,32,128]{3,2,1,0:T(8,128)S(1)} %stack_after.5.refs_4_.after_ref.refs_0_), channel_id=1, source_target_pairs={{0,8},{8,0},{16,24},{24,16},{1,9},{9,1},{17,25},{25,17},{2,10},{10... | collective-permute-start | bytes 786440 | tf_op jit(solution)/shard_map/ppermute | solution.py:724
  31.6 14.4 %copy-start.3 = (f32[32]{0:T(128)S(1)}, f32[32]{0:T(128)}, u32[]{:S(2)}) copy-start(f32[32]{0:T(128)} %constant.10.clone.coefs_ref) | copy-start | bytes 388
  43.3 2.7 %collective-permute-start.13 = (f32[4,4,4,32,128]{4,3,2,1,0:T(8,128)S(1)}, f32[4,4,4,32,128]{4,3,2,1,0:T(8,128)S(1)}, u32[]{:S(2)}, u32[]{:S(2)}) collective-permute-start(f32[4,4,4,32,128]{4,3,2,1,0:T(8,128)S(1)} %stack_after.7), channel_id=1, source_target_pairs={{0,1},{1,0},{2,3},{3,2},{4,5},{5,4},{6,7},{7,6},{8,9},{9,8},{10,11... | collective-permute-start | bytes 3145736 | tf_op jit(solution)/shard_map/ppermute | solution.py:724

commit v2 on v1

--- a/solution.py
+++ b/solution.py
@@ -64,42 +64,26 @@
 HBM = pl.BlockSpec(memory_space=pltpu.HBM)
 
 
-CUTS = 2
-
-
-def level_cuts(depth):
-    step = pl.cdiv(depth, CUTS)
-    return [(n, n * step, min(step, depth - n * step)) for n in range(CUTS)]
-
-
 def forcing_kernel(levels_ref, adjoint_ref, out_ref, levels_held, held, level_sem, sems):
     slots, comps, depth, rows, cols = held.shape
     level_copy = pltpu.make_async_copy(levels_ref, levels_held, level_sem)
     level_copy.start()
 
-    def copies_in(b):
-        return [
-            pltpu.make_async_copy(
-                adjoint_ref.at[b, c, pl.ds(low, size)], held.at[b, c, pl.ds(low, size)],
-                sems.at[b, c, n],
-            )
-            for c in range(comps)
-            for n, low, size in level_cuts(depth)
-        ]
+    def copy_in(b, c):
+        return pltpu.make_async_copy(adjoint_ref.at[b, c], held.at[b, c], sems.at[b, c])
 
     for b in range(slots):
-        for copy in copies_in(b):
-            copy.start()
+        for c in range(comps):
+            copy_in(b, c).start()
     level_copy.wait()
 
     def one_slot(b, carry):
-        for copy in copies_in(b):
-            copy.wait()
         levels = levels_held[b]
         totals = [jnp.zeros((rows, cols), jnp.float32) for _ in range(4)]
-        for k in range(depth):
-            both = held[b, 0, k] + held[b, 1, k]
-            totals[k % 4] = totals[k % 4] + jnp.where(levels > k, both, 0.0)
+        for c in range(comps):
+            copy_in(b, c).wait()
+            for k in range(depth):
+                totals[k % 4] = totals[k % 4] + jnp.where(levels > k, held[b, c, k], 0.0)
         out_ref[b] = force_scale * ((totals[0] + totals[1]) + (totals[2] + totals[3]))
         return carry
 
@@ -117,7 +101,7 @@
             pltpu.VMEM(level_count.shape, jnp.int32),
             pltpu.VMEM(adjoint_vel.shape, jnp.float32),
             pltpu.SemaphoreType.DMA,
-            pltpu.SemaphoreType.DMA((slots, comps, CUTS)),
+            pltpu.SemaphoreType.DMA((slots, comps)),
         ],
         compiler_params=params(FIRST_VMEM),
         cost_estimate=pl.CostEstimate(
@@ -143,22 +127,18 @@
 
     def copies_in(b):
         return [
-            pltpu.make_async_copy(
-                source.at[first + b, c, pl.ds(low, size)], target.at[b, c, pl.ds(low, size)],
-                in_sems.at[which, b, c, n],
-            )
-            for which, (source, target) in enumerate(
+            pltpu.make_async_copy(source.at[first + b, c], target.at[b, c], in_sems.at[n, b, c])
+            for n, (source, target) in enumerate(
                 ((adjoint_ref, adjoint), (velocity_ref, velocity))
             )
             for c in range(comps)
-            for n, low, size in level_cuts(depth)
         ]
 
-    def copies_out(b):
-        return [
-            pltpu.make_async_copy(column.at[b, c], column_ref.at[b, c], out_sems.at[b, c])
-            for c in range(comps)
-        ]
+    def copy_out(b, index):
+        span = pl.ds(pl.multiple_of(index * group, group), group)
+        return pltpu.make_async_copy(
+            column.at[b, :, :, span], column_ref.at[b, :, :, span], out_sems.at[b, index]
+        )
 
     for b in range(slots):
         for copy in copies_in(b):
@@ -233,18 +213,13 @@
                 copy.wait()
 
         one_group(b, index)
-
-        @pl.when(index == parts - 1)
-        def _():
-            for copy in copies_out(b):
-                copy.start()
-
+        copy_out(b, index).start()
         return carry
 
     lax.fori_loop(0, slots * parts, one, 0)
     for b in range(slots):
-        for copy in copies_out(b):
-            copy.wait()
+        for index in range(parts):
+            copy_out(b, index).wait()
 
 
 def column_mixing(adjoint_vel, velocity, drag_coef, level_count, block_ids, after, block_total,
@@ -266,8 +241,8 @@
             pltpu.VMEM(part, adjoint_vel.dtype),
             pltpu.VMEM(part, velocity.dtype),
             pltpu.VMEM(part, jnp.float32),
-            pltpu.SemaphoreType.DMA((2, slots, comps, CUTS)),
-            pltpu.SemaphoreType.DMA((slots, comps)),
+            pltpu.SemaphoreType.DMA((2, slots, comps)),
+            pltpu.SemaphoreType.DMA((slots, rows // 16)),
         ],
         compiler_params=params(MIXING_VMEM),
         cost_estimate=pl.CostEstimate(
@@ -738,7 +713,7 @@
     forcing = column_forcing(adjoint_vel, level_count)
 
     parts = [forcing] + [swap(forcing, "gy", 2 * m) for m in range(1, half)]
-    near_depths = stack_after(depth_parts, forcing)
+    near_depths = stack_after(depth_parts, parts[1])
     near_depths = [near_depths] + [swap(near_depths, "gx", m) for m in range(1, lon_count)]
     columns = (adjoint_vel, velocity, drag_coef, level_count, block_ids)
     middle = (slots + 1) // 2

time: 58.6 us -> 58.5 us (level)
  waiting for transfers between devices: 7.42 us -> 8.81 us
  Pallas kernels: 32.7 us -> 31.7 us
  starting transfers between devices: 17.5 us -> 16.9 us
    ppermute x14, waiting for transfers between devices: 7.42 us -> 8.81 us  [swap(): return lax.ppermute(values, axis, [(i, i ^ mask) for i in range(count)])]
    pallas_call x2, Pallas kernels: 12.4 us -> 11.6 us  [column_mixing(): pl.pallas_call(functools.partial(mixing_kernel, block_total, first, len(e...]
    ppermute x14, starting transfers between devices: 17.5 us -> 16.9 us  [swap(): return lax.ppermute(values, axis, [(i, i ^ mask) for i in range(count)])]
  transfers between devices with their start and end apart: 14 -> 14, of which waited for: 3 -> 5; matrix products, arithmetic and copies ran while one was open for 0% -> 0% of each run, Pallas kernels for 33% -> 26%
where the time goes in v2:
time: 58.5 us; the launch traced here: 58.3 us
  Pallas kernels  31.7 us (54%)
  starting transfers between devices  16.9 us (29%)
  waiting for transfers between devices  8.81 us (15%)
  between operations  0.8 us (1%)
    ppermute x14, starting transfers between devices, swap(): return lax.ppermute(values, axis, [(i, i ^ mask) for i in range(count)])  16.9 us
    pallas_call x1, Pallas kernels, surface_solve(): pl.pallas_call(functools.partial(solve_kernel, block_total), in_specs=[SM...  12.4 us
    pallas_call x2, Pallas kernels, column_mixing(): pl.pallas_call(functools.partial(mixing_kernel, block_total, first, len(e...  11.6 us
    ppermute x14, waiting for transfers between devices, swap(): return lax.ppermute(values, axis, [(i, i ^ mask) for i in range(count)])  8.81 us
    pallas_call x1, Pallas kernels, column_forcing(): pl.pallas_call(forcing_kernel, in_specs=[HBM, HBM], out_specs=VMEM, out_s...  3.99 us
    pallas_call x1, Pallas kernels, surface_weights(): pl.pallas_call(functools.partial(weights_kernel, slots, lon_count, lat_co...  2.74 us
  transfers between devices with their start and end apart: 14, of which 5 were waited for; matrix products, arithmetic and copies ran while one was open for 0% of the time, Pallas kernels for 26%

profile of v2, /device:TPU:0, one launch (start us, length us, event | category | flops | bytes accessed | tf_op | source)
XLA Modules:
  0.0 58.3 jit_solution(4060741322493748732)
XLA Ops:
  0.6 0.0 copy-start
  0.6 0.0 copy-start.2
  0.7 0.0 copy-start.1
  0.7 4.0 %column_forcing.1.after_ref.refs_0_ = f32[4,32,128]{2,1,0:T(8,128)S(1)} custom-call(s32[4,32,128]{2,1,0:T(8,128)} %levels_ref.7, f32[4,2,62,32,128]{4,3,2,1,0:T(8,128)} %adjoint_ref.5), custom_call_target="tpu_custom_call" | custom-call | flops 4063232 | bytes 8126464 | tf_op jit(solution)/shard_map/column_forcing/pallas_call | solution.py:95
  4.7 3.1 %collective-permute-start.3 = (f32[4,32,128]{2,1,0:T(8,128)S(1)}, f32[4,32,128]{2,1,0:T(8,128)S(1)}, u32[]{:S(2)}, u32[]{:S(2)}) collective-permute-start(f32[4,32,128]{2,1,0:T(8,128)S(1)} %column_forcing.1.after_ref.refs_0_), channel_id=1, source_target_pairs={{0,2},{1,3},{2,0},{3,1},{4,6},{5,7},{6,4},{7,5},{8,10},{9,11},{10,... | collective-permute-start | bytes 196616 | tf_op jit(solution)/shard_map/ppermute | solution.py:699
  7.8 0.8 %depth_payload.1.refs_0_ = f32[72,128]{1,0:T(8,128)S(1)} custom-call(s32[4]{0:T(128)} %ids_ref.9, f32[32,256]{1,0:T(8,128)} %bathymetry_ref.1, s32[32,256]{1,0:T(8,128)} %mask_ref.1), custom_call_target="tpu_custom_call" | custom-call | tf_op jit(solution)/shard_map/depth_payload/pallas_call | solution.py:350
  8.6 2.5 %collective-permute-start.2 = (f32[72,128]{1,0:T(8,128)S(1)}, f32[72,128]{1,0:T(8,128)S(1)}, u32[]{:S(2)}, u32[]{:S(2)}) collective-permute-start(f32[72,128]{1,0:T(8,128)S(1)} %depth_payload.1.refs_0_), channel_id=1, source_target_pairs={{0,6},{1,7},{2,4},{3,5},{4,2},{5,3},{6,0},{7,1},{8,14},{9,15},{10,... | collective-permute-start | bytes 110600 | tf_op jit(solution)/shard_map/ppermute | solution.py:699
  11.1 0.2 collective-permute-start.1
  11.3 1.7 %collective-permute-start = (f32[72,128]{1,0:T(8,128)S(1)}, f32[72,128]{1,0:T(8,128)S(1)}, u32[]{:S(2)}, u32[]{:S(2)}) collective-permute-start(f32[72,128]{1,0:T(8,128)S(1)} %depth_payload.1.refs_0_), channel_id=1, source_target_pairs={{0,2},{1,3},{2,0},{3,1},{4,6},{5,7},{6,4},{7,5},{8,10},{9,11},{10,... | collective-permute-start | bytes 110600 | tf_op jit(solution)/shard_map/ppermute | solution.py:699
  13.0 1.9 %collective-permute-done.2.refs_3_ = f32[72,128]{1,0:T(8,128)S(1)} collective-permute-done((f32[72,128]{1,0:T(8,128)S(1)}, f32[72,128]{1,0:T(8,128)S(1)}, u32[]{:S(2)}, u32[]{:S(2)}) %collective-permute-start.2) | collective-permute-done | bytes 36896 | tf_op jit(solution)/shard_map/ppermute | solution.py:699
  14.9 1.5 %collective-permute-done.1.refs_2_ = f32[72,128]{1,0:T(8,128)S(1)} collective-permute-done((f32[72,128]{1,0:T(8,128)S(1)}, f32[72,128]{1,0:T(8,128)S(1)}, u32[]{:S(2)}, u32[]{:S(2)}) %collective-permute-start.1) | collective-permute-done | bytes 36896 | tf_op jit(solution)/shard_map/ppermute | solution.py:699
  16.4 0.0 collective-permute-done.refs_1_
  16.4 0.0 collective-permute-done.3.refs_4_.refs_1_
  16.4 2.5 %collective-permute-start.6 = (f32[4,72,128]{2,1,0:T(8,128)S(1)}, f32[4,72,128]{2,1,0:T(8,128)S(1)}, u32[]{:S(2)}, u32[]{:S(2)}) collective-permute-start(f32[4,72,128]{2,1,0:T(8,128)S(1)} %stack_after.4.refs_0_), channel_id=1, source_target_pairs={{0,24},{8,16},{16,8},{24,0},{1,25},{9,17},{17,9},{25,1},{2,26},{10... | collective-permute-start | bytes 442376 | tf_op jit(solution)/shard_map/ppermute | solution.py:699
  18.9 0.5 collective-permute-start.5
  19.4 0.5 collective-permute-start.4
  19.9 1.9 %collective-permute-start.8 = (f32[4,32,128]{2,1,0:T(8,128)S(1)}, f32[4,32,128]{2,1,0:T(8,128)S(1)}, u32[]{:S(2)}, u32[]{:S(2)}) collective-permute-start(f32[4,32,128]{2,1,0:T(8,128)S(1)} %column_forcing.1.after_ref.refs_0_), channel_id=1, source_target_pairs={{0,6},{1,7},{2,4},{3,5},{4,2},{5,3},{6,0},{7,1},{8,14},{9,15},{10,... | collective-permute-start | bytes 196616 | tf_op jit(solution)/shard_map/ppermute | solution.py:699
  21.8 0.2 collective-permute-start.7
  22.0 0.0 copy-done
  22.0 0.0 copy-done.2
  22.0 0.0 copy-done.1
  22.0 5.5 %column_mixing.2 = (f32[2,2,62,32,128]{4,3,2,1,0:T(8,128)}, f32[2,2,32,128]{3,2,1,0:T(8,128)S(1)}, f32[2,32,128]{2,1,0:T(8,128)S(1)}) custom-call(s32[4]{0:T(128)S(1)} %copy-done.2, s32[4,32,128]{2,1,0:T(8,128)S(1)} %copy-done, f32[4,32,128]{2,1,0:T(8,128)S(1)} %copy-done.1, f32[4,2,62,32,128]{4,3,2,1,0:T(8,128)} %adjoint_ref.5, ...), custom_call_target="tpu_custom_call" | custom-call | flops 14221312 | bytes 10158080 | tf_op jit(solution)/shard_map/column_mixing/pallas_call | solution.py:231
  27.5 0.0 collective-permute-done.8.refs_3_
  27.5 0.0 collective-permute-done.7.refs_2_
  27.6 0.0 collective-permute-done.6.refs_3_
  27.6 0.0 collective-permute-done.5.refs_2_
  27.6 0.0 collective-permute-done.4.refs_1_
  27.6 0.1 collective-permute-start.9
  27.7 2.5 %collective-permute-start.12 = (f32[4,4,32,128]{3,2,1,0:T(8,128)S(1)}, f32[4,4,32,128]{3,2,1,0:T(8,128)S(1)}, u32[]{:S(2)}, u32[]{:S(2)}) collective-permute-start(f32[4,4,32,128]{3,2,1,0:T(8,128)S(1)} %stack_after.5.refs_4_.after_ref.refs_0_), channel_id=1, source_target_pairs={{0,24},{8,16},{16,8},{24,0},{1,25},{9,17},{17,9},{25,1},{2,26},{10... | collective-permute-start | bytes 786440 | tf_op jit(solution)/shard_map/ppermute | solution.py:699
  30.2 0.5 collective-permute-start.11
  30.7 0.5 collective-permute-start.10
  31.3 0.1 pad_add_fusion.me_ref
  31.4 0.0 copy-start.3
  31.4 6.1 %column_mixing.3 = (f32[2,2,62,32,128]{4,3,2,1,0:T(8,128)}, f32[4,2,32,128]{3,2,1,0:T(8,128)S(1)}, f32[4,32,128]{2,1,0:T(8,128)}) custom-call(s32[4]{0:T(128)S(1)} %copy-done.2, s32[4,32,128]{2,1,0:T(8,128)S(1)} %copy-done, f32[4,32,128]{2,1,0:T(8,128)S(1)} %copy-done.1, f32[4,2,62,32,128]{4,3,2,1,0:T(8,128)} %adjoint_ref.5, ...), custom_call_target="tpu_custom_call" | custom-call | flops 14221312 | bytes 10158080 | tf_op jit(solution)/shard_map/column_mixing/pallas_call | solution.py:231
  37.5 0.0 collective-permute-done.9.far_ref
  37.5 2.7 %surface_weights.1 = (f32[1040,128]{1,0:T(8,128)S(1)}, f32[1040,128]{1,0:T(8,128)S(1)}, f32[1040,128]{1,0:T(8,128)S(1)}, s32[54]{0:T(128)S(1)}) custom-call(s32[2]{0:T(128)S(1)} %pad_add_fusion.me_ref, s32[4]{0:T(128)S(1)} %copy-done.2, f32[16,72,128]{2,1,0:T(8,128)S(1)} %bitcast.7, f32[16,72,128]{2,1,0:T(8,128)S(1)} %collective-permute-done.9.far_ref), custom_call_target="tpu_custom_call" | custom-call | bytes 8388608 | tf_op jit(solution)/shard_map/surface_weights/pallas_call | solution.py:451
  40.3 0.0 collective-permute-done.12.refs_3_
  40.3 2.7 %collective-permute-done.11.refs_2_ = f32[4,4,32,128]{3,2,1,0:T(8,128)S(1)} collective-permute-done((f32[4,4,32,128]{3,2,1,0:T(8,128)S(1)}, f32[4,4,32,128]{3,2,1,0:T(8,128)S(1)}, u32[]{:S(2)}, u32[]{:S(2)}) %collective-permute-start.11) | collective-permute-done | bytes 262176 | tf_op jit(solution)/shard_map/ppermute | solution.py:699
  43.0 0.1 collective-permute-done.10.refs_1_
  43.1 0.1 stack_after.7
  43.1 0.1 collective-permute-start.13
  43.2 2.6 %collective-permute-done.13 = f32[4,4,4,32,128]{4,3,2,1,0:T(8,128)S(1)} collective-permute-done((f32[4,4,4,32,128]{4,3,2,1,0:T(8,128)S(1)}, f32[4,4,4,32,128]{4,3,2,1,0:T(8,128)S(1)}, u32[]{:S(2)}, u32[]{:S(2)}) %collective-permute-start.13) | collective-permute-done | bytes 1048608 | tf_op jit(solution)/shard_map/ppermute | solution.py:699
  45.9 0.0 copy-done.3
  45.9 12.4 %surface_solve.1 = (f32[4,2,62,32,128]{4,3,2,1,0:T(8,128)}, f32[32,256]{1,0:T(8,128)}, f32[32,256]{1,0:T(8,128)}) custom-call(s32[4]{0:T(128)S(1)} %copy-done.2, s32[54]{0:T(128)S(1)} %get-tuple-element.18.table_ref, f32[32]{0:T(128)S(1)} %copy-done.3, f32[1040,128]{1,0:T(8,128)S(1)} %get-tuple-element.19.refs_5_.root_ref, ...), custom_call_target="tpu_custom_call" | custom-call | flops 38338560 | bytes 2129920 | tf_op jit(solution)/shard_map/surface_solve/pallas_call | solution.py:653
  (3 shorter events, 0.1 us)
Async XLA Ops:
  0.6 21.4 %copy-start = (s32[4,32,128]{2,1,0:T(8,128)S(1)}, s32[4,32,128]{2,1,0:T(8,128)}, u32[]{:S(2)}) copy-start(s32[4,32,128]{2,1,0:T(8,128)} %levels_ref.7) | copy-start | bytes 196612
  0.6 21.4 %copy-start.2 = (s32[4]{0:T(128)S(1)}, s32[4]{0:T(128)}, u32[]{:S(2)}) copy-start(s32[4]{0:T(128)} %ids_ref.9) | copy-start | bytes 52
  0.7 21.4 %copy-start.1 = (f32[4,32,128]{2,1,0:T(8,128)S(1)}, f32[4,32,128]{2,1,0:T(8,128)}, u32[]{:S(2)}) copy-start(f32[4,32,128]{2,1,0:T(8,128)} %drag_ref.3) | copy-start | bytes 196612
  4.7 11.7 %collective-permute-start.3 = (f32[4,32,128]{2,1,0:T(8,128)S(1)}, f32[4,32,128]{2,1,0:T(8,128)S(1)}, u32[]{:S(2)}, u32[]{:S(2)}) collective-permute-start(f32[4,32,128]{2,1,0:T(8,128)S(1)} %column_forcing.1.after_ref.refs_0_), channel_id=1, source_target_pairs={{0,2},{1,3},{2,0},{3,1},{4,6},{5,7},{6,4},{7,5},{8,10},{9,11},{10,... | collective-permute-start | bytes 196616 | tf_op jit(solution)/shard_map/ppermute | solution.py:699
  8.6 6.3 %collective-permute-start.2 = (f32[72,128]{1,0:T(8,128)S(1)}, f32[72,128]{1,0:T(8,128)S(1)}, u32[]{:S(2)}, u32[]{:S(2)}) collective-permute-start(f32[72,128]{1,0:T(8,128)S(1)} %depth_payload.1.refs_0_), channel_id=1, source_target_pairs={{0,6},{1,7},{2,4},{3,5},{4,2},{5,3},{6,0},{7,1},{8,14},{9,15},{10,... | collective-permute-start | bytes 110600 | tf_op jit(solution)/shard_map/ppermute | solution.py:699
  11.1 5.3 %collective-permute-start.1 = (f32[72,128]{1,0:T(8,128)S(1)}, f32[72,128]{1,0:T(8,128)S(1)}, u32[]{:S(2)}, u32[]{:S(2)}) collective-permute-start(f32[72,128]{1,0:T(8,128)S(1)} %depth_payload.1.refs_0_), channel_id=1, source_target_pairs={{0,4},{1,5},{2,6},{3,7},{4,0},{5,1},{6,2},{7,3},{8,12},{9,13},{10,... | collective-permute-start | bytes 110600 | tf_op jit(solution)/shard_map/ppermute | solution.py:699
  11.3 5.1 %collective-permute-start = (f32[72,128]{1,0:T(8,128)S(1)}, f32[72,128]{1,0:T(8,128)S(1)}, u32[]{:S(2)}, u32[]{:S(2)}) collective-permute-start(f32[72,128]{1,0:T(8,128)S(1)} %depth_payload.1.refs_0_), channel_id=1, source_target_pairs={{0,2},{1,3},{2,0},{3,1},{4,6},{5,7},{6,4},{7,5},{8,10},{9,11},{10,... | collective-permute-start | bytes 110600 | tf_op jit(solution)/shard_map/ppermute | solution.py:699
  16.4 11.2 %collective-permute-start.6 = (f32[4,72,128]{2,1,0:T(8,128)S(1)}, f32[4,72,128]{2,1,0:T(8,128)S(1)}, u32[]{:S(2)}, u32[]{:S(2)}) collective-permute-start(f32[4,72,128]{2,1,0:T(8,128)S(1)} %stack_after.4.refs_0_), channel_id=1, source_target_pairs={{0,24},{8,16},{16,8},{24,0},{1,25},{9,17},{17,9},{25,1},{2,26},{10... | collective-permute-start | bytes 442376 | tf_op jit(solution)/shard_map/ppermute | solution.py:699
  18.9 8.7 %collective-permute-start.5 = (f32[4,72,128]{2,1,0:T(8,128)S(1)}, f32[4,72,128]{2,1,0:T(8,128)S(1)}, u32[]{:S(2)}, u32[]{:S(2)}) collective-permute-start(f32[4,72,128]{2,1,0:T(8,128)S(1)} %stack_after.4.refs_0_), channel_id=1, source_target_pairs={{0,16},{8,24},{16,0},{24,8},{1,17},{9,25},{17,1},{25,9},{2,18},{10... | collective-permute-start | bytes 442376 | tf_op jit(solution)/shard_map/ppermute | solution.py:699
  19.4 8.2 %collective-permute-start.4 = (f32[4,72,128]{2,1,0:T(8,128)S(1)}, f32[4,72,128]{2,1,0:T(8,128)S(1)}, u32[]{:S(2)}, u32[]{:S(2)}) collective-permute-start(f32[4,72,128]{2,1,0:T(8,128)S(1)} %stack_after.4.refs_0_), channel_id=1, source_target_pairs={{0,8},{8,0},{16,24},{24,16},{1,9},{9,1},{17,25},{25,17},{2,10},{10... | collective-permute-start | bytes 442376 | tf_op jit(solution)/shard_map/ppermute | solution.py:699
  19.9 7.6 %collective-permute-start.8 = (f32[4,32,128]{2,1,0:T(8,128)S(1)}, f32[4,32,128]{2,1,0:T(8,128)S(1)}, u32[]{:S(2)}, u32[]{:S(2)}) collective-permute-start(f32[4,32,128]{2,1,0:T(8,128)S(1)} %column_forcing.1.after_ref.refs_0_), channel_id=1, source_target_pairs={{0,6},{1,7},{2,4},{3,5},{4,2},{5,3},{6,0},{7,1},{8,14},{9,15},{10,... | collective-permute-start | bytes 196616 | tf_op jit(solution)/shard_map/ppermute | solution.py:699
  21.8 5.7 %collective-permute-start.7 = (f32[4,32,128]{2,1,0:T(8,128)S(1)}, f32[4,32,128]{2,1,0:T(8,128)S(1)}, u32[]{:S(2)}, u32[]{:S(2)}) collective-permute-start(f32[4,32,128]{2,1,0:T(8,128)S(1)} %column_forcing.1.after_ref.refs_0_), channel_id=1, source_target_pairs={{0,4},{1,5},{2,6},{3,7},{4,0},{5,1},{6,2},{7,3},{8,12},{9,13},{10,... | collective-permute-start | bytes 196616 | tf_op jit(solution)/shard_map/ppermute | solution.py:699
  27.6 9.8 %collective-permute-start.9 = (f32[16,72,128]{2,1,0:T(8,128)S(1)}, f32[16,72,128]{2,1,0:T(8,128)S(1)}, u32[]{:S(2)}, u32[]{:S(2)}) collective-permute-start(f32[16,72,128]{2,1,0:T(8,128)S(1)} %bitcast.6), channel_id=1, source_target_pairs={{0,1},{1,0},{2,3},{3,2},{4,5},{5,4},{6,7},{7,6},{8,9},{9,8},{10,11... | collective-permute-start | bytes 1769480 | tf_op jit(solution)/shard_map/ppermute | solution.py:699
  27.7 12.5 %collective-permute-start.12 = (f32[4,4,32,128]{3,2,1,0:T(8,128)S(1)}, f32[4,4,32,128]{3,2,1,0:T(8,128)S(1)}, u32[]{:S(2)}, u32[]{:S(2)}) collective-permute-start(f32[4,4,32,128]{3,2,1,0:T(8,128)S(1)} %stack_after.5.refs_4_.after_ref.refs_0_), channel_id=1, source_target_pairs={{0,24},{8,16},{16,8},{24,0},{1,25},{9,17},{17,9},{25,1},{2,26},{10... | collective-permute-start | bytes 786440 | tf_op jit(solution)/shard_map/ppermute | solution.py:699
  30.2 12.7 %collective-permute-start.11 = (f32[4,4,32,128]{3,2,1,0:T(8,128)S(1)}, f32[4,4,32,128]{3,2,1,0:T(8,128)S(1)}, u32[]{:S(2)}, u32[]{:S(2)}) collective-permute-start(f32[4,4,32,128]{3,2,1,0:T(8,128)S(1)} %stack_after.5.refs_4_.after_ref.refs_0_), channel_id=1, source_target_pairs={{0,16},{8,24},{16,0},{24,8},{1,17},{9,25},{17,1},{25,9},{2,18},{10... | collective-permute-start | bytes 786440 | tf_op jit(solution)/shard_map/ppermute | solution.py:699
  30.7 12.3 %collective-permute-start.10 = (f32[4,4,32,128]{3,2,1,0:T(8,128)S(1)}, f32[4,4,32,128]{3,2,1,0:T(8,128)S(1)}, u32[]{:S(2)}, u32[]{:S(2)}) collective-permute-start(f32[4,4,32,128]{3,2,1,0:T(8,128)S(1)} %stack_after.5.refs_4_.after_ref.refs_0_), channel_id=1, source_target_pairs={{0,8},{8,0},{16,24},{24,16},{1,9},{9,1},{17,25},{25,17},{2,10},{10... | collective-permute-start | bytes 786440 | tf_op jit(solution)/shard_map/ppermute | solution.py:699
  31.4 14.5 %copy-start.3 = (f32[32]{0:T(128)S(1)}, f32[32]{0:T(128)}, u32[]{:S(2)}) copy-start(f32[32]{0:T(128)} %constant.10.clone.coefs_ref) | copy-start | bytes 388
  43.1 2.7 %collective-permute-start.13 = (f32[4,4,4,32,128]{4,3,2,1,0:T(8,128)S(1)}, f32[4,4,4,32,128]{4,3,2,1,0:T(8,128)S(1)}, u32[]{:S(2)}, u32[]{:S(2)}) collective-permute-start(f32[4,4,4,32,128]{4,3,2,1,0:T(8,128)S(1)} %stack_after.7), channel_id=1, source_target_pairs={{0,1},{1,0},{2,3},{3,2},{4,5},{5,4},{6,7},{7,6},{8,9},{9,8},{10,11... | collective-permute-start | bytes 3145736 | tf_op jit(solution)/shard_map/ppermute | solution.py:699

commit v3 on v2

--- a/solution.py
+++ b/solution.py
@@ -114,20 +114,16 @@
 CHUNK = 8
 
 
-def mixing_kernel(block_total, first, earlier, ids_ref, levels_ref, drag_ref, adjoint_ref,
-                  velocity_ref, after_ref, *rest):
-    if earlier:
-        for target, ref in zip(rest[3:5], rest[:2]):
-            target[0:first] = ref[...]
-        rest = rest[2:]
-    column_ref, bottom_ref, gradient_ref, adjoint, velocity, column, in_sems, out_sems = rest
+def mixing_kernel(block_total, ids_ref, levels_ref, drag_ref, adjoint_ref, velocity_ref, after_ref,
+                  column_ref, bottom_ref, gradient_ref, adjoint, velocity, column,
+                  in_sems, out_sems):
     slots, comps, depth, rows, cols = adjoint.shape
     group = 16
     parts = rows // group
 
     def copies_in(b):
         return [
-            pltpu.make_async_copy(source.at[first + b, c], target.at[b, c], in_sems.at[n, b, c])
+            pltpu.make_async_copy(source.at[b, c], target.at[b, c], in_sems.at[n, b, c])
             for n, (source, target) in enumerate(
                 ((adjoint_ref, adjoint), (velocity_ref, velocity))
             )
@@ -146,7 +142,9 @@
 
     def one_component(b, c, span, levels):
         zero = jnp.zeros(levels.shape, jnp.float32)
-        x = once = first_flux = second_flux = flow = field = rate_before = zero
+        x = once = first_flux = second_flux = flow = field = zero
+        wets = []
+        rates = []
 
         def store(batch):
             for k, value in batch:
@@ -158,14 +156,14 @@
             for k in range(low, min(low + CHUNK, depth + 2)):
                 fresh_once = None
                 if k < depth:
-                    wet = levels > k
-                    rate = jnp.where(wet, mix_rate, 0.0)
-                    fresh = jnp.where(wet, adjoint[b, c, k, span, :], 0.0)
+                    wets.append(levels > k)
+                    rates.append(jnp.where(wets[k], mix_rate, 0.0))
+                    fresh = adjoint[b, c, k, span, :]
                     flow = jnp.where(
-                        levels == k + 1, velocity[b, c, k, span, :].astype(jnp.float32), flow
+                        wets[k], velocity[b, c, k, span, :].astype(jnp.float32), flow
                     )
                     if 1 <= k:
-                        flux = (fresh - x) * rate
+                        flux = (fresh - x) * rates[k]
                         fresh_once = x + (flux - first_flux)
                         first_flux = flux
                     x = fresh
@@ -173,35 +171,34 @@
                     fresh_once = x - first_flux
                 if 2 <= k:
                     if k <= depth:
-                        flux = (fresh_once - once) * rate_before
+                        flux = (fresh_once - once) * rates[k - 1]
                         twice = once + (flux - second_flux)
                         second_flux = flux
                     else:
                         twice = once - second_flux
                     batch.append((k - 2, twice))
-                    field = jnp.where(levels == k - 1, twice, field)
+                    field = jnp.where(wets[k - 2], twice, field)
                 if fresh_once is not None:
                     once = fresh_once
-                rate_before = rate
             store(late)
             late = batch
         store(late)
         return flow, field
 
     def one_group(b, index):
-        flag = jnp.where(ids_ref[first + b] < block_total, 1.0, 0.0)
+        flag = jnp.where(ids_ref[b] < block_total, 1.0, 0.0)
         span = pl.ds(pl.multiple_of(index * group, group), group)
-        levels = levels_ref[first + b, span, :]
+        levels = levels_ref[b, span, :]
         flow, field = zip(*[one_component(b, c, span, levels) for c in range(2)])
         speed = jnp.sqrt(flow[0] * flow[0] + flow[1] * flow[1] + speed_floor)
         along = flow[0] * field[0] + flow[1] * field[1]
         ratio = along / speed
-        drag = drag_ref[first + b, span, :]
+        drag = drag_ref[b, span, :]
         for c in range(2):
-            bottom_ref[first + b, c, span, :] = field[c] - drag_step * drag * (
+            bottom_ref[b, c, span, :] = field[c] - drag_step * drag * (
                 speed * field[c] + flow[c] * ratio
             )
-        gradient_ref[first + b, span, :] = -drag_step * speed * along * flag
+        gradient_ref[b, span, :] = -drag_step * speed * along * flag
 
     def one(step, carry):
         b = lax.div(step, parts)
@@ -222,25 +219,22 @@
             copy_out(b, index).wait()
 
 
-def column_mixing(adjoint_vel, velocity, drag_coef, level_count, block_ids, after, block_total,
-                  first, last, earlier=()):
-    comps, depth, rows, cols = adjoint_vel.shape[1:]
-    slots = last - first
-    part = (slots, comps, depth, rows, cols)
-    size = slots * comps * depth * rows * cols
+def column_mixing(adjoint_vel, velocity, drag_coef, level_count, block_ids, after, block_total):
+    slots, comps, depth, rows, cols = adjoint_vel.shape
+    size = adjoint_vel.size
     return pl.pallas_call(
-        functools.partial(mixing_kernel, block_total, first, len(earlier)),
-        in_specs=[SMEM, VMEM, VMEM, HBM, HBM, ANYWHERE] + [VMEM] * len(earlier),
+        functools.partial(mixing_kernel, block_total),
+        in_specs=[SMEM, VMEM, VMEM, HBM, HBM, ANYWHERE],
         out_specs=[HBM, VMEM, VMEM],
         out_shape=[
-            pltpu.HBM(part, jnp.float32),
-            pltpu.VMEM((last, comps, rows, cols), jnp.float32),
-            (pltpu.HBM if last == level_count.shape[0] else pltpu.VMEM)((last, rows, cols), jnp.float32),
+            pltpu.HBM(adjoint_vel.shape, jnp.float32),
+            pltpu.VMEM((slots, comps, rows, cols), jnp.float32),
+            pltpu.HBM((slots, rows, cols), jnp.float32),
         ],
         scratch_shapes=[
-            pltpu.VMEM(part, adjoint_vel.dtype),
-            pltpu.VMEM(part, velocity.dtype),
-            pltpu.VMEM(part, jnp.float32),
+            pltpu.VMEM(adjoint_vel.shape, adjoint_vel.dtype),
+            pltpu.VMEM(velocity.shape, velocity.dtype),
+            pltpu.VMEM(adjoint_vel.shape, jnp.float32),
             pltpu.SemaphoreType.DMA((2, slots, comps)),
             pltpu.SemaphoreType.DMA((slots, rows // 16)),
         ],
@@ -249,7 +243,7 @@
             flops=14 * size, bytes_accessed=10 * size, transcendentals=0
         ),
         name="column_mixing",
-    )(block_ids, level_count, drag_coef, adjoint_vel, velocity, after, *earlier)
+    )(block_ids, level_count, drag_coef, adjoint_vel, velocity, after)
 
 
 PAD = SUBLANES
@@ -473,18 +467,14 @@
 
 
 def solve_kernel(block_total, ids_ref, table_ref, coefs_ref, root_ref, centre_ref, around_ref,
-                 levels_ref, bottom_ref, first_column_ref, last_column_ref, near_ref, far_ref,
+                 levels_ref, bottom_ref, column_ref, near_ref, far_ref,
                  corrected_ref, height_ref, sensitivity_ref,
                  natural, source, even, odd, extra, column, in_sems, out_sems):
     slots, comps, depth, rows, cols = column.shape
     strips, deep, tall = window_shape(slots, rows)
 
-    middle = first_column_ref.shape[0]
     copies_in = [
-        pltpu.make_async_copy(first_column_ref, column.at[pl.ds(0, middle)], in_sems.at[0]),
-        pltpu.make_async_copy(
-            last_column_ref, column.at[pl.ds(middle, slots - middle)], in_sems.at[1]
-        ),
+        pltpu.make_async_copy(column_ref.at[b], column.at[b], in_sems.at[b]) for b in range(slots)
     ]
     for copy in copies_in:
         copy.start()
@@ -641,21 +631,19 @@
             copy_out(b, c).wait()
 
 
-def surface_solve(near, far, weights, block_ids, level_count, bottom, columns, block_total):
+def surface_solve(near, far, weights, block_ids, level_count, bottom, column, block_total):
     root, centre, around, table = weights
-    comps, depth, rows, cols = columns[0].shape[1:]
-    slots = level_count.shape[0]
+    slots, comps, depth, rows, cols = column.shape
     assert comps == 2
-    full = (slots, comps, depth, rows, cols)
     deep = window_shape(slots, rows)[1]
     turned = pltpu.VMEM(root.shape, jnp.float32)
     coefs = jnp.array(chebyshev_sum(STEPS)[0][::-1], jnp.float32)
     return pl.pallas_call(
         functools.partial(solve_kernel, block_total),
-        in_specs=[SMEM, SMEM, SMEM] + [VMEM] * 5 + [HBM] * 2 + [VMEM] * 2,
+        in_specs=[SMEM, SMEM, SMEM] + [VMEM] * 5 + [HBM] + [VMEM] * 2,
         out_specs=[HBM, VMEM, VMEM],
         out_shape=[
-            jax.ShapeDtypeStruct(full, jnp.float32),
+            jax.ShapeDtypeStruct(column.shape, jnp.float32),
             jax.ShapeDtypeStruct((rows, 2 * cols), jnp.float32),
             jax.ShapeDtypeStruct((rows, 2 * cols), jnp.float32),
         ],
@@ -665,8 +653,8 @@
             turned,
             turned,
             turned,
-            pltpu.VMEM(full, jnp.float32),
-            pltpu.SemaphoreType.DMA((2,)),
+            pltpu.VMEM(column.shape, jnp.float32),
+            pltpu.SemaphoreType.DMA((slots,)),
             pltpu.SemaphoreType.DMA((slots, comps)),
         ],
         compiler_params=params(SOLVE_VMEM),
@@ -674,7 +662,7 @@
             flops=9 * STEPS * root.size, bytes_accessed=16 * root.size, transcendentals=0
         ),
         name="surface_solve",
-    )(block_ids, table, coefs, root, centre, around, level_count, bottom, *columns, near, far)
+    )(block_ids, table, coefs, root, centre, around, level_count, bottom, column, near, far)
 
 
 def stack_kernel(parts, *refs):
@@ -713,19 +701,16 @@
     forcing = column_forcing(adjoint_vel, level_count)
 
     parts = [forcing] + [swap(forcing, "gy", 2 * m) for m in range(1, half)]
-    near_depths = stack_after(depth_parts, parts[1])
+    near_depths = stack_after(depth_parts, forcing)
     near_depths = [near_depths] + [swap(near_depths, "gx", m) for m in range(1, lon_count)]
-    columns = (adjoint_vel, velocity, drag_coef, level_count, block_ids)
-    middle = (slots + 1) // 2
-    first_column, *first_rest = column_mixing(*columns, forcing, block_total, 0, middle)
-    line = stack_after(parts, first_rest[0])
+    line = stack_after(parts)
 
     near = [line] + [swap(line, "gx", m) for m in range(1, lon_count)]
     near_depths = stack_after(near_depths, line)
     near_depths = near_depths.reshape((lon_count * half,) + depths.shape)
     far_depths = swap(near_depths, "gy", 1)
-    last_column, bottom, drag_gradient = column_mixing(
-        *columns, line, block_total, middle, slots, first_rest
+    column, bottom, drag_gradient = column_mixing(
+        adjoint_vel, velocity, drag_coef, level_count, block_ids, line, block_total
     )
     weights = surface_weights(
         near_depths, far_depths, me, block_ids, rows, lon_count, lat_count
@@ -736,7 +721,7 @@
 
     corrected, height, sensitivity = surface_solve(
         near.reshape((-1, rows, cols)), far.reshape((-1, rows, cols)), weights,
-        block_ids, level_count, bottom, (first_column, last_column), block_total,
+        block_ids, level_count, bottom, column, block_total,
     )
     return corrected, drag_gradient, height, sensitivity
 

time: 58.5 us -> 56.8 us (0.971)
  Pallas kernels: 31.7 us -> 29.2 us
  waiting for transfers between devices: 8.81 us -> 10.1 us
    pallas_call x2 -> x1, Pallas kernels: 11.6 us -> 9.18 us  [column_mixing(): pl.pallas_call(functools.partial(mixing_kernel, block_total), in_specs=[S...]
    ppermute x14, waiting for transfers between devices: 8.81 us -> 10.1 us  [swap(): return lax.ppermute(values, axis, [(i, i ^ mask) for i in range(count)])]
  transfers between devices with their start and end apart: 14 -> 14, of which waited for: 5 -> 5; matrix products, arithmetic and copies ran while one was open for 0% -> 0% of each run, Pallas kernels for 26% -> 28%
where the time goes in v3:
time: 56.8 us; the launch traced here: 56.6 us
  Pallas kernels  29.2 us (51%)
  starting transfers between devices  16.4 us (29%)
  waiting for transfers between devices  10.1 us (18%)
  between operations  0.81 us (1%)
    ppermute x14, starting transfers between devices, swap(): return lax.ppermute(values, axis, [(i, i ^ mask) for i in range(count)])  16.4 us
    pallas_call x1, Pallas kernels, surface_solve(): pl.pallas_call(functools.partial(solve_kernel, block_total), in_specs=[SM...  12.4 us
    ppermute x14, waiting for transfers between devices, swap(): return lax.ppermute(values, axis, [(i, i ^ mask) for i in range(count)])  10.1 us
    pallas_call x1, Pallas kernels, column_mixing(): pl.pallas_call(functools.partial(mixing_kernel, block_total), in_specs=[S...  9.18 us
    pallas_call x1, Pallas kernels, column_forcing(): pl.pallas_call(forcing_kernel, in_specs=[HBM, HBM], out_specs=VMEM, out_s...  3.86 us
    pallas_call x1, Pallas kernels, surface_weights(): pl.pallas_call(functools.partial(weights_kernel, slots, lon_count, lat_co...  2.74 us
  transfers between devices with their start and end apart: 14, of which 5 were waited for; matrix products, arithmetic and copies ran while one was open for 0% of the time, Pallas kernels for 28%

profile of v3, /device:TPU:0, one launch (start us, length us, event | category | flops | bytes accessed | tf_op | source)
XLA Modules:
  0.0 56.6 jit_solution(3325337442210375800)
XLA Ops:
  0.6 0.0 copy-start.2
  0.6 0.0 copy-start
  0.7 0.0 copy-start.1
  0.7 0.8 %depth_payload.1.refs_0_ = f32[72,128]{1,0:T(8,128)S(1)} custom-call(s32[4]{0:T(128)} %ids_ref.7, f32[32,256]{1,0:T(8,128)} %bathymetry_ref.1, s32[32,256]{1,0:T(8,128)} %mask_ref.1), custom_call_target="tpu_custom_call" | custom-call | tf_op jit(solution)/shard_map/depth_payload/pallas_call | solution.py:344
  1.5 5.1 %collective-permute-start.2 = (f32[72,128]{1,0:T(8,128)S(1)}, f32[72,128]{1,0:T(8,128)S(1)}, u32[]{:S(2)}, u32[]{:S(2)}) collective-permute-start(f32[72,128]{1,0:T(8,128)S(1)} %depth_payload.1.refs_0_), channel_id=1, source_target_pairs={{0,6},{1,7},{2,4},{3,5},{4,2},{5,3},{6,0},{7,1},{8,14},{9,15},{10,... | collective-permute-start | bytes 110600 | tf_op jit(solution)/shard_map/ppermute | solution.py:687
  6.6 0.0 collective-permute-start.1
  6.6 0.6 %collective-permute-start = (f32[72,128]{1,0:T(8,128)S(1)}, f32[72,128]{1,0:T(8,128)S(1)}, u32[]{:S(2)}, u32[]{:S(2)}) collective-permute-start(f32[72,128]{1,0:T(8,128)S(1)} %depth_payload.1.refs_0_), channel_id=1, source_target_pairs={{0,2},{1,3},{2,0},{3,1},{4,6},{5,7},{6,4},{7,5},{8,10},{9,11},{10,... | collective-permute-start | bytes 110600 | tf_op jit(solution)/shard_map/ppermute | solution.py:687
  7.3 3.9 %column_forcing.1.refs_4_.refs_0_ = f32[4,32,128]{2,1,0:T(8,128)S(1)} custom-call(s32[4,32,128]{2,1,0:T(8,128)} %levels_ref.5, f32[4,2,62,32,128]{4,3,2,1,0:T(8,128)} %adjoint_ref.3), custom_call_target="tpu_custom_call" | custom-call | flops 4063232 | bytes 8126464 | tf_op jit(solution)/shard_map/column_forcing/pallas_call | solution.py:95
  11.1 0.0 collective-permute-done.2.refs_3_
  11.2 0.3 collective-permute-done.1.refs_2_
  11.5 0.0 collective-permute-done.refs_1_
  11.5 2.5 %collective-permute-start.5 = (f32[4,72,128]{2,1,0:T(8,128)S(1)}, f32[4,72,128]{2,1,0:T(8,128)S(1)}, u32[]{:S(2)}, u32[]{:S(2)}) collective-permute-start(f32[4,72,128]{2,1,0:T(8,128)S(1)} %stack_after.4.refs_0_), channel_id=1, source_target_pairs={{0,24},{8,16},{16,8},{24,0},{1,25},{9,17},{17,9},{25,1},{2,26},{10... | collective-permute-start | bytes 442376 | tf_op jit(solution)/shard_map/ppermute | solution.py:687
  14.0 0.5 collective-permute-start.4
  14.5 0.5 collective-permute-start.3
  15.1 3.4 %collective-permute-start.8 = (f32[4,32,128]{2,1,0:T(8,128)S(1)}, f32[4,32,128]{2,1,0:T(8,128)S(1)}, u32[]{:S(2)}, u32[]{:S(2)}) collective-permute-start(f32[4,32,128]{2,1,0:T(8,128)S(1)} %column_forcing.1.refs_4_.refs_0_), channel_id=1, source_target_pairs={{0,6},{1,7},{2,4},{3,5},{4,2},{5,3},{6,0},{7,1},{8,14},{9,15},{10,... | collective-permute-start | bytes 196616 | tf_op jit(solution)/shard_map/ppermute | solution.py:687
  18.5 0.0 collective-permute-start.7
  18.5 2.8 %collective-permute-done.8.refs_3_ = f32[4,32,128]{2,1,0:T(8,128)S(1)} collective-permute-done((f32[4,32,128]{2,1,0:T(8,128)S(1)}, f32[4,32,128]{2,1,0:T(8,128)S(1)}, u32[]{:S(2)}, u32[]{:S(2)}) %collective-permute-start.8) | collective-permute-done | bytes 65568 | tf_op jit(solution)/shard_map/ppermute | solution.py:687
  21.3 0.0 collective-permute-start.6
  21.3 2.4 %collective-permute-done.7.refs_2_ = f32[4,32,128]{2,1,0:T(8,128)S(1)} collective-permute-done((f32[4,32,128]{2,1,0:T(8,128)S(1)}, f32[4,32,128]{2,1,0:T(8,128)S(1)}, u32[]{:S(2)}, u32[]{:S(2)}) %collective-permute-start.7) | collective-permute-done | bytes 65568 | tf_op jit(solution)/shard_map/ppermute | solution.py:687
  23.7 1.9 %collective-permute-done.6.refs_1_ = f32[4,32,128]{2,1,0:T(8,128)S(1)} collective-permute-done((f32[4,32,128]{2,1,0:T(8,128)S(1)}, f32[4,32,128]{2,1,0:T(8,128)S(1)}, u32[]{:S(2)}, u32[]{:S(2)}) %collective-permute-start.6) | collective-permute-done | bytes 65568 | tf_op jit(solution)/shard_map/ppermute | solution.py:687
  25.6 0.0 collective-permute-done.5.refs_3_
  25.6 0.0 collective-permute-done.4.refs_2_
  25.6 0.0 collective-permute-done.3.refs_1_
  25.7 0.1 collective-permute-start.9
  25.7 2.5 %collective-permute-start.12 = (f32[4,4,32,128]{3,2,1,0:T(8,128)S(1)}, f32[4,4,32,128]{3,2,1,0:T(8,128)S(1)}, u32[]{:S(2)}, u32[]{:S(2)}) collective-permute-start(f32[4,4,32,128]{3,2,1,0:T(8,128)S(1)} %stack_after.5.refs_4_.after_ref.refs_0_), channel_id=1, source_target_pairs={{0,24},{8,16},{16,8},{24,0},{1,25},{9,17},{17,9},{25,1},{2,26},{10... | collective-permute-start | bytes 786440 | tf_op jit(solution)/shard_map/ppermute | solution.py:687
  28.2 0.5 collective-permute-start.11
  28.7 0.5 collective-permute-start.10
  29.3 0.1 pad_add_fusion.me_ref
  29.4 0.0 copy-done.2
  29.4 0.0 copy-done
  29.4 0.0 copy-done.1
  29.4 0.0 copy-start.3
  29.4 9.2 %column_mixing.1 = (f32[4,2,62,32,128]{4,3,2,1,0:T(8,128)}, f32[4,2,32,128]{3,2,1,0:T(8,128)S(1)}, f32[4,32,128]{2,1,0:T(8,128)}) custom-call(s32[4]{0:T(128)S(1)} %copy-done.2, s32[4,32,128]{2,1,0:T(8,128)S(1)} %copy-done, f32[4,32,128]{2,1,0:T(8,128)S(1)} %copy-done.1, f32[4,2,62,32,128]{4,3,2,1,0:T(8,128)} %adjoint_ref.3, ...), custom_call_target="tpu_custom_call" | custom-call | flops 28442624 | bytes 20316160 | tf_op jit(solution)/shard_map/column_mixing/pallas_call | solution.py:225
  38.6 0.0 collective-permute-done.9.far_ref
  38.6 2.7 %surface_weights.1 = (f32[1040,128]{1,0:T(8,128)S(1)}, f32[1040,128]{1,0:T(8,128)S(1)}, f32[1040,128]{1,0:T(8,128)S(1)}, s32[54]{0:T(128)S(1)}) custom-call(s32[2]{0:T(128)S(1)} %pad_add_fusion.me_ref, s32[4]{0:T(128)S(1)} %copy-done.2, f32[16,72,128]{2,1,0:T(8,128)S(1)} %bitcast.7, f32[16,72,128]{2,1,0:T(8,128)S(1)} %collective-permute-done.9.far_ref), custom_call_target="tpu_custom_call" | custom-call | bytes 8388608 | tf_op jit(solution)/shard_map/surface_weights/pallas_call | solution.py:445
  41.3 0.0 collective-permute-done.12.refs_3_
  41.3 0.0 collective-permute-done.11.refs_2_
  41.4 0.0 collective-permute-done.10.refs_1_
  41.4 0.1 stack_after.7
  41.4 0.1 collective-permute-start.13
  41.5 2.6 %collective-permute-done.13 = f32[4,4,4,32,128]{4,3,2,1,0:T(8,128)S(1)} collective-permute-done((f32[4,4,4,32,128]{4,3,2,1,0:T(8,128)S(1)}, f32[4,4,4,32,128]{4,3,2,1,0:T(8,128)S(1)}, u32[]{:S(2)}, u32[]{:S(2)}) %collective-permute-start.13) | collective-permute-done | bytes 1048608 | tf_op jit(solution)/shard_map/ppermute | solution.py:687
  44.2 0.0 copy-done.3
  44.2 12.4 %surface_solve.1 = (f32[4,2,62,32,128]{4,3,2,1,0:T(8,128)}, f32[32,256]{1,0:T(8,128)}, f32[32,256]{1,0:T(8,128)}) custom-call(s32[4]{0:T(128)S(1)} %copy-done.2, s32[54]{0:T(128)S(1)} %get-tuple-element.14.table_ref, f32[32]{0:T(128)S(1)} %copy-done.3, f32[1040,128]{1,0:T(8,128)S(1)} %get-tuple-element.15.refs_5_.root_ref, ...), custom_call_target="tpu_custom_call" | custom-call | flops 38338560 | bytes 2129920 | tf_op jit(solution)/shard_map/surface_solve/pallas_call | solution.py:641
  (3 shorter events, 0.1 us)
Async XLA Ops:
  0.6 28.7 %copy-start.2 = (s32[4]{0:T(128)S(1)}, s32[4]{0:T(128)}, u32[]{:S(2)}) copy-start(s32[4]{0:T(128)} %ids_ref.7) | copy-start | bytes 52
  0.6 28.7 %copy-start = (s32[4,32,128]{2,1,0:T(8,128)S(1)}, s32[4,32,128]{2,1,0:T(8,128)}, u32[]{:S(2)}) copy-start(s32[4,32,128]{2,1,0:T(8,128)} %levels_ref.5) | copy-start | bytes 196612
  0.7 28.7 %copy-start.1 = (f32[4,32,128]{2,1,0:T(8,128)S(1)}, f32[4,32,128]{2,1,0:T(8,128)}, u32[]{:S(2)}) copy-start(f32[4,32,128]{2,1,0:T(8,128)} %drag_ref.1) | copy-start | bytes 196612
  1.5 9.6 %collective-permute-start.2 = (f32[72,128]{1,0:T(8,128)S(1)}, f32[72,128]{1,0:T(8,128)S(1)}, u32[]{:S(2)}, u32[]{:S(2)}) collective-permute-start(f32[72,128]{1,0:T(8,128)S(1)} %depth_payload.1.refs_0_), channel_id=1, source_target_pairs={{0,6},{1,7},{2,4},{3,5},{4,2},{5,3},{6,0},{7,1},{8,14},{9,15},{10,... | collective-permute-start | bytes 110600 | tf_op jit(solution)/shard_map/ppermute | solution.py:687
  6.6 4.9 %collective-permute-start.1 = (f32[72,128]{1,0:T(8,128)S(1)}, f32[72,128]{1,0:T(8,128)S(1)}, u32[]{:S(2)}, u32[]{:S(2)}) collective-permute-start(f32[72,128]{1,0:T(8,128)S(1)} %depth_payload.1.refs_0_), channel_id=1, source_target_pairs={{0,4},{1,5},{2,6},{3,7},{4,0},{5,1},{6,2},{7,3},{8,12},{9,13},{10,... | collective-permute-start | bytes 110600 | tf_op jit(solution)/shard_map/ppermute | solution.py:687
  6.6 4.9 %collective-permute-start = (f32[72,128]{1,0:T(8,128)S(1)}, f32[72,128]{1,0:T(8,128)S(1)}, u32[]{:S(2)}, u32[]{:S(2)}) collective-permute-start(f32[72,128]{1,0:T(8,128)S(1)} %depth_payload.1.refs_0_), channel_id=1, source_target_pairs={{0,2},{1,3},{2,0},{3,1},{4,6},{5,7},{6,4},{7,5},{8,10},{9,11},{10,... | collective-permute-start | bytes 110600 | tf_op jit(solution)/shard_map/ppermute | solution.py:687
  11.5 14.1 %collective-permute-start.5 = (f32[4,72,128]{2,1,0:T(8,128)S(1)}, f32[4,72,128]{2,1,0:T(8,128)S(1)}, u32[]{:S(2)}, u32[]{:S(2)}) collective-permute-start(f32[4,72,128]{2,1,0:T(8,128)S(1)} %stack_after.4.refs_0_), channel_id=1, source_target_pairs={{0,24},{8,16},{16,8},{24,0},{1,25},{9,17},{17,9},{25,1},{2,26},{10... | collective-permute-start | bytes 442376 | tf_op jit(solution)/shard_map/ppermute | solution.py:687
  14.0 11.6 %collective-permute-start.4 = (f32[4,72,128]{2,1,0:T(8,128)S(1)}, f32[4,72,128]{2,1,0:T(8,128)S(1)}, u32[]{:S(2)}, u32[]{:S(2)}) collective-permute-start(f32[4,72,128]{2,1,0:T(8,128)S(1)} %stack_after.4.refs_0_), channel_id=1, source_target_pairs={{0,16},{8,24},{16,0},{24,8},{1,17},{9,25},{17,1},{25,9},{2,18},{10... | collective-permute-start | bytes 442376 | tf_op jit(solution)/shard_map/ppermute | solution.py:687
  14.5 11.1 %collective-permute-start.3 = (f32[4,72,128]{2,1,0:T(8,128)S(1)}, f32[4,72,128]{2,1,0:T(8,128)S(1)}, u32[]{:S(2)}, u32[]{:S(2)}) collective-permute-start(f32[4,72,128]{2,1,0:T(8,128)S(1)} %stack_after.4.refs_0_), channel_id=1, source_target_pairs={{0,8},{8,0},{16,24},{24,16},{1,9},{9,1},{17,25},{25,17},{2,10},{10... | collective-permute-start | bytes 442376 | tf_op jit(solution)/shard_map/ppermute | solution.py:687
  15.1 6.2 %collective-permute-start.8 = (f32[4,32,128]{2,1,0:T(8,128)S(1)}, f32[4,32,128]{2,1,0:T(8,128)S(1)}, u32[]{:S(2)}, u32[]{:S(2)}) collective-permute-start(f32[4,32,128]{2,1,0:T(8,128)S(1)} %column_forcing.1.refs_4_.refs_0_), channel_id=1, source_target_pairs={{0,6},{1,7},{2,4},{3,5},{4,2},{5,3},{6,0},{7,1},{8,14},{9,15},{10,... | collective-permute-start | bytes 196616 | tf_op jit(solution)/shard_map/ppermute | solution.py:687
  18.5 5.2 %collective-permute-start.7 = (f32[4,32,128]{2,1,0:T(8,128)S(1)}, f32[4,32,128]{2,1,0:T(8,128)S(1)}, u32[]{:S(2)}, u32[]{:S(2)}) collective-permute-start(f32[4,32,128]{2,1,0:T(8,128)S(1)} %column_forcing.1.refs_4_.refs_0_), channel_id=1, source_target_pairs={{0,4},{1,5},{2,6},{3,7},{4,0},{5,1},{6,2},{7,3},{8,12},{9,13},{10,... | collective-permute-start | bytes 196616 | tf_op jit(solution)/shard_map/ppermute | solution.py:687
  21.3 4.3 %collective-permute-start.6 = (f32[4,32,128]{2,1,0:T(8,128)S(1)}, f32[4,32,128]{2,1,0:T(8,128)S(1)}, u32[]{:S(2)}, u32[]{:S(2)}) collective-permute-start(f32[4,32,128]{2,1,0:T(8,128)S(1)} %column_forcing.1.refs_4_.refs_0_), channel_id=1, source_target_pairs={{0,2},{1,3},{2,0},{3,1},{4,6},{5,7},{6,4},{7,5},{8,10},{9,11},{10,... | collective-permute-start | bytes 196616 | tf_op jit(solution)/shard_map/ppermute | solution.py:687
  25.7 12.9 %collective-permute-start.9 = (f32[16,72,128]{2,1,0:T(8,128)S(1)}, f32[16,72,128]{2,1,0:T(8,128)S(1)}, u32[]{:S(2)}, u32[]{:S(2)}) collective-permute-start(f32[16,72,128]{2,1,0:T(8,128)S(1)} %bitcast.6), channel_id=1, source_target_pairs={{0,1},{1,0},{2,3},{3,2},{4,5},{5,4},{6,7},{7,6},{8,9},{9,8},{10,11... | collective-permute-start | bytes 1769480 | tf_op jit(solution)/shard_map/ppermute | solution.py:687
  25.7 15.6 %collective-permute-start.12 = (f32[4,4,32,128]{3,2,1,0:T(8,128)S(1)}, f32[4,4,32,128]{3,2,1,0:T(8,128)S(1)}, u32[]{:S(2)}, u32[]{:S(2)}) collective-permute-start(f32[4,4,32,128]{3,2,1,0:T(8,128)S(1)} %stack_after.5.refs_4_.after_ref.refs_0_), channel_id=1, source_target_pairs={{0,24},{8,16},{16,8},{24,0},{1,25},{9,17},{17,9},{25,1},{2,26},{10... | collective-permute-start | bytes 786440 | tf_op jit(solution)/shard_map/ppermute | solution.py:687
  28.2 13.1 %collective-permute-start.11 = (f32[4,4,32,128]{3,2,1,0:T(8,128)S(1)}, f32[4,4,32,128]{3,2,1,0:T(8,128)S(1)}, u32[]{:S(2)}, u32[]{:S(2)}) collective-permute-start(f32[4,4,32,128]{3,2,1,0:T(8,128)S(1)} %stack_after.5.refs_4_.after_ref.refs_0_), channel_id=1, source_target_pairs={{0,16},{8,24},{16,0},{24,8},{1,17},{9,25},{17,1},{25,9},{2,18},{10... | collective-permute-start | bytes 786440 | tf_op jit(solution)/shard_map/ppermute | solution.py:687
  28.7 12.6 %collective-permute-start.10 = (f32[4,4,32,128]{3,2,1,0:T(8,128)S(1)}, f32[4,4,32,128]{3,2,1,0:T(8,128)S(1)}, u32[]{:S(2)}, u32[]{:S(2)}) collective-permute-start(f32[4,4,32,128]{3,2,1,0:T(8,128)S(1)} %stack_after.5.refs_4_.after_ref.refs_0_), channel_id=1, source_target_pairs={{0,8},{8,0},{16,24},{24,16},{1,9},{9,1},{17,25},{25,17},{2,10},{10... | collective-permute-start | bytes 786440 | tf_op jit(solution)/shard_map/ppermute | solution.py:687
  29.4 14.8 %copy-start.3 = (f32[32]{0:T(128)S(1)}, f32[32]{0:T(128)}, u32[]{:S(2)}) copy-start(f32[32]{0:T(128)} %constant.10.clone.coefs_ref) | copy-start | bytes 388
  41.4 2.7 %collective-permute-start.13 = (f32[4,4,4,32,128]{4,3,2,1,0:T(8,128)S(1)}, f32[4,4,4,32,128]{4,3,2,1,0:T(8,128)S(1)}, u32[]{:S(2)}, u32[]{:S(2)}) collective-permute-start(f32[4,4,4,32,128]{4,3,2,1,0:T(8,128)S(1)} %stack_after.7), channel_id=1, source_target_pairs={{0,1},{1,0},{2,3},{3,2},{4,5},{5,4},{6,7},{7,6},{8,9},{9,8},{10,11... | collective-permute-start | bytes 3145736 | tf_op jit(solution)/shard_map/ppermute | solution.py:687

commit v4 on v2

--- a/solution.py
+++ b/solution.py
@@ -144,55 +144,58 @@
         for copy in copies_in(b):
             copy.start()
 
-    def one_component(b, c, span, levels):
-        zero = jnp.zeros(levels.shape, jnp.float32)
-        x = once = first_flux = second_flux = flow = field = rate_before = zero
-
-        def store(batch):
-            for k, value in batch:
-                column[b, c, k, span, :] = value
-
-        late = []
-        for low in range(0, depth + 2, CHUNK):
-            batch = []
-            for k in range(low, min(low + CHUNK, depth + 2)):
-                fresh_once = None
-                if k < depth:
-                    wet = levels > k
-                    rate = jnp.where(wet, mix_rate, 0.0)
-                    fresh = jnp.where(wet, adjoint[b, c, k, span, :], 0.0)
-                    flow = jnp.where(
-                        levels == k + 1, velocity[b, c, k, span, :].astype(jnp.float32), flow
-                    )
-                    if 1 <= k:
-                        flux = (fresh - x) * rate
-                        fresh_once = x + (flux - first_flux)
-                        first_flux = flux
-                    x = fresh
-                elif k == depth:
-                    fresh_once = x - first_flux
-                if 2 <= k:
-                    if k <= depth:
-                        flux = (fresh_once - once) * rate_before
-                        twice = once + (flux - second_flux)
-                        second_flux = flux
-                    else:
-                        twice = once - second_flux
-                    batch.append((k - 2, twice))
-                    field = jnp.where(levels == k - 1, twice, field)
-                if fresh_once is not None:
-                    once = fresh_once
-                rate_before = rate
-            store(late)
-            late = batch
-        store(late)
-        return flow, field
-
     def one_group(b, index):
         flag = jnp.where(ids_ref[first + b] < block_total, 1.0, 0.0)
         span = pl.ds(pl.multiple_of(index * group, group), group)
         levels = levels_ref[first + b, span, :]
-        flow, field = zip(*[one_component(b, c, span, levels) for c in range(2)])
+        zero = jnp.zeros(levels.shape, jnp.float32)
+        x = [zero, zero]
+        once = [zero, zero]
+        first_flux = [zero, zero]
+        second_flux = [zero, zero]
+        flow = [zero, zero]
+        field = [zero, zero]
+        wets = []
+        rates = []
+        for low in range(0, depth + 2, CHUNK):
+            here = range(low, min(low + CHUNK, depth + 2))
+            loaded = {}
+            for k in here:
+                if k < depth:
+                    for c in range(2):
+                        loaded[k, c] = (adjoint[b, c, k, span, :], velocity[b, c, k, span, :])
+            done = []
+            for k in here:
+                if k < depth:
+                    wets.append(levels > k)
+                    rates.append(jnp.where(wets[k], mix_rate, 0.0))
+                for c in range(2):
+                    fresh_once = None
+                    if k < depth:
+                        fresh = loaded[k, c][0]
+                        flow[c] = jnp.where(
+                            wets[k], loaded[k, c][1].astype(jnp.float32), flow[c]
+                        )
+                        if 1 <= k:
+                            flux = (fresh - x[c]) * rates[k]
+                            fresh_once = x[c] + (flux - first_flux[c])
+                            first_flux[c] = flux
+                        x[c] = fresh
+                    elif k == depth:
+                        fresh_once = x[c] - first_flux[c]
+                    if 2 <= k:
+                        if k <= depth:
+                            flux = (fresh_once - once[c]) * rates[k - 1]
+                            twice = once[c] + (flux - second_flux[c])
+                            second_flux[c] = flux
+                        else:
+                            twice = once[c] - second_flux[c]
+                        done.append((c, k - 2, twice))
+                        field[c] = jnp.where(wets[k - 2], twice, field[c])
+                    if fresh_once is not None:
+                        once[c] = fresh_once
+            for c, k, value in done:
+                column[b, c, k, span, :] = value
         speed = jnp.sqrt(flow[0] * flow[0] + flow[1] * flow[1] + speed_floor)
         along = flow[0] * field[0] + flow[1] * field[1]
         ratio = along / speed
@@ -252,10 +255,9 @@
     )(block_ids, level_count, drag_coef, adjoint_vel, velocity, after, *earlier)
 
 
-PAD = SUBLANES
+WIDTH = LANES + 2 * STEPS
+SPAN = WIDTH // SUBLANES
 BATCH = 3
-WIDTH = LANES + 2 * STEPS
-PITCH = WIDTH + 2 * PAD
 NEIGHBOURS = [(down, right) for down in (-1, 0, 1) for right in (0, 1, -1)]
 
 
@@ -293,7 +295,25 @@
         natural[1, start:start + rows, :] = sides
 
 
-def turn(natural, deep, put):
+def strip_pieces(first, count):
+    pieces = []
+    x = first
+    while x < first + count:
+        length = min(SPAN - x % SPAN, first + count - x)
+        pieces.append((x - first, x // SPAN, x % SPAN, length))
+        x += length
+    return pieces
+
+
+def turned_rows(i, sublane, n, length):
+    return pl.ds(i * WIDTH + n * SUBLANES + sublane, length, stride=SUBLANES)
+
+
+def turn(natural, deep, target):
+    def put(i, first, values):
+        for offset, sublane, n, length in strip_pieces(first, values.shape[0]):
+            target[turned_rows(i, sublane, n, length), :] = values[offset:offset + length]
+
     for i in range(deep):
         put(i, STEPS, natural[0, pl.ds(i, LANES, stride=deep), :].T)
         sides = natural[1, pl.ds(i, LANES, stride=deep), :].T
@@ -301,27 +321,72 @@
         put(i, 0, sides[LANES - STEPS:])
 
 
-def rows_at(ref, start, shift=0):
-    return ref[pl.ds(start + shift, SUBLANES), :]
-
-
-def in_batches(chunks, work):
+def turn_back(source, natural, tile, deep):
+    for i in range(deep):
+        values = jnp.concatenate(
+            [
+                source[turned_rows(i, sublane, n, length), :]
+                for _, sublane, n, length in strip_pieces(STEPS, LANES)
+            ],
+            axis=0,
+        )
+        natural[tile, pl.ds(i, LANES, stride=deep), :] = values.T
+
+
+def vector(i, n):
+    start = (i * SPAN + n) * SUBLANES
+    return slice(start, start + SUBLANES)
+
+
+def in_batches(deep, work):
     late = []
-    for start in range(0, len(chunks), BATCH):
-        batch = [item for chunk in chunks[start:start + BATCH] for item in work(chunk)]
-        for ref, a, value in late:
-            ref[pl.ds(a, SUBLANES), :] = value
+    for start in range(0, SPAN, BATCH):
+        batch = [
+            (ref, vector(i, n), value)
+            for n in range(start, min(start + BATCH, SPAN))
+            for i in range(deep)
+            for ref, value in work(i, n)
+        ]
+        for ref, at, value in late:
+            ref[at, :] = value
         late = batch
-    for ref, a, value in late:
-        ref[pl.ds(a, SUBLANES), :] = value
-
-
-def strip_rows(ref, chunk, deep):
-    at = [i * PITCH + PAD + chunk * SUBLANES for i in range(deep)]
-    here = [rows_at(ref, a) for a in at]
-    above = [pltpu.roll(here[-1], 1, 1)] + here[:-1]
-    below = here[1:] + [pltpu.roll(here[0], LANES - 1, 1)]
-    return here, above, below, at
+    for ref, at, value in late:
+        ref[at, :] = value
+
+
+class Around:
+    def __init__(self, ref, deep):
+        self.ref = ref
+        self.deep = deep
+        self.held = {}
+
+    def here(self, i, n):
+        if (i, n) not in self.held:
+            self.held[i, n] = self.ref[vector(i, n), :]
+        return self.held[i, n]
+
+    def east(self, i, n):
+        if n + 1 < SPAN:
+            return self.here(i, n + 1)
+        return pltpu.roll(self.ref[vector(i, 0), :], SUBLANES - 1, 0)
+
+    def west(self, i, n):
+        if n > 0:
+            return self.here(i, n - 1)
+        return pltpu.roll(self.ref[vector(i, SPAN - 1), :], 1, 0)
+
+    def north(self, i, n):
+        if i > 0:
+            return self.here(i - 1, n)
+        return pltpu.roll(self.here(self.deep - 1, n), 1, 1)
+
+    def south(self, i, n):
+        if i + 1 < self.deep:
+            return self.here(i + 1, n)
+        return pltpu.roll(self.here(0, n), LANES - 1, 1)
+
+    def total(self, i, n):
+        return (self.east(i, n) + self.west(i, n)) + (self.north(i, n) + self.south(i, n))
 
 
 def depth_kernel(ids_ref, bathymetry_ref, mask_ref, out_ref, ids, bathymetry, mask, sems):
@@ -421,33 +486,26 @@
 
     scale = chebyshev_sum(STEPS)[1]
 
-    def put(i, x, values):
-        start = i * PITCH + PAD + x
-        root_ref[start:start + values.shape[0], :] = jnp.sqrt(values)
-        around_ref[start:start + values.shape[0], :] = scale * values
-
-    turn(natural, deep, put)
-    zeros = jnp.zeros((PAD, LANES), jnp.float32)
-    for i in range(deep):
-        root_ref[i * PITCH:i * PITCH + PAD, :] = zeros
-        root_ref[(i + 1) * PITCH - PAD:(i + 1) * PITCH, :] = zeros
-
-    def work(chunk):
-        here, above, below, at = strip_rows(root_ref, chunk, deep)
-        out = []
-        for i, a in enumerate(at):
-            others = (rows_at(root_ref, a, 1) + rows_at(root_ref, a, -1)) + (above[i] + below[i])
-            out.append((centre_ref, a, 2.0 - scale * here[i] * others))
-        return out
-
-    in_batches(range(WIDTH // SUBLANES), work)
+    turn(natural, deep, around_ref)
+
+    def roots(i, n):
+        scaled = around_ref[vector(i, n), :]
+        return [(root_ref, jnp.sqrt(scaled)), (around_ref, scale * scaled)]
+
+    in_batches(deep, roots)
+    root = Around(root_ref, deep)
+
+    def centres(i, n):
+        return [(centre_ref, 2.0 - scale * root.here(i, n) * root.total(i, n))]
+
+    in_batches(deep, centres)
 
 
 def surface_weights(near, far, me, block_ids, rows, lon_count, lat_count):
     slots = block_ids.shape[0]
     assert near.shape[-1] == LANES
     strips, deep, tall = window_shape(slots, rows)
-    shape = jax.ShapeDtypeStruct((deep * PITCH, LANES), jnp.float32)
+    shape = jax.ShapeDtypeStruct((deep * WIDTH, LANES), jnp.float32)
     return pl.pallas_call(
         functools.partial(weights_kernel, slots, lon_count, lat_count),
         in_specs=[SMEM, SMEM, VMEM, VMEM],
@@ -502,95 +560,62 @@
 
     coefs, step_scale = chebyshev_sum(STEPS)
 
-    def put(i, x, values):
-        start = i * PITCH + PAD + x
-        stop = start + values.shape[0]
-        root = root_ref[start:stop, :]
-        values = jnp.where(root > 0.0, root * values, 0.0)
-        source[start:stop, :] = values
-        even[start:stop, :] = coefs[STEPS - 1] * values
-        odd[start:stop, :] = jnp.zeros_like(values)
-
-    zeros = jnp.zeros((PAD, LANES), jnp.float32)
-    for ref in (even, odd):
-        for i in range(deep):
-            ref[i * PITCH:i * PITCH + PAD, :] = zeros
-            ref[(i + 1) * PITCH - PAD:(i + 1) * PITCH, :] = zeros
-    turn(natural, deep, put)
-
-    chunks = WIDTH // SUBLANES
-
-    def apply(current, target, coef, gain, m):
-        def work(chunk):
-            here, above, below, at = strip_rows(current, chunk, deep)
-            out = []
-            for i, a in enumerate(at):
-                others = (rows_at(current, a, 1) + rows_at(current, a, -1)) + (
-                    above[i] + below[i]
-                )
-                pushed = rows_at(centre_ref, a) * here[i] + rows_at(around_ref, a) * others
-                if gain != 1.0:
-                    pushed = gain * pushed
-                kept = coef * rows_at(source, a) - rows_at(target, a)
-                out.append((target, a, kept + pushed))
-            return out
-
-        in_batches(range(m // SUBLANES, chunks - m // SUBLANES), work)
-
-    runs = []
-    for m in range(1, STEPS - 1, 2):
-        if runs and runs[-1][0] // SUBLANES == m // SUBLANES:
-            runs[-1][1] += 1
-        else:
-            runs.append([m, 1])
-    for first, pairs in runs:
-        def two_steps(pair, carry, first=first):
-            m = first + 2 * pair
-            apply(even, odd, coefs_ref[m], 1.0, first)
-            apply(odd, even, coefs_ref[m + 1], 1.0, first)
-            return carry
-
-        lax.fori_loop(0, pairs, two_steps, 0)
-    apply(even, odd, coefs[0], 0.5, STEPS - 1)
-
-    low = STEPS // SUBLANES - 1
-
-    def one_height(chunk):
-        out = []
-        for i in range(deep):
-            a = i * PITCH + PAD + chunk * SUBLANES
-            root = rows_at(root_ref, a)
-            out.append((extra, a, jnp.where(root > 0.0, rows_at(odd, a) / root, 0.0)))
-        return out
-
-    in_batches(range(low, chunks - low), one_height)
-
-    def differences(chunk):
-        here, above, below, at = strip_rows(extra, chunk, deep)
-        root, root_above, root_below, _ = strip_rows(root_ref, chunk, deep)
-        out = []
-        for i, a in enumerate(at):
-            east_step = rows_at(extra, a, 1) - here[i]
-            west_step = here[i] - rows_at(extra, a, -1)
-            south_step = below[i] - here[i]
-            north_step = here[i] - above[i]
-            energy = root[i] * (
-                (rows_at(root_ref, a, 1) * east_step * east_step
-                 + rows_at(root_ref, a, -1) * west_step * west_step)
-                + (root_below[i] * south_step * south_step
-                   + root_above[i] * north_step * north_step)
-            )
-            scaled = rows_at(around_ref, a) * (1.0 / step_scale)
-            out.append((even, a, east_step))
-            out.append((source, a, 0.25 * energy / jnp.maximum(scaled, 0.25)))
-        return out
-
-    in_batches(range(low + 1, chunks - low - 1), differences)
-
-    def turn_back(ref, tile):
-        for i in range(deep):
-            start = i * PITCH + PAD + STEPS
-            natural[tile, pl.ds(i, LANES, stride=deep), :] = ref[start:start + LANES, :].T
+    turn(natural, deep, source)
+
+    def starts(i, n):
+        at = vector(i, n)
+        root = root_ref[at, :]
+        value = jnp.where(root > 0.0, root * source[at, :], 0.0)
+        return [(source, value), (even, coefs[STEPS - 1] * value), (odd, jnp.zeros_like(value))]
+
+    in_batches(deep, starts)
+
+    def apply(current, target, coef, gain):
+        values = Around(current, deep)
+
+        def work(i, n):
+            at = vector(i, n)
+            pushed = centre_ref[at, :] * values.here(i, n) + around_ref[at, :] * values.total(i, n)
+            if gain != 1.0:
+                pushed = gain * pushed
+            return [(target, (coef * source[at, :] - target[at, :]) + pushed)]
+
+        in_batches(deep, work)
+
+    def two_steps(pair, carry):
+        apply(even, odd, coefs_ref[2 * pair + 1], 1.0)
+        apply(odd, even, coefs_ref[2 * pair + 2], 1.0)
+        return carry
+
+    lax.fori_loop(0, (STEPS - 2) // 2, two_steps, 0)
+    apply(even, odd, coefs[0], 0.5)
+
+    def heights(i, n):
+        at = vector(i, n)
+        root = root_ref[at, :]
+        return [(extra, jnp.where(root > 0.0, odd[at, :] / root, 0.0))]
+
+    in_batches(deep, heights)
+    height = Around(extra, deep)
+    root = Around(root_ref, deep)
+
+    def differences(i, n):
+        here = height.here(i, n)
+        energy = None
+        east_step = height.east(i, n) - here
+        for step, weight in (
+            (east_step, root.east(i, n)),
+            (here - height.west(i, n), root.west(i, n)),
+            (height.south(i, n) - here, root.south(i, n)),
+            (here - height.north(i, n), root.north(i, n)),
+        ):
+            part = weight * step * step
+            energy = part if energy is None else energy + part
+        energy = root.here(i, n) * energy
+        scaled = around_ref[vector(i, n), :] * (1.0 / step_scale)
+        return [(even, east_step), (source, 0.25 * energy / jnp.maximum(scaled, 0.25))]
+
+    in_batches(deep, differences)
 
     def cut(tile, w, shift=0):
         return natural[tile, pl.ds(w * tall + STEPS + shift, rows), :]
@@ -616,7 +641,7 @@
             column[b, c, k] = value
         copy_out(b, c).start()
 
-    turn_back(even, 0)
+    turn_back(even, natural, 0, deep)
     for copy in copies_in:
         copy.wait()
 
@@ -629,9 +654,9 @@
         return carry
 
     lax.fori_loop(0, slots, correct_east, 0)
-    turn_back(extra, 1)
+    turn_back(extra, natural, 1, deep)
     lax.fori_loop(0, slots, correct_north, 0)
-    turn_back(source, 0)
+    turn_back(source, natural, 0, deep)
     for h in range(2):
         height_ref[:, h * LANES:(h + 1) * LANES] = cut(1, slots + h)
         sensitivity_ref[:, h * LANES:(h + 1) * LANES] = cut(0, slots + h)
@@ -694,6 +719,9 @@
     )(*parts, *tokens)
 
 
+FIRST_SLOTS = 1
+
+
 def swap(values, axis, mask):
     count = lax.axis_size(axis)
     return lax.ppermute(values, axis, [(i, i ^ mask) for i in range(count)])
@@ -713,11 +741,10 @@
     forcing = column_forcing(adjoint_vel, level_count)
 
     parts = [forcing] + [swap(forcing, "gy", 2 * m) for m in range(1, half)]
-    near_depths = stack_after(depth_parts, parts[1])
+    near_depths = stack_after(depth_parts, forcing)
     near_depths = [near_depths] + [swap(near_depths, "gx", m) for m in range(1, lon_count)]
     columns = (adjoint_vel, velocity, drag_coef, level_count, block_ids)
-    middle = (slots + 1) // 2
-    first_column, *first_rest = column_mixing(*columns, forcing, block_total, 0, middle)
+    first_column, *first_rest = column_mixing(*columns, forcing, block_total, 0, FIRST_SLOTS)
     line = stack_after(parts, first_rest[0])
 
     near = [line] + [swap(line, "gx", m) for m in range(1, lon_count)]
@@ -725,7 +752,7 @@
     near_depths = near_depths.reshape((lon_count * half,) + depths.shape)
     far_depths = swap(near_depths, "gy", 1)
     last_column, bottom, drag_gradient = column_mixing(
-        *columns, line, block_total, middle, slots, first_rest
+        *columns, line, block_total, FIRST_SLOTS, slots, first_rest
     )
     weights = surface_weights(
         near_depths, far_depths, me, block_ids, rows, lon_count, lat_count

time: 58.5 us -> 57.5 us (0.983)
  waiting for transfers between devices: 8.81 us -> 6.7 us
  Pallas kernels: 31.7 us -> 33 us
    ppermute x14, waiting for transfers between devices: 8.81 us -> 6.7 us  [swap(): return lax.ppermute(values, axis, [(i, i ^ mask) for i in range(count)])]
    pallas_call x1, Pallas kernels: 12.4 us -> 13.2 us  [surface_solve(): pl.pallas_call(functools.partial(solve_kernel, block_total), in_specs=[SM...]
    pallas_call x2, Pallas kernels: 11.6 us -> 12.2 us  [column_mixing(): pl.pallas_call(functools.partial(mixing_kernel, block_total, first, len(e...]
  transfers between devices with their start and end apart: 14 -> 14, of which waited for: 5 -> 5; matrix products, arithmetic and copies ran while one was open for 0% -> 0% of each run, Pallas kernels for 26% -> 33%
where the time goes in v4:
time: 57.5 us; the launch traced here: 57.1 us
  Pallas kernels  33 us (57%)
  starting transfers between devices  16.4 us (29%)
  waiting for transfers between devices  6.7 us (12%)
  between operations  0.82 us (1%)
    ppermute x14, starting transfers between devices, swap(): return lax.ppermute(values, axis, [(i, i ^ mask) for i in range(count)])  16.4 us
    pallas_call x1, Pallas kernels, surface_solve(): pl.pallas_call(functools.partial(solve_kernel, block_total), in_specs=[SM...  13.2 us
    pallas_call x2, Pallas kernels, column_mixing(): pl.pallas_call(functools.partial(mixing_kernel, block_total, first, len(e...  12.2 us
    ppermute x14, waiting for transfers between devices, swap(): return lax.ppermute(values, axis, [(i, i ^ mask) for i in range(count)])  6.7 us
    pallas_call x1, Pallas kernels, column_forcing(): pl.pallas_call(forcing_kernel, in_specs=[HBM, HBM], out_specs=VMEM, out_s...  3.86 us
    pallas_call x1, Pallas kernels, surface_weights(): pl.pallas_call(functools.partial(weights_kernel, slots, lon_count, lat_co...  2.78 us
  transfers between devices with their start and end apart: 14, of which 5 were waited for; matrix products, arithmetic and copies ran while one was open for 0% of the time, Pallas kernels for 33%

profile of v4, /device:TPU:0, one launch (start us, length us, event | category | flops | bytes accessed | tf_op | source)
XLA Modules:
  0.0 57.1 jit_solution(13815022237431864701)
XLA Ops:
  0.6 0.0 copy-start.2
  0.6 0.0 copy-start
  0.7 0.0 copy-start.1
  0.7 0.8 %depth_payload.1.refs_0_ = f32[72,128]{1,0:T(8,128)S(1)} custom-call(s32[4]{0:T(128)} %ids_ref.9, f32[32,256]{1,0:T(8,128)} %bathymetry_ref.1, s32[32,256]{1,0:T(8,128)} %mask_ref.1), custom_call_target="tpu_custom_call" | custom-call | tf_op jit(solution)/shard_map/depth_payload/pallas_call | solution.py:415
  1.5 5.1 %collective-permute-start.2 = (f32[72,128]{1,0:T(8,128)S(1)}, f32[72,128]{1,0:T(8,128)S(1)}, u32[]{:S(2)}, u32[]{:S(2)}) collective-permute-start(f32[72,128]{1,0:T(8,128)S(1)} %depth_payload.1.refs_0_), channel_id=1, source_target_pairs={{0,6},{1,7},{2,4},{3,5},{4,2},{5,3},{6,0},{7,1},{8,14},{9,15},{10,... | collective-permute-start | bytes 110600 | tf_op jit(solution)/shard_map/ppermute | solution.py:727
  6.6 0.0 collective-permute-start.1
  6.6 0.6 %collective-permute-start = (f32[72,128]{1,0:T(8,128)S(1)}, f32[72,128]{1,0:T(8,128)S(1)}, u32[]{:S(2)}, u32[]{:S(2)}) collective-permute-start(f32[72,128]{1,0:T(8,128)S(1)} %depth_payload.1.refs_0_), channel_id=1, source_target_pairs={{0,2},{1,3},{2,0},{3,1},{4,6},{5,7},{6,4},{7,5},{8,10},{9,11},{10,... | collective-permute-start | bytes 110600 | tf_op jit(solution)/shard_map/ppermute | solution.py:727
  7.3 3.9 %column_forcing.1.refs_4_.after_ref.refs_0_ = f32[4,32,128]{2,1,0:T(8,128)S(1)} custom-call(s32[4,32,128]{2,1,0:T(8,128)} %levels_ref.7, f32[4,2,62,32,128]{4,3,2,1,0:T(8,128)} %adjoint_ref.5), custom_call_target="tpu_custom_call" | custom-call | flops 4063232 | bytes 8126464 | tf_op jit(solution)/shard_map/column_forcing/pallas_call | solution.py:95
  11.1 0.0 collective-permute-done.2.refs_3_
  11.2 0.3 collective-permute-done.1.refs_2_
  11.5 0.0 collective-permute-done.refs_1_
  11.5 2.5 %collective-permute-start.5 = (f32[4,72,128]{2,1,0:T(8,128)S(1)}, f32[4,72,128]{2,1,0:T(8,128)S(1)}, u32[]{:S(2)}, u32[]{:S(2)}) collective-permute-start(f32[4,72,128]{2,1,0:T(8,128)S(1)} %stack_after.4.refs_0_), channel_id=1, source_target_pairs={{0,24},{8,16},{16,8},{24,0},{1,25},{9,17},{17,9},{25,1},{2,26},{10... | collective-permute-start | bytes 442376 | tf_op jit(solution)/shard_map/ppermute | solution.py:727
  14.0 0.5 collective-permute-start.4
  14.5 0.5 collective-permute-start.3
  15.1 3.4 %collective-permute-start.8 = (f32[4,32,128]{2,1,0:T(8,128)S(1)}, f32[4,32,128]{2,1,0:T(8,128)S(1)}, u32[]{:S(2)}, u32[]{:S(2)}) collective-permute-start(f32[4,32,128]{2,1,0:T(8,128)S(1)} %column_forcing.1.refs_4_.after_ref.refs_0_), channel_id=1, source_target_pairs={{0,6},{1,7},{2,4},{3,5},{4,2},{5,3},{6,0},{7,1},{8,14},{9,15},{10,... | collective-permute-start | bytes 196616 | tf_op jit(solution)/shard_map/ppermute | solution.py:727
  18.5 0.0 collective-permute-start.7
  18.5 2.8 %collective-permute-done.8.refs_3_ = f32[4,32,128]{2,1,0:T(8,128)S(1)} collective-permute-done((f32[4,32,128]{2,1,0:T(8,128)S(1)}, f32[4,32,128]{2,1,0:T(8,128)S(1)}, u32[]{:S(2)}, u32[]{:S(2)}) %collective-permute-start.8) | collective-permute-done | bytes 65568 | tf_op jit(solution)/shard_map/ppermute | solution.py:727
  21.3 0.0 collective-permute-start.6
  21.3 0.0 copy-done.2
  21.3 0.0 copy-done
  21.3 0.0 copy-done.1
  21.3 4.2 %column_mixing.2 = (f32[1,2,62,32,128]{4,3,2,1,0:T(8,128)}, f32[1,2,32,128]{3,2,1,0:T(8,128)S(1)}, f32[1,32,128]{2,1,0:T(8,128)S(1)}) custom-call(s32[4]{0:T(128)S(1)} %copy-done.2, s32[4,32,128]{2,1,0:T(8,128)S(1)} %copy-done, f32[4,32,128]{2,1,0:T(8,128)S(1)} %copy-done.1, f32[4,2,62,32,128]{4,3,2,1,0:T(8,128)} %adjoint_ref.5, ...), custom_call_target="tpu_custom_call" | custom-call | flops 7110656 | bytes 5079040 | tf_op jit(solution)/shard_map/column_mixing/pallas_call | solution.py:234
  25.6 0.0 collective-permute-done.7.refs_2_
  25.6 0.0 collective-permute-done.6.refs_1_
  25.6 0.0 collective-permute-done.5.refs_3_
  25.6 0.0 collective-permute-done.4.refs_2_
  25.6 0.0 collective-permute-done.3.refs_1_
  25.7 0.1 collective-permute-start.9
  25.8 2.5 %collective-permute-start.12 = (f32[4,4,32,128]{3,2,1,0:T(8,128)S(1)}, f32[4,4,32,128]{3,2,1,0:T(8,128)S(1)}, u32[]{:S(2)}, u32[]{:S(2)}) collective-permute-start(f32[4,4,32,128]{3,2,1,0:T(8,128)S(1)} %stack_after.5.refs_4_.after_ref.refs_0_), channel_id=1, source_target_pairs={{0,24},{8,16},{16,8},{24,0},{1,25},{9,17},{17,9},{25,1},{2,26},{10... | collective-permute-start | bytes 786440 | tf_op jit(solution)/shard_map/ppermute | solution.py:727
  28.3 0.5 collective-permute-start.11
  28.8 0.5 collective-permute-start.10
  29.3 0.1 pad_add_fusion.me_ref
  29.4 0.0 copy-start.3
  29.4 8.0 %column_mixing.3 = (f32[3,2,62,32,128]{4,3,2,1,0:T(8,128)}, f32[4,2,32,128]{3,2,1,0:T(8,128)S(1)}, f32[4,32,128]{2,1,0:T(8,128)}) custom-call(s32[4]{0:T(128)S(1)} %copy-done.2, s32[4,32,128]{2,1,0:T(8,128)S(1)} %copy-done, f32[4,32,128]{2,1,0:T(8,128)S(1)} %copy-done.1, f32[4,2,62,32,128]{4,3,2,1,0:T(8,128)} %adjoint_ref.5, ...), custom_call_target="tpu_custom_call" | custom-call | flops 21331968 | bytes 15237120 | tf_op jit(solution)/shard_map/column_mixing/pallas_call | solution.py:234
  37.4 0.0 collective-permute-done.9.far_ref
  37.4 2.8 %surface_weights.1 = (f32[960,128]{1,0:T(8,128)S(1)}, f32[960,128]{1,0:T(8,128)S(1)}, f32[960,128]{1,0:T(8,128)S(1)}, s32[54]{0:T(128)S(1)}) custom-call(s32[2]{0:T(128)S(1)} %pad_add_fusion.me_ref, s32[4]{0:T(128)S(1)} %copy-done.2, f32[16,72,128]{2,1,0:T(8,128)S(1)} %bitcast.7, f32[16,72,128]{2,1,0:T(8,128)S(1)} %collective-permute-done.9.far_ref), custom_call_target="tpu_custom_call" | custom-call | bytes 8388608 | tf_op jit(solution)/shard_map/surface_weights/pallas_call | solution.py:509
  40.2 0.0 collective-permute-done.12.refs_3_
  40.2 0.8 %collective-permute-done.11.refs_2_ = f32[4,4,32,128]{3,2,1,0:T(8,128)S(1)} collective-permute-done((f32[4,4,32,128]{3,2,1,0:T(8,128)S(1)}, f32[4,4,32,128]{3,2,1,0:T(8,128)S(1)}, u32[]{:S(2)}, u32[]{:S(2)}) %collective-permute-start.11) | collective-permute-done | bytes 262176 | tf_op jit(solution)/shard_map/ppermute | solution.py:727
  41.0 0.1 collective-permute-done.10.refs_1_
  41.1 0.1 stack_after.7
  41.2 0.1 collective-permute-start.13
  41.3 2.6 %collective-permute-done.13 = f32[4,4,4,32,128]{4,3,2,1,0:T(8,128)S(1)} collective-permute-done((f32[4,4,4,32,128]{4,3,2,1,0:T(8,128)S(1)}, f32[4,4,4,32,128]{4,3,2,1,0:T(8,128)S(1)}, u32[]{:S(2)}, u32[]{:S(2)}) %collective-permute-start.13) | collective-permute-done | bytes 1048608 | tf_op jit(solution)/shard_map/ppermute | solution.py:727
  43.9 0.0 copy-done.3
  43.9 13.2 %surface_solve.1 = (f32[4,2,62,32,128]{4,3,2,1,0:T(8,128)}, f32[32,256]{1,0:T(8,128)}, f32[32,256]{1,0:T(8,128)}) custom-call(s32[4]{0:T(128)S(1)} %copy-done.2, s32[54]{0:T(128)S(1)} %get-tuple-element.18.table_ref, f32[32]{0:T(128)S(1)} %copy-done.3, f32[960,128]{1,0:T(8,128)S(1)} %get-tuple-element.19.refs_5_.root_ref, ...), custom_call_target="tpu_custom_call" | custom-call | flops 35389440 | bytes 1966080 | tf_op jit(solution)/shard_map/surface_solve/pallas_call | solution.py:678
  (3 shorter events, 0.1 us)
Async XLA Ops:
  0.6 20.7 %copy-start.2 = (s32[4]{0:T(128)S(1)}, s32[4]{0:T(128)}, u32[]{:S(2)}) copy-start(s32[4]{0:T(128)} %ids_ref.9) | copy-start | bytes 52
  0.6 20.6 %copy-start = (s32[4,32,128]{2,1,0:T(8,128)S(1)}, s32[4,32,128]{2,1,0:T(8,128)}, u32[]{:S(2)}) copy-start(s32[4,32,128]{2,1,0:T(8,128)} %levels_ref.7) | copy-start | bytes 196612
  0.7 20.6 %copy-start.1 = (f32[4,32,128]{2,1,0:T(8,128)S(1)}, f32[4,32,128]{2,1,0:T(8,128)}, u32[]{:S(2)}) copy-start(f32[4,32,128]{2,1,0:T(8,128)} %drag_ref.3) | copy-start | bytes 196612
  1.5 9.6 %collective-permute-start.2 = (f32[72,128]{1,0:T(8,128)S(1)}, f32[72,128]{1,0:T(8,128)S(1)}, u32[]{:S(2)}, u32[]{:S(2)}) collective-permute-start(f32[72,128]{1,0:T(8,128)S(1)} %depth_payload.1.refs_0_), channel_id=1, source_target_pairs={{0,6},{1,7},{2,4},{3,5},{4,2},{5,3},{6,0},{7,1},{8,14},{9,15},{10,... | collective-permute-start | bytes 110600 | tf_op jit(solution)/shard_map/ppermute | solution.py:727
  6.6 4.9 %collective-permute-start.1 = (f32[72,128]{1,0:T(8,128)S(1)}, f32[72,128]{1,0:T(8,128)S(1)}, u32[]{:S(2)}, u32[]{:S(2)}) collective-permute-start(f32[72,128]{1,0:T(8,128)S(1)} %depth_payload.1.refs_0_), channel_id=1, source_target_pairs={{0,4},{1,5},{2,6},{3,7},{4,0},{5,1},{6,2},{7,3},{8,12},{9,13},{10,... | collective-permute-start | bytes 110600 | tf_op jit(solution)/shard_map/ppermute | solution.py:727
  6.6 4.9 %collective-permute-start = (f32[72,128]{1,0:T(8,128)S(1)}, f32[72,128]{1,0:T(8,128)S(1)}, u32[]{:S(2)}, u32[]{:S(2)}) collective-permute-start(f32[72,128]{1,0:T(8,128)S(1)} %depth_payload.1.refs_0_), channel_id=1, source_target_pairs={{0,2},{1,3},{2,0},{3,1},{4,6},{5,7},{6,4},{7,5},{8,10},{9,11},{10,... | collective-permute-start | bytes 110600 | tf_op jit(solution)/shard_map/ppermute | solution.py:727
  11.5 14.1 %collective-permute-start.5 = (f32[4,72,128]{2,1,0:T(8,128)S(1)}, f32[4,72,128]{2,1,0:T(8,128)S(1)}, u32[]{:S(2)}, u32[]{:S(2)}) collective-permute-start(f32[4,72,128]{2,1,0:T(8,128)S(1)} %stack_after.4.refs_0_), channel_id=1, source_target_pairs={{0,24},{8,16},{16,8},{24,0},{1,25},{9,17},{17,9},{25,1},{2,26},{10... | collective-permute-start | bytes 442376 | tf_op jit(solution)/shard_map/ppermute | solution.py:727
  14.0 11.6 %collective-permute-start.4 = (f32[4,72,128]{2,1,0:T(8,128)S(1)}, f32[4,72,128]{2,1,0:T(8,128)S(1)}, u32[]{:S(2)}, u32[]{:S(2)}) collective-permute-start(f32[4,72,128]{2,1,0:T(8,128)S(1)} %stack_after.4.refs_0_), channel_id=1, source_target_pairs={{0,16},{8,24},{16,0},{24,8},{1,17},{9,25},{17,1},{25,9},{2,18},{10... | collective-permute-start | bytes 442376 | tf_op jit(solution)/shard_map/ppermute | solution.py:727
  14.5 11.1 %collective-permute-start.3 = (f32[4,72,128]{2,1,0:T(8,128)S(1)}, f32[4,72,128]{2,1,0:T(8,128)S(1)}, u32[]{:S(2)}, u32[]{:S(2)}) collective-permute-start(f32[4,72,128]{2,1,0:T(8,128)S(1)} %stack_after.4.refs_0_), channel_id=1, source_target_pairs={{0,8},{8,0},{16,24},{24,16},{1,9},{9,1},{17,25},{25,17},{2,10},{10... | collective-permute-start | bytes 442376 | tf_op jit(solution)/shard_map/ppermute | solution.py:727
  15.1 6.2 %collective-permute-start.8 = (f32[4,32,128]{2,1,0:T(8,128)S(1)}, f32[4,32,128]{2,1,0:T(8,128)S(1)}, u32[]{:S(2)}, u32[]{:S(2)}) collective-permute-start(f32[4,32,128]{2,1,0:T(8,128)S(1)} %column_forcing.1.refs_4_.after_ref.refs_0_), channel_id=1, source_target_pairs={{0,6},{1,7},{2,4},{3,5},{4,2},{5,3},{6,0},{7,1},{8,14},{9,15},{10,... | collective-permute-start | bytes 196616 | tf_op jit(solution)/shard_map/ppermute | solution.py:727
  18.5 7.1 %collective-permute-start.7 = (f32[4,32,128]{2,1,0:T(8,128)S(1)}, f32[4,32,128]{2,1,0:T(8,128)S(1)}, u32[]{:S(2)}, u32[]{:S(2)}) collective-permute-start(f32[4,32,128]{2,1,0:T(8,128)S(1)} %column_forcing.1.refs_4_.after_ref.refs_0_), channel_id=1, source_target_pairs={{0,4},{1,5},{2,6},{3,7},{4,0},{5,1},{6,2},{7,3},{8,12},{9,13},{10,... | collective-permute-start | bytes 196616 | tf_op jit(solution)/shard_map/ppermute | solution.py:727
  21.3 4.3 %collective-permute-start.6 = (f32[4,32,128]{2,1,0:T(8,128)S(1)}, f32[4,32,128]{2,1,0:T(8,128)S(1)}, u32[]{:S(2)}, u32[]{:S(2)}) collective-permute-start(f32[4,32,128]{2,1,0:T(8,128)S(1)} %column_forcing.1.refs_4_.after_ref.refs_0_), channel_id=1, source_target_pairs={{0,2},{1,3},{2,0},{3,1},{4,6},{5,7},{6,4},{7,5},{8,10},{9,11},{10,... | collective-permute-start | bytes 196616 | tf_op jit(solution)/shard_map/ppermute | solution.py:727
  25.7 11.7 %collective-permute-start.9 = (f32[16,72,128]{2,1,0:T(8,128)S(1)}, f32[16,72,128]{2,1,0:T(8,128)S(1)}, u32[]{:S(2)}, u32[]{:S(2)}) collective-permute-start(f32[16,72,128]{2,1,0:T(8,128)S(1)} %bitcast.6), channel_id=1, source_target_pairs={{0,1},{1,0},{2,3},{3,2},{4,5},{5,4},{6,7},{7,6},{8,9},{9,8},{10,11... | collective-permute-start | bytes 1769480 | tf_op jit(solution)/shard_map/ppermute | solution.py:727
  25.8 14.4 %collective-permute-start.12 = (f32[4,4,32,128]{3,2,1,0:T(8,128)S(1)}, f32[4,4,32,128]{3,2,1,0:T(8,128)S(1)}, u32[]{:S(2)}, u32[]{:S(2)}) collective-permute-start(f32[4,4,32,128]{3,2,1,0:T(8,128)S(1)} %stack_after.5.refs_4_.after_ref.refs_0_), channel_id=1, source_target_pairs={{0,24},{8,16},{16,8},{24,0},{1,25},{9,17},{17,9},{25,1},{2,26},{10... | collective-permute-start | bytes 786440 | tf_op jit(solution)/shard_map/ppermute | solution.py:727
  28.3 12.7 %collective-permute-start.11 = (f32[4,4,32,128]{3,2,1,0:T(8,128)S(1)}, f32[4,4,32,128]{3,2,1,0:T(8,128)S(1)}, u32[]{:S(2)}, u32[]{:S(2)}) collective-permute-start(f32[4,4,32,128]{3,2,1,0:T(8,128)S(1)} %stack_after.5.refs_4_.after_ref.refs_0_), channel_id=1, source_target_pairs={{0,16},{8,24},{16,0},{24,8},{1,17},{9,25},{17,1},{25,9},{2,18},{10... | collective-permute-start | bytes 786440 | tf_op jit(solution)/shard_map/ppermute | solution.py:727
  28.8 12.3 %collective-permute-start.10 = (f32[4,4,32,128]{3,2,1,0:T(8,128)S(1)}, f32[4,4,32,128]{3,2,1,0:T(8,128)S(1)}, u32[]{:S(2)}, u32[]{:S(2)}) collective-permute-start(f32[4,4,32,128]{3,2,1,0:T(8,128)S(1)} %stack_after.5.refs_4_.after_ref.refs_0_), channel_id=1, source_target_pairs={{0,8},{8,0},{16,24},{24,16},{1,9},{9,1},{17,25},{25,17},{2,10},{10... | collective-permute-start | bytes 786440 | tf_op jit(solution)/shard_map/ppermute | solution.py:727
  29.4 14.5 %copy-start.3 = (f32[32]{0:T(128)S(1)}, f32[32]{0:T(128)}, u32[]{:S(2)}) copy-start(f32[32]{0:T(128)} %constant.10.clone.coefs_ref) | copy-start | bytes 388
  41.2 2.7 %collective-permute-start.13 = (f32[4,4,4,32,128]{4,3,2,1,0:T(8,128)S(1)}, f32[4,4,4,32,128]{4,3,2,1,0:T(8,128)S(1)}, u32[]{:S(2)}, u32[]{:S(2)}) collective-permute-start(f32[4,4,4,32,128]{4,3,2,1,0:T(8,128)S(1)} %stack_after.7), channel_id=1, source_target_pairs={{0,1},{1,0},{2,3},{3,2},{4,5},{5,4},{6,7},{7,6},{8,9},{9,8},{10,11... | collective-permute-start | bytes 3145736 | tf_op jit(solution)/shard_map/ppermute | solution.py:727

commit v5 on v2

--- a/solution.py
+++ b/solution.py
@@ -125,13 +125,16 @@
     group = 16
     parts = rows // group
 
-    def copies_in(b):
+    def copies_in(b, index):
+        span = pl.ds(pl.multiple_of(index * group, group), group)
         return [
-            pltpu.make_async_copy(source.at[first + b, c], target.at[b, c], in_sems.at[n, b, c])
+            pltpu.make_async_copy(
+                source.at[first + b, :, :, span], target.at[b, :, :, span],
+                in_sems.at[n, b, index],
+            )
             for n, (source, target) in enumerate(
                 ((adjoint_ref, adjoint), (velocity_ref, velocity))
             )
-            for c in range(comps)
         ]
 
     def copy_out(b, index):
@@ -141,58 +144,62 @@
         )
 
     for b in range(slots):
-        for copy in copies_in(b):
-            copy.start()
-
-    def one_component(b, c, span, levels):
-        zero = jnp.zeros(levels.shape, jnp.float32)
-        x = once = first_flux = second_flux = flow = field = rate_before = zero
-
-        def store(batch):
-            for k, value in batch:
-                column[b, c, k, span, :] = value
-
-        late = []
-        for low in range(0, depth + 2, CHUNK):
-            batch = []
-            for k in range(low, min(low + CHUNK, depth + 2)):
-                fresh_once = None
-                if k < depth:
-                    wet = levels > k
-                    rate = jnp.where(wet, mix_rate, 0.0)
-                    fresh = jnp.where(wet, adjoint[b, c, k, span, :], 0.0)
-                    flow = jnp.where(
-                        levels == k + 1, velocity[b, c, k, span, :].astype(jnp.float32), flow
-                    )
-                    if 1 <= k:
-                        flux = (fresh - x) * rate
-                        fresh_once = x + (flux - first_flux)
-                        first_flux = flux
-                    x = fresh
-                elif k == depth:
-                    fresh_once = x - first_flux
-                if 2 <= k:
-                    if k <= depth:
-                        flux = (fresh_once - once) * rate_before
-                        twice = once + (flux - second_flux)
-                        second_flux = flux
-                    else:
-                        twice = once - second_flux
-                    batch.append((k - 2, twice))
-                    field = jnp.where(levels == k - 1, twice, field)
-                if fresh_once is not None:
-                    once = fresh_once
-                rate_before = rate
-            store(late)
-            late = batch
-        store(late)
-        return flow, field
+        for index in range(parts):
+            for copy in copies_in(b, index):
+                copy.start()
 
     def one_group(b, index):
         flag = jnp.where(ids_ref[first + b] < block_total, 1.0, 0.0)
         span = pl.ds(pl.multiple_of(index * group, group), group)
         levels = levels_ref[first + b, span, :]
-        flow, field = zip(*[one_component(b, c, span, levels) for c in range(2)])
+        zero = jnp.zeros(levels.shape, jnp.float32)
+        x = [zero, zero]
+        once = [zero, zero]
+        first_flux = [zero, zero]
+        second_flux = [zero, zero]
+        flow = [zero, zero]
+        field = [zero, zero]
+        wets = []
+        rates = []
+        for low in range(0, depth + 2, CHUNK):
+            here = range(low, min(low + CHUNK, depth + 2))
+            loaded = {}
+            for k in here:
+                if k < depth:
+                    for c in range(2):
+                        loaded[k, c] = (adjoint[b, c, k, span, :], velocity[b, c, k, span, :])
+            done = []
+            for k in here:
+                if k < depth:
+                    wets.append(levels > k)
+                    rates.append(jnp.where(wets[k], mix_rate, 0.0))
+                for c in range(2):
+                    fresh_once = None
+                    if k < depth:
+                        fresh = loaded[k, c][0]
+                        flow[c] = jnp.where(
+                            wets[k], loaded[k, c][1].astype(jnp.float32), flow[c]
+                        )
+                        if 1 <= k:
+                            flux = (fresh - x[c]) * rates[k]
+                            fresh_once = x[c] + (flux - first_flux[c])
+                            first_flux[c] = flux
+                        x[c] = fresh
+                    elif k == depth:
+                        fresh_once = x[c] - first_flux[c]
+                    if 2 <= k:
+                        if k <= depth:
+                            flux = (fresh_once - once[c]) * rates[k - 1]
+                            twice = once[c] + (flux - second_flux[c])
+                            second_flux[c] = flux
+                        else:
+                            twice = once[c] - second_flux[c]
+                        done.append((c, k - 2, twice))
+                        field[c] = jnp.where(wets[k - 2], twice, field[c])
+                    if fresh_once is not None:
+                        once[c] = fresh_once
+            for c, k, value in done:
+                column[b, c, k, span, :] = value
         speed = jnp.sqrt(flow[0] * flow[0] + flow[1] * flow[1] + speed_floor)
         along = flow[0] * field[0] + flow[1] * field[1]
         ratio = along / speed
@@ -207,11 +214,8 @@
         b = lax.div(step, parts)
         index = lax.rem(step, parts)
 
-        @pl.when(index == 0)
-        def _():
-            for copy in copies_in(b):
-                copy.wait()
-
+        for copy in copies_in(b, index):
+            copy.wait()
         one_group(b, index)
         copy_out(b, index).start()
         return carry
@@ -241,7 +245,7 @@
             pltpu.VMEM(part, adjoint_vel.dtype),
             pltpu.VMEM(part, velocity.dtype),
             pltpu.VMEM(part, jnp.float32),
-            pltpu.SemaphoreType.DMA((2, slots, comps)),
+            pltpu.SemaphoreType.DMA((2, slots, rows // 16)),
             pltpu.SemaphoreType.DMA((slots, rows // 16)),
         ],
         compiler_params=params(MIXING_VMEM),
@@ -253,7 +257,7 @@
 
 
 PAD = SUBLANES
-BATCH = 3
+BATCH = 2
 WIDTH = LANES + 2 * STEPS
 PITCH = WIDTH + 2 * PAD
 NEIGHBOURS = [(down, right) for down in (-1, 0, 1) for right in (0, 1, -1)]
@@ -694,6 +698,9 @@
     )(*parts, *tokens)
 
 
+FIRST_SLOTS = 1
+
+
 def swap(values, axis, mask):
     count = lax.axis_size(axis)
     return lax.ppermute(values, axis, [(i, i ^ mask) for i in range(count)])
@@ -713,11 +720,10 @@
     forcing = column_forcing(adjoint_vel, level_count)
 
     parts = [forcing] + [swap(forcing, "gy", 2 * m) for m in range(1, half)]
-    near_depths = stack_after(depth_parts, parts[1])
+    near_depths = stack_after(depth_parts, forcing)
     near_depths = [near_depths] + [swap(near_depths, "gx", m) for m in range(1, lon_count)]
     columns = (adjoint_vel, velocity, drag_coef, level_count, block_ids)
-    middle = (slots + 1) // 2
-    first_column, *first_rest = column_mixing(*columns, forcing, block_total, 0, middle)
+    first_column, *first_rest = column_mixing(*columns, forcing, block_total, 0, FIRST_SLOTS)
     line = stack_after(parts, first_rest[0])
 
     near = [line] + [swap(line, "gx", m) for m in range(1, lon_count)]
@@ -725,7 +731,7 @@
     near_depths = near_depths.reshape((lon_count * half,) + depths.shape)
     far_depths = swap(near_depths, "gy", 1)
     last_column, bottom, drag_gradient = column_mixing(
-        *columns, line, block_total, middle, slots, first_rest
+        *columns, line, block_total, FIRST_SLOTS, slots, first_rest
     )
     weights = surface_weights(
         near_depths, far_depths, me, block_ids, rows, lon_count, lat_count

time: 58.5 us -> 56.5 us (0.966)
  waiting for transfers between devices: 8.81 us -> 7.3 us
    ppermute x14, waiting for transfers between devices: 8.81 us -> 7.3 us  [swap(): return lax.ppermute(values, axis, [(i, i ^ mask) for i in range(count)])]
  transfers between devices with their start and end apart: 14 -> 14, of which waited for: 5 -> 6; matrix products, arithmetic and copies ran while one was open for 0% -> 0% of each run, Pallas kernels for 26% -> 32%
where the time goes in v5:
time: 56.5 us; the launch traced here: 56.3 us
  Pallas kernels  31.7 us (56%)
  starting transfers between devices  16.4 us (29%)
  waiting for transfers between devices  7.3 us (13%)
  between operations  0.81 us (1%)
    ppermute x14, starting transfers between devices, swap(): return lax.ppermute(values, axis, [(i, i ^ mask) for i in range(count)])  16.4 us
    pallas_call x1, Pallas kernels, surface_solve(): pl.pallas_call(functools.partial(solve_kernel, block_total), in_specs=[SM...  12.4 us
    pallas_call x2, Pallas kernels, column_mixing(): pl.pallas_call(functools.partial(mixing_kernel, block_total, first, len(e...  11.6 us
    ppermute x14, waiting for transfers between devices, swap(): return lax.ppermute(values, axis, [(i, i ^ mask) for i in range(count)])  7.3 us
    pallas_call x1, Pallas kernels, column_forcing(): pl.pallas_call(forcing_kernel, in_specs=[HBM, HBM], out_specs=VMEM, out_s...  3.86 us
    pallas_call x1, Pallas kernels, surface_weights(): pl.pallas_call(functools.partial(weights_kernel, slots, lon_count, lat_co...  2.74 us
  transfers between devices with their start and end apart: 14, of which 6 were waited for; matrix products, arithmetic and copies ran while one was open for 0% of the time, Pallas kernels for 32%

profile of v5, /device:TPU:0, one launch (start us, length us, event | category | flops | bytes accessed | tf_op | source)
XLA Modules:
  0.0 56.3 jit_solution(15914899177589001629)
XLA Ops:
  0.6 0.0 copy-start.2
  0.6 0.0 copy-start
  0.7 0.0 copy-start.1
  0.7 0.8 %depth_payload.1.refs_0_ = f32[72,128]{1,0:T(8,128)S(1)} custom-call(s32[4]{0:T(128)} %ids_ref.9, f32[32,256]{1,0:T(8,128)} %bathymetry_ref.1, s32[32,256]{1,0:T(8,128)} %mask_ref.1), custom_call_target="tpu_custom_call" | custom-call | tf_op jit(solution)/shard_map/depth_payload/pallas_call | solution.py:354
  1.5 5.1 %collective-permute-start.2 = (f32[72,128]{1,0:T(8,128)S(1)}, f32[72,128]{1,0:T(8,128)S(1)}, u32[]{:S(2)}, u32[]{:S(2)}) collective-permute-start(f32[72,128]{1,0:T(8,128)S(1)} %depth_payload.1.refs_0_), channel_id=1, source_target_pairs={{0,6},{1,7},{2,4},{3,5},{4,2},{5,3},{6,0},{7,1},{8,14},{9,15},{10,... | collective-permute-start | bytes 110600 | tf_op jit(solution)/shard_map/ppermute | solution.py:706
  6.6 0.0 collective-permute-start.1
  6.6 0.6 %collective-permute-start = (f32[72,128]{1,0:T(8,128)S(1)}, f32[72,128]{1,0:T(8,128)S(1)}, u32[]{:S(2)}, u32[]{:S(2)}) collective-permute-start(f32[72,128]{1,0:T(8,128)S(1)} %depth_payload.1.refs_0_), channel_id=1, source_target_pairs={{0,2},{1,3},{2,0},{3,1},{4,6},{5,7},{6,4},{7,5},{8,10},{9,11},{10,... | collective-permute-start | bytes 110600 | tf_op jit(solution)/shard_map/ppermute | solution.py:706
  7.3 3.9 %column_forcing.1.refs_4_.after_ref.refs_0_ = f32[4,32,128]{2,1,0:T(8,128)S(1)} custom-call(s32[4,32,128]{2,1,0:T(8,128)} %levels_ref.7, f32[4,2,62,32,128]{4,3,2,1,0:T(8,128)} %adjoint_ref.5), custom_call_target="tpu_custom_call" | custom-call | flops 4063232 | bytes 8126464 | tf_op jit(solution)/shard_map/column_forcing/pallas_call | solution.py:95
  11.1 0.0 collective-permute-done.2.refs_3_
  11.2 0.3 collective-permute-done.1.refs_2_
  11.5 0.0 collective-permute-done.refs_1_
  11.5 2.5 %collective-permute-start.5 = (f32[4,72,128]{2,1,0:T(8,128)S(1)}, f32[4,72,128]{2,1,0:T(8,128)S(1)}, u32[]{:S(2)}, u32[]{:S(2)}) collective-permute-start(f32[4,72,128]{2,1,0:T(8,128)S(1)} %stack_after.4.refs_0_), channel_id=1, source_target_pairs={{0,24},{8,16},{16,8},{24,0},{1,25},{9,17},{17,9},{25,1},{2,26},{10... | collective-permute-start | bytes 442376 | tf_op jit(solution)/shard_map/ppermute | solution.py:706
  14.0 0.5 collective-permute-start.4
  14.5 0.5 collective-permute-start.3
  15.1 3.4 %collective-permute-start.8 = (f32[4,32,128]{2,1,0:T(8,128)S(1)}, f32[4,32,128]{2,1,0:T(8,128)S(1)}, u32[]{:S(2)}, u32[]{:S(2)}) collective-permute-start(f32[4,32,128]{2,1,0:T(8,128)S(1)} %column_forcing.1.refs_4_.after_ref.refs_0_), channel_id=1, source_target_pairs={{0,6},{1,7},{2,4},{3,5},{4,2},{5,3},{6,0},{7,1},{8,14},{9,15},{10,... | collective-permute-start | bytes 196616 | tf_op jit(solution)/shard_map/ppermute | solution.py:706
  18.5 0.0 collective-permute-start.7
  18.5 2.8 %collective-permute-done.8.refs_3_ = f32[4,32,128]{2,1,0:T(8,128)S(1)} collective-permute-done((f32[4,32,128]{2,1,0:T(8,128)S(1)}, f32[4,32,128]{2,1,0:T(8,128)S(1)}, u32[]{:S(2)}, u32[]{:S(2)}) %collective-permute-start.8) | collective-permute-done | bytes 65568 | tf_op jit(solution)/shard_map/ppermute | solution.py:706
  21.3 0.0 collective-permute-start.6
  21.3 0.0 copy-done.2
  21.3 0.0 copy-done
  21.3 0.0 copy-done.1
  21.3 3.8 %column_mixing.2 = (f32[1,2,62,32,128]{4,3,2,1,0:T(8,128)}, f32[1,2,32,128]{3,2,1,0:T(8,128)S(1)}, f32[1,32,128]{2,1,0:T(8,128)S(1)}) custom-call(s32[4]{0:T(128)S(1)} %copy-done.2, s32[4,32,128]{2,1,0:T(8,128)S(1)} %copy-done, f32[4,32,128]{2,1,0:T(8,128)S(1)} %copy-done.1, f32[4,2,62,32,128]{4,3,2,1,0:T(8,128)} %adjoint_ref.5, ...), custom_call_target="tpu_custom_call" | custom-call | flops 7110656 | bytes 5079040 | tf_op jit(solution)/shard_map/column_mixing/pallas_call | solution.py:235
  25.1 0.0 collective-permute-done.7.refs_2_
  25.1 0.4 collective-permute-done.6.refs_1_
  25.6 0.0 collective-permute-done.5.refs_3_
  25.6 0.0 collective-permute-done.4.refs_2_
  25.6 0.0 collective-permute-done.3.refs_1_
  25.7 0.1 collective-permute-start.9
  25.7 2.5 %collective-permute-start.12 = (f32[4,4,32,128]{3,2,1,0:T(8,128)S(1)}, f32[4,4,32,128]{3,2,1,0:T(8,128)S(1)}, u32[]{:S(2)}, u32[]{:S(2)}) collective-permute-start(f32[4,4,32,128]{3,2,1,0:T(8,128)S(1)} %stack_after.5.refs_4_.after_ref.refs_0_), channel_id=1, source_target_pairs={{0,24},{8,16},{16,8},{24,0},{1,25},{9,17},{17,9},{25,1},{2,26},{10... | collective-permute-start | bytes 786440 | tf_op jit(solution)/shard_map/ppermute | solution.py:706
  28.2 0.5 collective-permute-start.11
  28.7 0.5 collective-permute-start.10
  29.3 0.1 pad_add_fusion.me_ref
  29.4 0.0 copy-start.3
  29.4 7.8 %column_mixing.3 = (f32[3,2,62,32,128]{4,3,2,1,0:T(8,128)}, f32[4,2,32,128]{3,2,1,0:T(8,128)S(1)}, f32[4,32,128]{2,1,0:T(8,128)}) custom-call(s32[4]{0:T(128)S(1)} %copy-done.2, s32[4,32,128]{2,1,0:T(8,128)S(1)} %copy-done, f32[4,32,128]{2,1,0:T(8,128)S(1)} %copy-done.1, f32[4,2,62,32,128]{4,3,2,1,0:T(8,128)} %adjoint_ref.5, ...), custom_call_target="tpu_custom_call" | custom-call | flops 21331968 | bytes 15237120 | tf_op jit(solution)/shard_map/column_mixing/pallas_call | solution.py:235
  37.2 0.0 collective-permute-done.9.far_ref
  37.2 2.7 %surface_weights.1 = (f32[1040,128]{1,0:T(8,128)S(1)}, f32[1040,128]{1,0:T(8,128)S(1)}, f32[1040,128]{1,0:T(8,128)S(1)}, s32[54]{0:T(128)S(1)}) custom-call(s32[2]{0:T(128)S(1)} %pad_add_fusion.me_ref, s32[4]{0:T(128)S(1)} %copy-done.2, f32[16,72,128]{2,1,0:T(8,128)S(1)} %bitcast.7, f32[16,72,128]{2,1,0:T(8,128)S(1)} %collective-permute-done.9.far_ref), custom_call_target="tpu_custom_call" | custom-call | bytes 8388608 | tf_op jit(solution)/shard_map/surface_weights/pallas_call | solution.py:455
  40.0 0.0 collective-permute-done.12.refs_3_
  40.0 1.0 %collective-permute-done.11.refs_2_ = f32[4,4,32,128]{3,2,1,0:T(8,128)S(1)} collective-permute-done((f32[4,4,32,128]{3,2,1,0:T(8,128)S(1)}, f32[4,4,32,128]{3,2,1,0:T(8,128)S(1)}, u32[]{:S(2)}, u32[]{:S(2)}) %collective-permute-start.11) | collective-permute-done | bytes 262176 | tf_op jit(solution)/shard_map/ppermute | solution.py:706
  41.0 0.1 collective-permute-done.10.refs_1_
  41.1 0.1 stack_after.7
  41.1 0.1 collective-permute-start.13
  41.2 2.6 %collective-permute-done.13 = f32[4,4,4,32,128]{4,3,2,1,0:T(8,128)S(1)} collective-permute-done((f32[4,4,4,32,128]{4,3,2,1,0:T(8,128)S(1)}, f32[4,4,4,32,128]{4,3,2,1,0:T(8,128)S(1)}, u32[]{:S(2)}, u32[]{:S(2)}) %collective-permute-start.13) | collective-permute-done | bytes 1048608 | tf_op jit(solution)/shard_map/ppermute | solution.py:706
  43.9 0.0 copy-done.3
  43.9 12.4 %surface_solve.1 = (f32[4,2,62,32,128]{4,3,2,1,0:T(8,128)}, f32[32,256]{1,0:T(8,128)}, f32[32,256]{1,0:T(8,128)}) custom-call(s32[4]{0:T(128)S(1)} %copy-done.2, s32[54]{0:T(128)S(1)} %get-tuple-element.18.table_ref, f32[32]{0:T(128)S(1)} %copy-done.3, f32[1040,128]{1,0:T(8,128)S(1)} %get-tuple-element.19.refs_5_.root_ref, ...), custom_call_target="tpu_custom_call" | custom-call | flops 38338560 | bytes 2129920 | tf_op jit(solution)/shard_map/surface_solve/pallas_call | solution.py:657
  (3 shorter events, 0.1 us)
Async XLA Ops:
  0.6 20.7 %copy-start.2 = (s32[4]{0:T(128)S(1)}, s32[4]{0:T(128)}, u32[]{:S(2)}) copy-start(s32[4]{0:T(128)} %ids_ref.9) | copy-start | bytes 52
  0.6 20.6 %copy-start = (s32[4,32,128]{2,1,0:T(8,128)S(1)}, s32[4,32,128]{2,1,0:T(8,128)}, u32[]{:S(2)}) copy-start(s32[4,32,128]{2,1,0:T(8,128)} %levels_ref.7) | copy-start | bytes 196612
  0.7 20.6 %copy-start.1 = (f32[4,32,128]{2,1,0:T(8,128)S(1)}, f32[4,32,128]{2,1,0:T(8,128)}, u32[]{:S(2)}) copy-start(f32[4,32,128]{2,1,0:T(8,128)} %drag_ref.3) | copy-start | bytes 196612
  1.5 9.6 %collective-permute-start.2 = (f32[72,128]{1,0:T(8,128)S(1)}, f32[72,128]{1,0:T(8,128)S(1)}, u32[]{:S(2)}, u32[]{:S(2)}) collective-permute-start(f32[72,128]{1,0:T(8,128)S(1)} %depth_payload.1.refs_0_), channel_id=1, source_target_pairs={{0,6},{1,7},{2,4},{3,5},{4,2},{5,3},{6,0},{7,1},{8,14},{9,15},{10,... | collective-permute-start | bytes 110600 | tf_op jit(solution)/shard_map/ppermute | solution.py:706
  6.6 4.9 %collective-permute-start.1 = (f32[72,128]{1,0:T(8,128)S(1)}, f32[72,128]{1,0:T(8,128)S(1)}, u32[]{:S(2)}, u32[]{:S(2)}) collective-permute-start(f32[72,128]{1,0:T(8,128)S(1)} %depth_payload.1.refs_0_), channel_id=1, source_target_pairs={{0,4},{1,5},{2,6},{3,7},{4,0},{5,1},{6,2},{7,3},{8,12},{9,13},{10,... | collective-permute-start | bytes 110600 | tf_op jit(solution)/shard_map/ppermute | solution.py:706
  6.6 4.9 %collective-permute-start = (f32[72,128]{1,0:T(8,128)S(1)}, f32[72,128]{1,0:T(8,128)S(1)}, u32[]{:S(2)}, u32[]{:S(2)}) collective-permute-start(f32[72,128]{1,0:T(8,128)S(1)} %depth_payload.1.refs_0_), channel_id=1, source_target_pairs={{0,2},{1,3},{2,0},{3,1},{4,6},{5,7},{6,4},{7,5},{8,10},{9,11},{10,... | collective-permute-start | bytes 110600 | tf_op jit(solution)/shard_map/ppermute | solution.py:706
  11.5 14.1 %collective-permute-start.5 = (f32[4,72,128]{2,1,0:T(8,128)S(1)}, f32[4,72,128]{2,1,0:T(8,128)S(1)}, u32[]{:S(2)}, u32[]{:S(2)}) collective-permute-start(f32[4,72,128]{2,1,0:T(8,128)S(1)} %stack_after.4.refs_0_), channel_id=1, source_target_pairs={{0,24},{8,16},{16,8},{24,0},{1,25},{9,17},{17,9},{25,1},{2,26},{10... | collective-permute-start | bytes 442376 | tf_op jit(solution)/shard_map/ppermute | solution.py:706
  14.0 11.6 %collective-permute-start.4 = (f32[4,72,128]{2,1,0:T(8,128)S(1)}, f32[4,72,128]{2,1,0:T(8,128)S(1)}, u32[]{:S(2)}, u32[]{:S(2)}) collective-permute-start(f32[4,72,128]{2,1,0:T(8,128)S(1)} %stack_after.4.refs_0_), channel_id=1, source_target_pairs={{0,16},{8,24},{16,0},{24,8},{1,17},{9,25},{17,1},{25,9},{2,18},{10... | collective-permute-start | bytes 442376 | tf_op jit(solution)/shard_map/ppermute | solution.py:706
  14.5 11.1 %collective-permute-start.3 = (f32[4,72,128]{2,1,0:T(8,128)S(1)}, f32[4,72,128]{2,1,0:T(8,128)S(1)}, u32[]{:S(2)}, u32[]{:S(2)}) collective-permute-start(f32[4,72,128]{2,1,0:T(8,128)S(1)} %stack_after.4.refs_0_), channel_id=1, source_target_pairs={{0,8},{8,0},{16,24},{24,16},{1,9},{9,1},{17,25},{25,17},{2,10},{10... | collective-permute-start | bytes 442376 | tf_op jit(solution)/shard_map/ppermute | solution.py:706
  15.1 6.2 %collective-permute-start.8 = (f32[4,32,128]{2,1,0:T(8,128)S(1)}, f32[4,32,128]{2,1,0:T(8,128)S(1)}, u32[]{:S(2)}, u32[]{:S(2)}) collective-permute-start(f32[4,32,128]{2,1,0:T(8,128)S(1)} %column_forcing.1.refs_4_.after_ref.refs_0_), channel_id=1, source_target_pairs={{0,6},{1,7},{2,4},{3,5},{4,2},{5,3},{6,0},{7,1},{8,14},{9,15},{10,... | collective-permute-start | bytes 196616 | tf_op jit(solution)/shard_map/ppermute | solution.py:706
  18.5 6.6 %collective-permute-start.7 = (f32[4,32,128]{2,1,0:T(8,128)S(1)}, f32[4,32,128]{2,1,0:T(8,128)S(1)}, u32[]{:S(2)}, u32[]{:S(2)}) collective-permute-start(f32[4,32,128]{2,1,0:T(8,128)S(1)} %column_forcing.1.refs_4_.after_ref.refs_0_), channel_id=1, source_target_pairs={{0,4},{1,5},{2,6},{3,7},{4,0},{5,1},{6,2},{7,3},{8,12},{9,13},{10,... | collective-permute-start | bytes 196616 | tf_op jit(solution)/shard_map/ppermute | solution.py:706
  21.3 4.3 %collective-permute-start.6 = (f32[4,32,128]{2,1,0:T(8,128)S(1)}, f32[4,32,128]{2,1,0:T(8,128)S(1)}, u32[]{:S(2)}, u32[]{:S(2)}) collective-permute-start(f32[4,32,128]{2,1,0:T(8,128)S(1)} %column_forcing.1.refs_4_.after_ref.refs_0_), channel_id=1, source_target_pairs={{0,2},{1,3},{2,0},{3,1},{4,6},{5,7},{6,4},{7,5},{8,10},{9,11},{10,... | collective-permute-start | bytes 196616 | tf_op jit(solution)/shard_map/ppermute | solution.py:706
  25.7 11.6 %collective-permute-start.9 = (f32[16,72,128]{2,1,0:T(8,128)S(1)}, f32[16,72,128]{2,1,0:T(8,128)S(1)}, u32[]{:S(2)}, u32[]{:S(2)}) collective-permute-start(f32[16,72,128]{2,1,0:T(8,128)S(1)} %bitcast.6), channel_id=1, source_target_pairs={{0,1},{1,0},{2,3},{3,2},{4,5},{5,4},{6,7},{7,6},{8,9},{9,8},{10,11... | collective-permute-start | bytes 1769480 | tf_op jit(solution)/shard_map/ppermute | solution.py:706
  25.7 14.2 %collective-permute-start.12 = (f32[4,4,32,128]{3,2,1,0:T(8,128)S(1)}, f32[4,4,32,128]{3,2,1,0:T(8,128)S(1)}, u32[]{:S(2)}, u32[]{:S(2)}) collective-permute-start(f32[4,4,32,128]{3,2,1,0:T(8,128)S(1)} %stack_after.5.refs_4_.after_ref.refs_0_), channel_id=1, source_target_pairs={{0,24},{8,16},{16,8},{24,0},{1,25},{9,17},{17,9},{25,1},{2,26},{10... | collective-permute-start | bytes 786440 | tf_op jit(solution)/shard_map/ppermute | solution.py:706
  28.2 12.7 %collective-permute-start.11 = (f32[4,4,32,128]{3,2,1,0:T(8,128)S(1)}, f32[4,4,32,128]{3,2,1,0:T(8,128)S(1)}, u32[]{:S(2)}, u32[]{:S(2)}) collective-permute-start(f32[4,4,32,128]{3,2,1,0:T(8,128)S(1)} %stack_after.5.refs_4_.after_ref.refs_0_), channel_id=1, source_target_pairs={{0,16},{8,24},{16,0},{24,8},{1,17},{9,25},{17,1},{25,9},{2,18},{10... | collective-permute-start | bytes 786440 | tf_op jit(solution)/shard_map/ppermute | solution.py:706
  28.7 12.3 %collective-permute-start.10 = (f32[4,4,32,128]{3,2,1,0:T(8,128)S(1)}, f32[4,4,32,128]{3,2,1,0:T(8,128)S(1)}, u32[]{:S(2)}, u32[]{:S(2)}) collective-permute-start(f32[4,4,32,128]{3,2,1,0:T(8,128)S(1)} %stack_after.5.refs_4_.after_ref.refs_0_), channel_id=1, source_target_pairs={{0,8},{8,0},{16,24},{24,16},{1,9},{9,1},{17,25},{25,17},{2,10},{10... | collective-permute-start | bytes 786440 | tf_op jit(solution)/shard_map/ppermute | solution.py:706
  29.4 14.5 %copy-start.3 = (f32[32]{0:T(128)S(1)}, f32[32]{0:T(128)}, u32[]{:S(2)}) copy-start(f32[32]{0:T(128)} %constant.10.clone.coefs_ref) | copy-start | bytes 388
  41.1 2.7 %collective-permute-start.13 = (f32[4,4,4,32,128]{4,3,2,1,0:T(8,128)S(1)}, f32[4,4,4,32,128]{4,3,2,1,0:T(8,128)S(1)}, u32[]{:S(2)}, u32[]{:S(2)}) collective-permute-start(f32[4,4,4,32,128]{4,3,2,1,0:T(8,128)S(1)} %stack_after.7), channel_id=1, source_target_pairs={{0,1},{1,0},{2,3},{3,2},{4,5},{5,4},{6,7},{7,6},{8,9},{9,8},{10,11... | collective-permute-start | bytes 3145736 | tf_op jit(solution)/shard_map/ppermute | solution.py:706
